TPU v7x, 256 devices: a whole 4x4x8 slice. The times are simulated.
256 devices in a mesh: node: 16 (over y, x_hi, core), local: 16 (over x_lo, z).
Axes of the slice: x: 4 (x_hi: 2, x_lo: 2; x = x_hi * 2 + x_lo), y: 4, z: 8, core: 2. Of those that a mesh axis runs over, the one named last changes fastest.
Arguments:
- partials: float32 [256, 638976], P(('node', 'local')), may hold values from -6 to 6
- master: float32 [638976], P(('node', 'local')), may hold values from -4 to 4
- first: float32 [638976], P(('node', 'local')), may hold values from -6 to 6
- second: float32 [638976], P(('node', 'local')), may hold values from 0.02 to 64
- acts: bfloat16 [32768, 6144], P(('node', 'local')), may hold values from -6 to 6
- up_cot: bfloat16 [32768, 6144], P(('node', 'local')), may hold values from -4 to 4
- out_cot: bfloat16 [32768, 6144], P(('node', 'local')), may hold values from -4 to 4
- ln_gain: bfloat16 [6144], replicated, may hold values from 0.5 to 1.5
Outputs:
- new_master: float32 [638976], P(('node', 'local'))
- new_first: float32 [638976], P(('node', 'local'))
- new_second: float32 [638976], P(('node', 'local'))
- new_params: bfloat16 [638976], P('node')
- trust: float32 [64], replicated
- input_grad: bfloat16 [32768, 6144], P(('node', 'local'))
All inputs are finite; a program needn't handle non-finite values.
Results may differ from a plain program's by a relative error of at most 0.0004.
Values may be sent and summed in bfloat16 or wider, within the bound.
No kernel may reach another device: no remote copies, remote signals or barrier semaphores. Data moves between devices by JAX's collectives and lax.ppermute only.
A program may use at most 64 MiB of HBM per device.

v0:
```python
import jax
import jax.numpy as jnp
from jax import lax
from jax.sharding import PartitionSpec as P

FF = 24576
LAYERS = 8


beta_one = 0.9
beta_two = 0.999
adam_epsilon = 1e-06
norm_epsilon = 1e-05
learn_rate = 0.01


def tensor_ids(position, width, hidden, length):
    layer = position // length
    offset = position - layer * length
    bounds = (width, 2 * width, 5 * width, 6 * width, 7 * width, 8 * width, 8 * width + hidden)
    kind = jnp.zeros_like(position)
    for bound in bounds:
        kind = kind + (offset >= bound).astype(jnp.int32)
    return layer * 8 + kind


def last_layer(acts, up_cot, out_cot, ln_gain):
    values = acts.astype(jnp.float32)
    center = jnp.mean(values, axis=-1, keepdims=True)
    centered = values - center
    variance = jnp.mean(centered * centered, axis=-1, keepdims=True)
    inverse = lax.rsqrt(variance + norm_epsilon)
    normed = centered * inverse
    upward = up_cot.astype(jnp.float32)
    outward = out_cot.astype(jnp.float32)
    gain_part = jnp.sum(upward * normed, axis=0)
    shift_part = jnp.sum(upward, axis=0)
    bias_part = jnp.sum(outward, axis=0)
    scaled = upward * ln_gain.astype(jnp.float32)
    inner = (
        scaled
        - jnp.mean(scaled, axis=-1, keepdims=True)
        - normed * jnp.mean(scaled * normed, axis=-1, keepdims=True)
    )
    input_grad = (outward + inverse * inner).astype(jnp.bfloat16)
    return (gain_part, shift_part, bias_part, input_grad)


def local(partials, master, first, second, acts, up_cot, out_cot, ln_gain):
    width = acts.shape[1]
    total = partials.shape[1]
    length = 9 * width + FF
    count = 8 * LAYERS
    nodes = lax.axis_size("node")
    locals_count = lax.axis_size("local")
    shard = master.shape[0]
    owner = lax.axis_index("node") * locals_count + lax.axis_index("local")
    position = owner * shard + jnp.arange(shard, dtype=jnp.int32)
    ids = tensor_ids(position, width, FF, length)
    onehot = (ids[:, None] == jnp.arange(count, dtype=jnp.int32)[None, :]).astype(jnp.float32)
    weight_part = jnp.dot(master * master, onehot, precision=lax.Precision.HIGHEST)
    weight_sq = lax.psum(weight_part, ("node", "local"))
    gain_part, shift_part, bias_part, input_grad = last_layer(acts, up_cot, out_cot, ln_gain)
    base = (LAYERS - 1) * length
    flat = partials[0]
    flat = flat.at[base + 6 * width : base + 7 * width].add(gain_part)
    flat = flat.at[base + 7 * width : base + 8 * width].add(shift_part)
    flat = flat.at[base + 8 * width + FF : base + 9 * width + FF].add(bias_part)
    grid = flat.reshape(nodes, locals_count, total // (nodes * locals_count))
    within = lax.psum_scatter(grid, "local", scatter_dimension=1, tiled=True)
    grad = lax.psum_scatter(within, "node", scatter_dimension=0, tiled=True).reshape(shard)
    new_first = beta_one * first + (1.0 - beta_one) * grad
    new_second = beta_two * second + (1.0 - beta_two) * grad * grad
    update = new_first / (jnp.sqrt(new_second) + adam_epsilon)
    update_part = jnp.dot(update * update, onehot, precision=lax.Precision.HIGHEST)
    update_sq = lax.psum(update_part, ("node", "local"))
    trust = jnp.sqrt(weight_sq) / (jnp.sqrt(update_sq) + adam_epsilon)
    spread = jnp.dot(onehot, trust, precision=lax.Precision.HIGHEST)
    new_master = master - learn_rate * spread * update
    new_params = lax.all_gather(new_master.astype(jnp.bfloat16), "local", axis=0, tiled=True)
    return (new_master, new_first, new_second, new_params, trust, input_grad)


def solution(mesh):
    in_specs = (
        P(("node", "local"), None),
        P(("node", "local")),
        P(("node", "local")),
        P(("node", "local")),
        P(("node", "local"), None),
        P(("node", "local"), None),
        P(("node", "local"), None),
        P(),
    )
    out_specs = (
        P(("node", "local")),
        P(("node", "local")),
        P(("node", "local")),
        P("node"),
        P(),
        P(("node", "local"), None),
    )
    return jax.shard_map(local, mesh=mesh, in_specs=in_specs, out_specs=out_specs, check_vma=False)
```

profile of v0, /device:TPU:1, one launch (start us, length us, event | category | flops | bytes accessed | tf_op | source)
XLA Modules:
  0.0 444.5 jit_solution(1480410316971503664)
XLA Ops:
  7.2 0.0 copy-start
  7.2 0.0 reduce-scatter.2.cloned.1.call-start
  7.2 4.8 %copy.24 = f32[1,638976]{1,0:T(1,128)} copy(f32[1,638976]{1,0:T(1,128)} %param.14) | data formatting | bytes 5111808
  12.0 0.0 copy-done
  12.0 0.3 convert_reduce_fusion.2
  12.3 0.0 copy-start.2
  12.3 0.6 fusion.8
  12.9 0.0 copy-done.9
  12.9 0.8 slice.42
  13.7 0.0 copy-done.1
  13.7 1.4 fusion.10
  15.1 0.6 add_dynamic-update-slice_fusion
  15.8 1.3 fusion.22
  17.1 0.0 copy-done.2
  17.1 2.9 fusion.9
  20.0 1.3 fusion.21
  21.3 2.7 reshape.139
  24.0 3.0 copy.15
  27.1 0.0 copy-start.8
  27.1 0.0 reduce-scatter.2.cloned.1.call-update
  27.1 0.0 all-reduce.8.cloned.1.call-start
  27.2 69.7 %reduce-scatter.2.cloned.1.call-done = f32[16,1,2496]{2,0,1:T(8,128)} async-done(((f32[16,16,2496]{2,0,1:T(8,128)}), f32[16,1,2496]{2,0,1:T(8,128)}) %reduce-scatter.2.cloned.1.call-update) | async-done | bytes 159760 | tf_op jit(solution)/shard_map/reduce_scatter | solution.py:70
  96.9 1.7 copy.16
  98.6 0.0 all-reduce.8.cloned.1.call-update
  98.6 0.0 all-reduce.6.cloned.1.call-start
  98.7 0.0 copy-done.4
  98.8 0.0 copy-done.11
  98.8 0.6 dynamic-slice.23
  99.4 0.0 copy-done.10
  99.4 0.6 dynamic-slice.22
  100.6 0.7 fusion.16
  101.3 137.5 %all-reduce.8.cloned.1.call-done = f32[16,1,2496]{2,1,0:T(1,128)} async-done(((f32[16,1,2496]{2,1,0:T(1,128)}), f32[16,1,2496]{2,1,0:T(1,128)}) %all-reduce.8.cloned.1.call-update) | async-done | bytes 159760
  238.7 1.4 dynamic-slice_reduce_fusion
  240.1 0.0 copy-done.7
  240.1 0.0 copy-done.8
  240.2 0.0 copy-start.5
  240.2 0.0 copy-start.6
  240.2 0.7 fusion.17
  240.9 77.5 %all-reduce.2 = (f32[64]{0:T(128)S(1)}, f32[64]{0:T(128)S(1)}) all-reduce(f32[64]{0:T(128)S(1)} %fusion.17, f32[64]{0:T(128)S(1)} %fusion.16), channel_id=1, replica_groups=mesh['node'=16,'local'=16] {'node','local'}, use_global_device_ids=true, to_apply=%region_8.9 | all-reduce | flops 128 | bytes 1024 | tf_op jit(solution)/shard_map/psum | solution.py:76
  318.3 0.0 copy-start.12
  318.4 0.9 fusion.15
  319.2 0.6 fusion.29
  319.9 0.3 dynamic-update-slice.6
  320.2 0.6 copy-done.3
  320.8 0.0 all-reduce.6.cloned.1.call-update
  320.8 115.5 %all-reduce.6.cloned.1.call-done = bf16[39936]{0:T(1024)(128)(2,1)} async-done(((bf16[39936]{0:T(1024)(128)(2,1)}), bf16[39936]{0:T(1024)(128)(2,1)}) %all-reduce.6.cloned.1.call-update) | async-done | bytes 79888
  436.4 1.5 copy.25
  437.9 0.0 copy-done.5
  (20 shorter events, 0.1 us)
Async XLA Ops:
  7.2 4.8 %copy-start = (bf16[128,6144]{1,0:T(8,128)(2,1)S(1)}, bf16[128,6144]{1,0:T(8,128)(2,1)}, u32[]{:S(2)}) copy-start(bf16[128,6144]{1,0:T(8,128)(2,1)} %param.18) | copy-start | bytes 4718596
  7.2 89.7 %reduce-scatter.2.cloned.1.call-start = ((), (), s32[]{:S(2)}) async-start(), calls=%async_computation.1 | async-start | bytes 2785280 | tf_op jit(solution)/shard_map/reduce_scatter | solution.py:70
  12.0 0.9 copy-start.9
  12.0 1.7 copy-start.1
  12.3 4.8 %copy-start.2 = (bf16[128,6144]{1,0:T(8,128)(2,1)S(1)}, bf16[128,6144]{1,0:T(8,128)(2,1)}, u32[]{:S(2)}) copy-start(bf16[128,6144]{1,0:T(8,128)(2,1)} %param.20) | copy-start | bytes 4718596
  27.1 71.7 %copy-start.4 = (f32[2496]{0:T(1024)S(1)}, f32[2496]{0:T(1024)}, u32[]{:S(2)}) copy-start(f32[2496]{0:T(1024)} %param.15) | copy-start | bytes 29956
  27.1 71.7 %copy-start.11 = (u32[256]{0:T(256)S(1)}, u32[256]{0:T(256)}, u32[]{:S(2)}) copy-start(u32[256]{0:T(256)} %constant.150) | copy-start | bytes 3076
  27.1 72.3 %copy-start.10 = (u32[256]{0:T(256)S(1)}, u32[256]{0:T(256)}, u32[]{:S(2)}) copy-start(u32[256]{0:T(256)} %constant.144) | copy-start | bytes 3076
  27.1 213.1 %copy-start.7 = (f32[2496]{0:T(1024)S(1)}, f32[2496]{0:T(1024)}, u32[]{:S(2)}) copy-start(f32[2496]{0:T(1024)} %param.17) | copy-start | bytes 29956
  27.1 213.1 %copy-start.8 = (f32[2496]{0:T(1024)S(1)}, f32[2496]{0:T(1024)}, u32[]{:S(2)}) copy-start(f32[2496]{0:T(1024)} %param.16) | copy-start | bytes 29956
  27.1 211.6 %all-reduce.8.cloned.1.call-start = ((), (), s32[]{:S(2)}) async-start(), calls=%async_computation.3 | async-start | bytes 327680
  98.6 337.8 %all-reduce.6.cloned.1.call-start = ((), (), s32[]{:S(2)}) async-start(), calls=%async_computation.2 | async-start | bytes 159744
  240.2 197.7 %copy-start.5 = (f32[2496]{0:T(1024)}, f32[2496]{0:T(1024)S(1)}, u32[]{:S(2)}) copy-start(f32[2496]{0:T(1024)S(1)} %get-tuple-element.59) | copy-start | bytes 29956
  240.2 197.7 %copy-start.6 = (f32[2496]{0:T(1024)}, f32[2496]{0:T(1024)S(1)}, u32[]{:S(2)}) copy-start(f32[2496]{0:T(1024)S(1)} %get-tuple-element.58) | copy-start | bytes 29956
  318.3 119.6 %copy-start.12 = (f32[64]{0:T(128)}, f32[64]{0:T(128)S(1)}, u32[]{:S(2)}) copy-start(f32[64]{0:T(128)S(1)} %add_divide_fusion.1) | copy-start | bytes 772
  320.2 0.6 copy-start.3
Sparse Core Ops, SparseCore 0:
  27.2 69.5 reduce-scatter.1
  99.5 139.2 all-reduce.7
  321.0 115.3 all-reduce.5
where the time goes:
time: 453 us; the launch traced here: 444 us
  waiting for transfers between devices  323 us (71%)
  blocking collectives  77.5 us (17%)
  local copies, waits for them, and re-layouts  18.1 us (4%)
  between operations  14.6 us (3%)
  other arithmetic  9.18 us (2%)
    unnamed x5, waiting for transfers between devices  253 us
    psum x1, blocking collectives, local(): update_sq = lax.psum(update_part, ('node', 'local'))  77.5 us
    reduce_scatter x1, waiting for transfers between devices, local(): within = lax.psum_scatter(grid, 'local', scatter_dimension=1, tiled=True)  69.7 us
  transfers between devices with their start and end apart: 3, of which 3 were waited for; matrix products, arithmetic and copies ran while one was open for 0% of the time, Pallas kernels for 0%

commit v1 on v0

v1 whole, which is shorter than its diff:
```python
import jax
import jax.numpy as jnp
from jax import lax
from jax.experimental import pallas as pl
from jax.experimental.pallas import tpu as pltpu
from jax.sharding import Mesh, PartitionSpec as P

D = 6144
FF = 24576
LAYERS = 8
LENGTH = 9 * D + FF
PARAMS = LAYERS * LENGTH
LANES = 128
NODES = 16
LOCALS = 16
SHARD = PARAMS // (NODES * LOCALS)
NODE_PART = PARAMS // NODES
NODE_ROWS = NODE_PART // LANES
CHUNK_ROWS = NODE_ROWS // 2
CHUNK_PAD = 160
PIECE = 24
PAIR_ROWS = 2 * SHARD // LANES
BOUNDS = (0, D, 2 * D, 5 * D, 6 * D, 7 * D, 8 * D, 8 * D + FF, LENGTH)

beta_one = 0.9
beta_two = 0.999
adam_epsilon = 1e-06
norm_epsilon = 1e-05
learn_rate = 0.01

f32 = jnp.float32
TOKENS_STEP = 32
COLS = D // LANES
VMEM_LIMIT = 48 * 1024 * 1024


def whole():
    return pl.BlockSpec(memory_space=pltpu.VMEM)


def params():
    return pltpu.CompilerParams(vmem_limit_bytes=VMEM_LIMIT)


def norm_kernel(acts, up, out, gain, grad, parts, sums):
    step = pl.program_id(0)
    rows = acts.shape[0]

    def cols(j):
        return slice(j * LANES, (j + 1) * LANES)

    total = jnp.zeros((rows, LANES), f32)
    for j in range(COLS):
        total = total + acts[:, cols(j)].astype(f32)
    center = jnp.broadcast_to(jnp.sum(total, axis=1, keepdims=True) * (1.0 / D), (rows, LANES))
    squares = jnp.zeros((rows, LANES), f32)
    scaled = jnp.zeros((rows, LANES), f32)
    cross = jnp.zeros((rows, LANES), f32)
    for j in range(COLS):
        x = acts[:, cols(j)].astype(f32) - center
        s = up[:, cols(j)].astype(f32) * gain[:, cols(j)].astype(f32)
        squares = squares + x * x
        scaled = scaled + s
        cross = cross + s * x
    variance = jnp.sum(squares, axis=1, keepdims=True) * (1.0 / D)
    inverse_col = lax.rsqrt(variance + norm_epsilon)
    mean_scaled = jnp.sum(scaled, axis=1, keepdims=True) * (1.0 / D)
    mean_cross = jnp.sum(cross, axis=1, keepdims=True) * (1.0 / D) * inverse_col
    inverse = jnp.broadcast_to(inverse_col, (rows, LANES))
    mean_scaled = jnp.broadcast_to(mean_scaled, (rows, LANES))
    mean_cross = jnp.broadcast_to(mean_cross, (rows, LANES))

    def fold(v):
        return jnp.sum(v.reshape(rows // 8, 8, LANES), axis=0)

    @pl.when(step == 0)
    def _():
        sums[...] = jnp.zeros_like(sums)

    for j in range(COLS):
        normed = (acts[:, cols(j)].astype(f32) - center) * inverse
        u = up[:, cols(j)].astype(f32)
        o = out[:, cols(j)].astype(f32)
        inner = u * gain[:, cols(j)].astype(f32) - mean_scaled - normed * mean_cross
        grad[:, cols(j)] = (o + inverse * inner).astype(jnp.bfloat16)
        sums[0, :, cols(j)] += fold(u * normed)
        sums[1, :, cols(j)] += fold(u)
        sums[2, :, cols(j)] += fold(o)

    @pl.when(step == pl.num_programs(0) - 1)
    def _():
        for which in range(3):
            for j in range(COLS):
                row = which * COLS + j
                parts[row : row + 1, :] = jnp.sum(sums[which, :, cols(j)], axis=0, keepdims=True)


def norm_backward(acts, up, out, gain):
    tokens = acts.shape[0]
    block = pl.BlockSpec((TOKENS_STEP, D), lambda i: (i, 0))
    return pl.pallas_call(
        norm_kernel,
        grid=(tokens // TOKENS_STEP,),
        in_specs=[block, block, block, pl.BlockSpec((1, D), lambda i: (0, 0))],
        out_specs=[block, pl.BlockSpec((3 * COLS, LANES), lambda i: (0, 0))],
        out_shape=[
            jax.ShapeDtypeStruct((tokens, D), jnp.bfloat16),
            jax.ShapeDtypeStruct((3 * COLS, LANES), f32),
        ],
        scratch_shapes=[pltpu.VMEM((3, 8, D), f32)],
        compiler_params=params(),
        cost_estimate=pl.CostEstimate(flops=30 * tokens * D, bytes_accessed=8 * tokens * D, transcendentals=0),
    )(acts, up, out, gain.reshape(1, D))


def pair_kernel(core, own, other, parts, parts_other, result):
    step = pl.program_id(0)
    result[0, 0, 0:CHUNK_ROWS, :] = own[0, 0, 0:CHUNK_ROWS, :] + other[0, 0:CHUNK_ROWS, :]
    result[0, 1, 0:CHUNK_ROWS, :] = own[0, 0, CHUNK_ROWS:NODE_ROWS, :] + other[0, CHUNK_ROWS:NODE_ROWS, :]
    for half in range(2):
        result[0, half, CHUNK_ROWS:CHUNK_PAD, :] = jnp.zeros((CHUNK_PAD - CHUNK_ROWS, LANES), f32)

    def add(half, row, first, count):
        total = parts[first : first + count, :] + parts_other[first : first + count, :]
        result[0, half, row : row + count, :] += total

    @pl.when((step == pl.num_programs(0) - 1) & (core[0] == 0))
    def _():
        add(1, CHUNK_ROWS - COLS // 2, 0, COLS // 2)

    @pl.when((step == pl.num_programs(0) - 1) & (core[0] == 1))
    def _():
        add(0, 0, COLS // 2, COLS // 2)
        add(0, COLS // 2, COLS, COLS)
        add(1, CHUNK_ROWS - COLS, 2 * COLS, COLS)


def pair_sum(core, grid, other, parts, parts_other):
    small = pl.BlockSpec((3 * COLS, LANES), lambda i, c: (0, 0))
    return pl.pallas_call(
        pair_kernel,
        grid_spec=pltpu.PrefetchScalarGridSpec(
            num_scalar_prefetch=1,
            grid=(NODES // 2,),
            in_specs=[
                pl.BlockSpec((1, 1, NODE_ROWS, LANES), lambda i, c: (i, c[0], 0, 0)),
                pl.BlockSpec((1, NODE_ROWS, LANES), lambda i, c: (i, 0, 0)),
                small,
                small,
            ],
            out_specs=pl.BlockSpec((1, 2, CHUNK_PAD, LANES), lambda i, c: (i, 0, 0, 0)),
        ),
        out_shape=jax.ShapeDtypeStruct((NODES // 2, 2, CHUNK_PAD, LANES), f32),
        compiler_params=params(),
    )(core, grid, other, parts, parts_other)


def lane_index(rows):
    return lax.broadcasted_iota(jnp.int32, (rows, LANES), 1)


def split_kernel(blocks, pieces, total):
    total[...] = jnp.sum(blocks[...], axis=0)
    high = lane_index(20) >= LANES // 2
    for z in range(8):
        base = PAIR_ROWS * (z // 2)
        if z % 2 == 0:
            piece = total[base : base + 20, :]
        else:
            start = base + PAIR_ROWS // 2
            piece = pltpu.roll(
                jnp.where(high, total[start : start + 20, :], total[start + 1 : start + 21, :]), LANES // 2, 1
            )
        pieces[z, 0:20, :] = piece
        pieces[z, 20:PIECE, :] = jnp.zeros((PIECE - 20, LANES), f32)


def split_sum(blocks):
    return pl.pallas_call(
        split_kernel,
        in_specs=[whole()],
        out_specs=whole(),
        out_shape=jax.ShapeDtypeStruct((8, PIECE, LANES), f32),
        scratch_shapes=[pltpu.VMEM((CHUNK_PAD, LANES), f32)],
        compiler_params=params(),
    )(blocks)


def step_kernel(pieces, master, first, second, new_first, new_second, message):
    grad = jnp.sum(pieces[...], axis=0)
    moment = beta_one * first[...] + (1.0 - beta_one) * grad
    spread = beta_two * second[...] + (1.0 - beta_two) * grad * grad
    new_first[...] = moment
    new_second[...] = spread
    update = moment / (jnp.sqrt(spread) + adam_epsilon)
    held = master[...]
    for i in range(LOCALS):
        message[i, 0:PIECE, :] = update
        message[i, PIECE : 2 * PIECE, :] = held


def step(pieces, master, first, second):
    shard = jax.ShapeDtypeStruct((PIECE, LANES), f32)
    return pl.pallas_call(
        step_kernel,
        in_specs=[whole()] * 4,
        out_specs=[whole()] * 3,
        out_shape=[shard, shard, jax.ShapeDtypeStruct((LOCALS, 2 * PIECE, LANES), f32)],
        compiler_params=params(),
    )(pieces, master, first, second)


def kinds_of(piece):
    found = set()
    for half in range(2):
        low = half * NODE_PART + piece * SHARD
        high = low + SHARD
        found |= {k for k in range(8) if BOUNDS[k] < high and BOUNDS[k + 1] > low}
    return sorted(found)


def place(rows):
    return lax.broadcasted_iota(jnp.int32, (rows, LANES), 0) * LANES + lane_index(rows)


def sums_kernel(core, gathered, message):
    start = core[0] * NODE_PART
    inside = place(PIECE)
    valid = inside < SHARD
    weights = [jnp.zeros((8, LANES), f32) for _ in range(8)]
    updates = [jnp.zeros((8, LANES), f32) for _ in range(8)]
    for i in range(LOCALS):
        offset = inside + (start + i * SHARD)
        update = gathered[i, 0:PIECE, :]
        held = gathered[i, PIECE : 2 * PIECE, :]
        update_sq = jnp.where(valid, update * update, 0.0)
        held_sq = jnp.where(valid, held * held, 0.0)
        for k in kinds_of(i):
            mask = (offset >= BOUNDS[k]) & (offset < BOUNDS[k + 1])
            weights[k] += jnp.sum(jnp.where(mask, held_sq, 0.0).reshape(3, 8, LANES), axis=0)
            updates[k] += jnp.sum(jnp.where(mask, update_sq, 0.0).reshape(3, 8, LANES), axis=0)
    rows = [jnp.sum(v, axis=0, keepdims=True) for v in weights + updates]
    table = jnp.concatenate(rows, axis=0)
    for i in range(NODES):
        message[i, :, :] = table


def node_sums(core, gathered):
    return pl.pallas_call(
        sums_kernel,
        in_specs=[pl.BlockSpec(memory_space=pltpu.SMEM), whole()],
        out_specs=whole(),
        out_shape=jax.ShapeDtypeStruct((NODES, 16, LANES), f32),
        compiler_params=params(),
    )(core, gathered)


def final_kernel(where, tables, gathered, new_master, new_params, trust, masters, flat, shifted):
    core, layer, mine = where[0], where[1], where[2]
    for n in range(LAYERS):
        table = tables[2 * n, :, :] + tables[2 * n + 1, :, :]
        weight_sq = jnp.sum(table[0:8, :], axis=1, keepdims=True)
        update_sq = jnp.sum(table[8:16, :], axis=1, keepdims=True)
        ratio = jnp.sqrt(weight_sq) / (jnp.sqrt(update_sq) + adam_epsilon)
        trust[n, :, :] = jnp.broadcast_to(ratio, (8, LANES))
    ratios = trust[layer]
    start = core * NODE_PART
    inside = place(PIECE)
    for i in range(LOCALS):
        offset = inside + (start + i * SHARD)
        kinds = kinds_of(i)
        factor = jnp.broadcast_to(ratios[kinds[0] : kinds[0] + 1, :], (PIECE, LANES))
        for k in kinds[1:]:
            factor = jnp.where(offset >= BOUNDS[k], ratios[k : k + 1, :], factor)
        masters[i, :, :] = gathered[i, PIECE : 2 * PIECE, :] - learn_rate * factor * gathered[i, 0:PIECE, :]
    new_master[...] = masters[mine]
    low = lane_index(20) < LANES // 2
    for k in range(LOCALS // 2):
        base = PAIR_ROWS * k
        flat[base : base + 19, :] = masters[2 * k, 0:19, :]
        shifted[0:1, :] = masters[2 * k, 19:20, :]
        shifted[1:21, :] = pltpu.roll(masters[2 * k + 1, 0:20, :], LANES // 2, 1)
        flat[base + 19 : base + 39, :] = jnp.where(low, shifted[0:20, :], shifted[1:21, :])
    new_params[...] = flat[...].astype(jnp.bfloat16)


def finish(where, tables, gathered):
    return pl.pallas_call(
        final_kernel,
        in_specs=[pl.BlockSpec(memory_space=pltpu.SMEM), whole(), whole()],
        out_specs=[whole()] * 3,
        out_shape=[
            jax.ShapeDtypeStruct((PIECE, LANES), f32),
            jax.ShapeDtypeStruct((NODE_ROWS, LANES), jnp.bfloat16),
            jax.ShapeDtypeStruct((LAYERS, 8, LANES), f32),
        ],
        scratch_shapes=[
            pltpu.VMEM((LOCALS, PIECE, LANES), f32),
            pltpu.VMEM((NODE_ROWS, LANES), f32),
            pltpu.VMEM((24, LANES), f32),
        ],
        compiler_params=params(),
    )(where, tables, gathered)


def padded(vector):
    return jnp.pad(vector, (0, PIECE * LANES - SHARD)).reshape(PIECE, LANES)


def local(partials, master, first, second, acts, up_cot, out_cot, ln_gain):
    core = lax.axis_index("c")
    node = (lax.axis_index("y") * 2 + lax.axis_index("xh")) * 2 + core
    mine = lax.axis_index("xl") * 8 + lax.axis_index("z")
    swap = ((0, 1), (1, 0))
    core_scalar = core.astype(jnp.int32).reshape(1)
    where = jnp.stack([core, node // 2, mine]).astype(jnp.int32)

    grid = partials.reshape(NODES // 2, 2, NODE_ROWS, LANES)
    sent = lax.dynamic_index_in_dim(grid, 1 - core, axis=1, keepdims=False)
    other = lax.ppermute(sent, "c", swap)
    input_grad, parts = norm_backward(acts, up_cot, out_cot, ln_gain)
    parts_other = lax.ppermute(parts, "c", swap)
    chunks = pair_sum(core_scalar, grid, other, parts, parts_other)
    chunks = chunks.reshape(NODES, CHUNK_PAD, LANES)
    blocks = lax.all_to_all(chunks, ("y", "xh", "xl"), 0, 0, tiled=True)
    pieces = lax.all_to_all(split_sum(blocks), "z", 0, 0, tiled=True)
    new_first, new_second, message = step(pieces, padded(master), padded(first), padded(second))
    gathered = lax.all_to_all(message, ("xl", "z"), 0, 0, tiled=True)
    tables = lax.all_to_all(node_sums(core_scalar, gathered), ("y", "xh", "c"), 0, 0, tiled=True)
    new_master, new_params, trust = finish(where, tables, gathered)

    def flat(piece):
        return piece.reshape(PIECE * LANES)[:SHARD]

    return (
        flat(new_master),
        flat(new_first),
        flat(new_second),
        new_params.reshape(NODE_PART),
        trust[:, :, 0].reshape(8 * LAYERS),
        input_grad,
    )


def solution(mesh):
    fine = Mesh(mesh.devices.reshape(4, 2, 2, 2, 8), ("y", "xh", "c", "xl", "z"))
    every = ("y", "xh", "c", "xl", "z")
    in_specs = (P(every, None), P(every), P(every), P(every), P(every, None), P(every, None), P(every, None), P())
    out_specs = (P(every), P(every), P(every), P(("y", "xh", "c")), P(), P(every, None))
    return jax.shard_map(local, mesh=fine, in_specs=in_specs, out_specs=out_specs, check_vma=False)
```

time: 453 us -> 87.4 us (0.19); the launches traced: 444 us -> 87 us
  waiting for transfers between devices: 323 us -> 16.3 us
  blocking collectives: 77.5 us -> 36.4 us
  starting transfers between devices: 0.12 us -> 19.7 us
  between operations: 14.6 us -> 0.75 us
  local copies, waits for them, and re-layouts: 18.1 us -> 5.06 us
  other arithmetic: 9.18 us -> 0.08 us
  Pallas kernels: 0 us -> 8.71 us
    unnamed x5 -> x0, waiting for transfers between devices: 253 us -> none
    psum x1 -> x0, blocking collectives: 77.5 us -> none  [local(): update_sq = lax.psum(update_part, ('node', 'local'))]
    reduce_scatter x1 -> x0, waiting for transfers between devices: 69.7 us -> none  [local(): within = lax.psum_scatter(grid, 'local', scatter_dimension=1, tiled=True)]
    all_to_all x0 -> x2, blocking collectives: none -> 36.4 us  [the longest x1 24.6 us: local(): blocks = lax.all_to_all(chunks, ('y', 'xh', 'xl'), 0, 0, tiled=True)]
    all_to_all x0 -> x2, starting transfers between devices: none -> 16.2 us  [the longest x1 8.19 us: local(): pieces = lax.all_to_all(split_sum(blocks), 'z', 0, 0, tiled=True)]
    all_to_all x0 -> x2, waiting for transfers between devices: none -> 15.2 us  [the longest x1 7.66 us: local(): lax.all_to_all(node_sums(core_scalar, gathered), ('y', 'xh', 'c'), 0, 0,...]
    pallas_call x0 -> x6, Pallas kernels: none -> 8.71 us  [the longest x1 4.66 us: norm_backward(): pl.pallas_call(norm_kernel, grid=(tokens // TOKENS_STEP,), in_specs=[bloc...]
    reshape x3, local copies, waits for them, and re-layouts: 7.1 us -> 0.03 us  [the longest x1 0.02 us: norm_backward(): gain.reshape(1, D)]
  transfers between devices with their start and end apart: 3 -> 4, of which waited for: 3 -> 3; matrix products, arithmetic and copies ran while one was open for 0% -> 0% of each run, Pallas kernels for 0% -> 5%
where the time goes in v1:
time: 87.4 us; the launch traced here: 87 us
  blocking collectives  36.4 us (42%)
  starting transfers between devices  19.7 us (23%)
  waiting for transfers between devices  16.3 us (19%)
  Pallas kernels  8.71 us (10%)
  local copies, waits for them, and re-layouts  5.06 us (6%)
    all_to_all x1, blocking collectives, local(): blocks = lax.all_to_all(chunks, ('y', 'xh', 'xl'), 0, 0, tiled=True)  24.6 us
    all_to_all x1, blocking collectives, local(): gathered = lax.all_to_all(message, ('xl', 'z'), 0, 0, tiled=True)  11.8 us
    all_to_all x1, starting transfers between devices, local(): pieces = lax.all_to_all(split_sum(blocks), 'z', 0, 0, tiled=True)  8.19 us
    all_to_all x1, starting transfers between devices, local(): lax.all_to_all(node_sums(core_scalar, gathered), ('y', 'xh', 'c'), 0, 0,...  8.01 us
    all_to_all x1, waiting for transfers between devices, local(): lax.all_to_all(node_sums(core_scalar, gathered), ('y', 'xh', 'c'), 0, 0,...  7.66 us
    all_to_all x1, waiting for transfers between devices, local(): pieces = lax.all_to_all(split_sum(blocks), 'z', 0, 0, tiled=True)  7.53 us
    pallas_call x1, Pallas kernels, norm_backward(): pl.pallas_call(norm_kernel, grid=(tokens // TOKENS_STEP,), in_specs=[bloc...  4.66 us
    ppermute x1, starting transfers between devices, local(): other = lax.ppermute(sent, 'c', swap)  3.33 us
  transfers between devices with their start and end apart: 4, of which 3 were waited for; matrix products, arithmetic and copies ran while one was open for 0% of the time, Pallas kernels for 5%

profile of v1, /device:TPU:1, one launch (start us, length us, event | category | flops | bytes accessed | tf_op | source)
XLA Modules:
  0.0 87.0 jit_solution(6989814801546984347)
XLA Ops:
  0.6 0.0 copy-start.5
  0.6 0.0 copy-start.1
  0.7 1.5 %dynamic-slice_bitcast_fusion = f32[8,312,128]{2,1,0:T(8,128)S(1)} fusion(f32[8,2,312,128]{3,2,1,0:T(8,128)} %bitcast.20, s32[]{:T(128)S(6)} %select_n.10), kind=kLoop, calls=%fused_computation | loop fusion | bytes 2555908 | tf_op jit(solution)/shard_map/jit(dynamic_index_in_dim)/squeeze | solution.py:319
  2.2 3.3 %collective-permute-start = (f32[8,312,128]{2,1,0:T(8,128)S(1)}, f32[8,312,128]{2,1,0:T(8,128)S(1)}, u32[]{:S(2)}, u32[]{:S(2)}) collective-permute-start(f32[8,312,128]{2,1,0:T(8,128)S(1)} %dynamic-slice_bitcast_fusion), channel_id=1, source_target_pairs={{0,16},{16,0},{1,17},{17,1},{2,18},{18,2},{3,19},{19,3},{4,20},{20... | collective-permute-start | bytes 3833864 | tf_op jit(solution)/shard_map/ppermute | solution.py:320
  5.5 0.0 copy-done.5
  5.5 0.0 copy-done.1
  5.5 0.0 copy-start.2
  5.5 1.4 %copy-done.2 = bf16[128,6144]{1,0:T(8,128)(2,1)S(1)} copy-done((bf16[128,6144]{1,0:T(8,128)(2,1)S(1)}, bf16[128,6144]{1,0:T(8,128)(2,1)}, u32[]{:S(2)}) %copy-start.2) | copy-done | bytes 1572888
  6.9 0.0 copy-start.3
  6.9 1.4 %copy-done.3 = bf16[128,6144]{1,0:T(8,128)(2,1)S(1)} copy-done((bf16[128,6144]{1,0:T(8,128)(2,1)S(1)}, bf16[128,6144]{1,0:T(8,128)(2,1)}, u32[]{:S(2)}) %copy-start.3) | copy-done | bytes 1572888
  8.4 0.0 copy-start
  8.4 4.7 %shard_map.127 = (bf16[128,6144]{1,0:T(8,128)(2,1)}, f32[144,128]{1,0:T(8,128)S(1)}) custom-call(bf16[128,6144]{1,0:T(8,128)(2,1)S(1)} %copy-done.1, bf16[128,6144]{1,0:T(8,128)(2,1)S(1)} %copy-done.2, bf16[128,6144]{1,0:T(8,128)(2,1)S(1)} %copy-done.3, bf16[1,6144]{1,0:T(2,128)(2,1)S(1)} %reshape.44.gain), custom_call_target="tpu_custom_call" | custom-call | flops 23592960 | bytes 6291456 | tf_op jit(solution)/shard_map/pallas_call | solution.py:101
  13.0 0.1 collective-permute-start.1
  13.2 1.1 %collective-permute-done.1.parts_other = f32[144,128]{1,0:T(8,128)S(1)} collective-permute-done((f32[144,128]{1,0:T(8,128)S(1)}, f32[144,128]{1,0:T(8,128)S(1)}, u32[]{:S(2)}, u32[]{:S(2)}) %collective-permute-start.1) | collective-permute-done | bytes 73760 | tf_op jit(solution)/shard_map/ppermute | solution.py:322
  14.3 0.0 collective-permute-done.other
  14.3 0.0 copy-done
  14.3 0.3 shard_map.128
  14.6 0.0 copy-start.4
  14.7 0.0 copy-start.6
  14.7 0.0 copy-start.7
  14.7 24.6 %all_to_all.20.blocks = f32[16,160,128]{2,1,0:T(8,128)S(1)} all-to-all(f32[16,160,128]{2,1,0:T(8,128)S(1)} %bitcast.22), channel_id=1, replica_groups=mesh['y'=4,'xh'=2,'c'=2,'xl'=2,'z'=8] {'y','xh','xl'}, dimensions={0} | all-to-all | bytes 2621440 | tf_op jit(solution)/shard_map/all_to_all | solution.py:325
  39.3 0.8 shard_map.129
  40.1 8.2 %all-to-all-start.1 = ((f32[8,24,128]{2,1,0:T(8,128)}), f32[8,24,128]{2,1,0:T(8,128)S(1)}, u32[]{:S(2)}, u32[]{:S(2)}) async-start(f32[8,24,128]{2,1,0:T(8,128)} %shard_map.129), calls=%async_computation.1 | async-start | bytes 196608 | tf_op jit(solution)/shard_map/all_to_all | solution.py:326
  48.2 0.0 copy-done.4
  48.3 0.0 copy-done.6
  48.3 0.0 copy-done.7
  48.3 7.5 %all-to-all-done.1.pieces = f32[8,24,128]{2,1,0:T(8,128)S(1)} async-done(((f32[8,24,128]{2,1,0:T(8,128)}), f32[8,24,128]{2,1,0:T(8,128)S(1)}, u32[]{:S(2)}, u32[]{:S(2)}) %all-to-all-start.1) | async-done | bytes 98336 | tf_op jit(solution)/shard_map/all_to_all | solution.py:326
  55.8 0.6 shard_map.130
  56.4 11.8 %all_to_all.21.gathered = f32[16,48,128]{2,1,0:T(8,128)S(1)} all-to-all(f32[16,48,128]{2,1,0:T(8,128)S(1)} %get-tuple-element.15), channel_id=1, replica_groups=mesh['y'=4,'xh'=2,'c'=2,'xl'=2,'z'=8] {'xl','z'}, dimensions={0} | all-to-all | bytes 786432 | tf_op jit(solution)/shard_map/all_to_all | solution.py:328
  68.3 0.9 shard_map.131
  69.1 8.0 %all-to-all-start.3 = ((f32[16,16,128]{2,1,0:T(8,128)}), f32[16,16,128]{2,1,0:T(8,128)S(1)}, u32[]{:S(2)}, u32[]{:S(2)}) async-start(f32[16,16,128]{2,1,0:T(8,128)} %shard_map.131), calls=%async_computation.3 | async-start | bytes 262144 | tf_op jit(solution)/shard_map/all_to_all | solution.py:329
  77.1 0.1 pad_add_fusion.where
  77.2 7.7 %all-to-all-done.3.tables = f32[16,16,128]{2,1,0:T(8,128)S(1)} async-done(((f32[16,16,128]{2,1,0:T(8,128)}), f32[16,16,128]{2,1,0:T(8,128)S(1)}, u32[]{:S(2)}, u32[]{:S(2)}) %all-to-all-start.3) | async-done | bytes 131104 | tf_op jit(solution)/shard_map/all_to_all | solution.py:329
  84.9 1.4 %shard_map.132 = (f32[24,128]{1,0:T(8,128)}, bf16[312,128]{1,0:T(8,128)(2,1)}, f32[8,8,128]{2,1,0:T(8,128)S(1)}) custom-call(s32[3]{0:T(128)S(1)} %pad_add_fusion.where, f32[16,16,128]{2,1,0:T(8,128)S(1)} %all-to-all-done.3.tables, f32[16,48,128]{2,1,0:T(8,128)S(1)} %all_to_all.21.gathered), custom_call_target="tpu_custom_call" | custom-call | tf_op jit(solution)/shard_map/pallas_call | solution.py:288
  86.3 0.1 slice_reduce_fusion
  86.4 0.6 reshape_squeeze.3
  (3 shorter events, 0.0 us)
Async XLA Ops:
  0.6 4.9 %copy-start.5 = (bf16[6144]{0:T(1024)(128)(2,1)S(1)}, bf16[6144]{0:T(1024)(128)(2,1)}, u32[]{:S(2)}) copy-start(bf16[6144]{0:T(1024)(128)(2,1)} %param.15) | copy-start | bytes 36868
  0.6 4.9 %copy-start.1 = (bf16[128,6144]{1,0:T(8,128)(2,1)S(1)}, bf16[128,6144]{1,0:T(8,128)(2,1)}, u32[]{:S(2)}) copy-start(bf16[128,6144]{1,0:T(8,128)(2,1)} %acts.1) | copy-start | bytes 4718596
  2.2 12.1 %collective-permute-start = (f32[8,312,128]{2,1,0:T(8,128)S(1)}, f32[8,312,128]{2,1,0:T(8,128)S(1)}, u32[]{:S(2)}, u32[]{:S(2)}) collective-permute-start(f32[8,312,128]{2,1,0:T(8,128)S(1)} %dynamic-slice_bitcast_fusion), channel_id=1, source_target_pairs={{0,16},{16,0},{1,17},{17,1},{2,18},{18,2},{3,19},{19,3},{4,20},{20... | collective-permute-start | bytes 3833864 | tf_op jit(solution)/shard_map/ppermute | solution.py:320
  5.5 1.4 %copy-start.2 = (bf16[128,6144]{1,0:T(8,128)(2,1)S(1)}, bf16[128,6144]{1,0:T(8,128)(2,1)}, u32[]{:S(2)}) copy-start(bf16[128,6144]{1,0:T(8,128)(2,1)} %up.1) | copy-start | bytes 4718596
  6.9 1.4 %copy-start.3 = (bf16[128,6144]{1,0:T(8,128)(2,1)S(1)}, bf16[128,6144]{1,0:T(8,128)(2,1)}, u32[]{:S(2)}) copy-start(bf16[128,6144]{1,0:T(8,128)(2,1)} %out.1) | copy-start | bytes 4718596
  8.4 5.9 %copy-start = (f32[1,638976]{1,0:T(1,128)S(1)}, f32[1,638976]{1,0:T(1,128)}, u32[]{:S(2)}) copy-start(f32[1,638976]{1,0:T(1,128)} %param.8) | copy-start | bytes 7667716
  13.0 1.3 %collective-permute-start.1 = (f32[144,128]{1,0:T(8,128)S(1)}, f32[144,128]{1,0:T(8,128)S(1)}, u32[]{:S(2)}, u32[]{:S(2)}) collective-permute-start(f32[144,128]{1,0:T(8,128)S(1)} %get-tuple-element.14.parts), channel_id=1, source_target_pairs={{0,16},{16,0},{1,17},{17,1},{2,18},{18,2},{3,19},{19,3},{4,20},{20... | collective-permute-start | bytes 221192 | tf_op jit(solution)/shard_map/ppermute | solution.py:322
  14.6 33.6 %copy-start.4 = (f32[2496]{0:T(1024)S(1)}, f32[2496]{0:T(1024)}, u32[]{:S(2)}) copy-start(f32[2496]{0:T(1024)} %param.9) | copy-start | bytes 29956
  14.7 33.6 %copy-start.6 = (f32[2496]{0:T(1024)S(1)}, f32[2496]{0:T(1024)}, u32[]{:S(2)}) copy-start(f32[2496]{0:T(1024)} %param.11) | copy-start | bytes 29956
  14.7 33.6 %copy-start.7 = (f32[2496]{0:T(1024)S(1)}, f32[2496]{0:T(1024)}, u32[]{:S(2)}) copy-start(f32[2496]{0:T(1024)} %param.10) | copy-start | bytes 29956
  40.1 15.8 %all-to-all-start.1 = ((f32[8,24,128]{2,1,0:T(8,128)}), f32[8,24,128]{2,1,0:T(8,128)S(1)}, u32[]{:S(2)}, u32[]{:S(2)}) async-start(f32[8,24,128]{2,1,0:T(8,128)} %shard_map.129), calls=%async_computation.1 | async-start | bytes 196608 | tf_op jit(solution)/shard_map/all_to_all | solution.py:326
  69.1 15.7 %all-to-all-start.3 = ((f32[16,16,128]{2,1,0:T(8,128)}), f32[16,16,128]{2,1,0:T(8,128)S(1)}, u32[]{:S(2)}, u32[]{:S(2)}) async-start(f32[16,16,128]{2,1,0:T(8,128)} %shard_map.131), calls=%async_computation.3 | async-start | bytes 262144 | tf_op jit(solution)/shard_map/all_to_all | solution.py:329

commit v2 on v0

v2 whole, which is shorter than its diff:
```python
import jax
import jax.numpy as jnp
from jax import lax
from jax.experimental import pallas as pl
from jax.experimental.pallas import tpu as pltpu
from jax.sharding import Mesh, PartitionSpec as P

D = 6144
FF = 24576
LAYERS = 8
LENGTH = 9 * D + FF
PARAMS = LAYERS * LENGTH
LANES = 128
NODES = 16
LOCALS = 16
SHARD = PARAMS // (NODES * LOCALS)
NODE_PART = PARAMS // NODES
NODE_ROWS = NODE_PART // LANES
CHUNK_ROWS = NODE_ROWS // 2
CHUNK_PAD = 160
PIECE = 24
QUARTER = LENGTH // 4
SHARD_ROWS = 20
PAIR_ROWS = 2 * SHARD // LANES
BOUNDS = (0, D, 2 * D, 5 * D, 6 * D, 7 * D, 8 * D, 8 * D + FF, LENGTH)

beta_one = 0.9
beta_two = 0.999
adam_epsilon = 1e-06
norm_epsilon = 1e-05
learn_rate = 0.01

f32 = jnp.float32
f16 = jnp.float16
SCALE = 256.0
PARTS_SCALE = 1.0 / 32.0
LOW_SCALE = 2048.0
TOKENS_STEP = 32
COLS = D // LANES
VMEM_LIMIT = 16 * 1024 * 1024
SUMS_VMEM_LIMIT = 55 * 1024 * 1024


def whole():
    return pl.BlockSpec(memory_space=pltpu.VMEM)


def params(limit=VMEM_LIMIT):
    return pltpu.CompilerParams(vmem_limit_bytes=limit)


def cols(j):
    return slice(j * LANES, (j + 1) * LANES)


def wide(column):
    return jnp.broadcast_to(column, (column.shape[0], LANES))


def parts_kernel(acts, up, out, parts, center_rows, inverse_rows, acts_buf, up_buf, out_buf, sums, sems):
    steps = acts.shape[0] // TOKENS_STEP

    def copies(i):
        rows = pl.ds(pl.multiple_of(i * TOKENS_STEP, TOKENS_STEP), TOKENS_STEP)
        pairs = ((acts, acts_buf), (up, up_buf), (out, out_buf))
        return [pltpu.make_async_copy(a.at[rows], b.at[rows], sems.at[k, i]) for k, (a, b) in enumerate(pairs)]

    for i in range(steps):
        for copy in copies(i):
            copy.start()
    sums[...] = jnp.zeros_like(sums)

    def fold(v):
        return jnp.sum(v.reshape(TOKENS_STEP // 8, 8, LANES), axis=0)

    def body(i, carry):
        rows = pl.ds(pl.multiple_of(i * TOKENS_STEP, TOKENS_STEP), TOKENS_STEP)
        for copy in copies(i):
            copy.wait()
        total = jnp.zeros((TOKENS_STEP, LANES), f32)
        for j in range(COLS):
            total = total + acts_buf[rows, cols(j)].astype(f32)
        center = wide(jnp.sum(total, axis=1, keepdims=True) * (1.0 / D))
        squares = jnp.zeros((TOKENS_STEP, LANES), f32)
        for j in range(COLS):
            x = acts_buf[rows, cols(j)].astype(f32) - center
            squares = squares + x * x
        variance = jnp.sum(squares, axis=1, keepdims=True) * (1.0 / D)
        inverse = wide(lax.rsqrt(variance + norm_epsilon))
        center_rows[rows, :] = center
        inverse_rows[rows, :] = inverse
        for j in range(COLS):
            normed = (acts_buf[rows, cols(j)].astype(f32) - center) * inverse
            u = up_buf[rows, cols(j)].astype(f32)
            sums[0, :, cols(j)] += fold(u * normed)
            sums[1, :, cols(j)] += fold(u)
            sums[2, :, cols(j)] += fold(out_buf[rows, cols(j)].astype(f32))
        return carry

    lax.fori_loop(0, steps, body, 0)
    for which in range(3):
        for j in range(COLS):
            row = which * COLS + j
            parts[row : row + 1, :] = jnp.sum(sums[which, :, cols(j)], axis=0, keepdims=True)


def token_sums(acts, up, out):
    tokens = acts.shape[0]
    hbm = pl.BlockSpec(memory_space=pltpu.HBM)
    return pl.pallas_call(
        parts_kernel,
        in_specs=[hbm, hbm, hbm],
        out_specs=[whole()] * 3,
        out_shape=[
            jax.ShapeDtypeStruct((3 * COLS, LANES), f32),
            jax.ShapeDtypeStruct((tokens, LANES), f32),
            jax.ShapeDtypeStruct((tokens, LANES), f32),
        ],
        scratch_shapes=[pltpu.VMEM((tokens, D), jnp.bfloat16)] * 3
        + [pltpu.VMEM((3, 8, D), f32), pltpu.SemaphoreType.DMA((3, tokens // TOKENS_STEP))],
        compiler_params=params(SUMS_VMEM_LIMIT),
        cost_estimate=pl.CostEstimate(flops=15 * tokens * D, bytes_accessed=6 * tokens * D, transcendentals=0),
    )(acts, up, out)


def grad_kernel(acts, up, out, gain, center_rows, inverse_rows, grad):
    rows = acts.shape[0]
    center = center_rows[...]
    inverse = inverse_rows[...]
    scaled = jnp.zeros((rows, LANES), f32)
    cross = jnp.zeros((rows, LANES), f32)
    for j in range(COLS):
        s = up[:, cols(j)].astype(f32) * gain[:, cols(j)].astype(f32)
        scaled = scaled + s
        cross = cross + s * (acts[:, cols(j)].astype(f32) - center)
    mean_scaled = wide(jnp.sum(scaled, axis=1, keepdims=True) * (1.0 / D))
    mean_cross = wide(jnp.sum(cross, axis=1, keepdims=True) * (1.0 / D)) * inverse
    for j in range(COLS):
        normed = (acts[:, cols(j)].astype(f32) - center) * inverse
        s = up[:, cols(j)].astype(f32) * gain[:, cols(j)].astype(f32)
        inner = s - mean_scaled - normed * mean_cross
        grad[:, cols(j)] = (out[:, cols(j)].astype(f32) + inverse * inner).astype(jnp.bfloat16)


def input_gradient(acts, up, out, gain, center_rows, inverse_rows):
    tokens = acts.shape[0]
    block = pl.BlockSpec((TOKENS_STEP, D), lambda i: (i, 0))
    rows = pl.BlockSpec((TOKENS_STEP, LANES), lambda i: (i, 0))
    return pl.pallas_call(
        grad_kernel,
        grid=(tokens // TOKENS_STEP,),
        in_specs=[block, block, block, pl.BlockSpec((1, D), lambda i: (0, 0)), rows, rows],
        out_specs=block,
        out_shape=jax.ShapeDtypeStruct((tokens, D), jnp.bfloat16),
        compiler_params=params(),
        cost_estimate=pl.CostEstimate(flops=15 * tokens * D, bytes_accessed=8 * tokens * D, transcendentals=0),
    )(acts, up, out, gain.reshape(1, D), center_rows, inverse_rows)


def pair_kernel(core, grid, other, parts, parts_other, result, own_buf, other_buf, parts_buf, sems, parts_sems):
    own_copies = [
        pltpu.make_async_copy(grid.at[i, core[0]], own_buf.at[i], sems.at[0, i]) for i in range(NODES // 2)
    ]
    other_copies = [pltpu.make_async_copy(other.at[i], other_buf.at[i], sems.at[1, i]) for i in range(NODES // 2)]
    parts_copies = [
        pltpu.make_async_copy(source, parts_buf.at[k], parts_sems.at[k])
        for k, source in enumerate((parts, parts_other))
    ]
    for own, theirs in zip(own_copies, other_copies):
        own.start()
        theirs.start()
    for copy in parts_copies:
        copy.start()

    def pair(i, half, low, high):
        rows = slice(half * CHUNK_ROWS + low, half * CHUNK_ROWS + high)
        return own_buf[i, rows, :] + other_buf[i, rows, :]

    for i in range(NODES // 2):
        own_copies[i].wait()
        other_copies[i].wait()
        for half in range(2):
            result[i, half, 0:CHUNK_ROWS, :] = pair(i, half, 0, CHUNK_ROWS) * SCALE
            result[i, half, CHUNK_ROWS:CHUNK_PAD, :] = jnp.zeros((CHUNK_PAD - CHUNK_ROWS, LANES), f32)
    for copy in parts_copies:
        copy.wait()
    last = NODES // 2 - 1

    def add(half, row, first, count):
        total = parts_buf[0, first : first + count, :] + parts_buf[1, first : first + count, :]
        result[last, half, row : row + count, :] = (pair(last, half, row, row + count) + total) * PARTS_SCALE

    @pl.when(core[0] == 0)
    def _():
        add(1, CHUNK_ROWS - COLS // 2, 0, COLS // 2)

    @pl.when(core[0] == 1)
    def _():
        add(0, 0, COLS // 2, 3 * COLS // 2)
        add(1, CHUNK_ROWS - COLS, 2 * COLS, COLS)


def pair_sum(core, grid, other, parts, parts_other):
    hbm = pl.BlockSpec(memory_space=pltpu.HBM)
    return pl.pallas_call(
        pair_kernel,
        in_specs=[pl.BlockSpec(memory_space=pltpu.SMEM), hbm, hbm, hbm, hbm],
        out_specs=whole(),
        out_shape=jax.ShapeDtypeStruct((NODES // 2, 2, CHUNK_PAD, LANES), f32),
        scratch_shapes=[
            pltpu.VMEM((NODES // 2, NODE_ROWS, LANES), f32),
            pltpu.VMEM((NODES // 2, NODE_ROWS, LANES), f32),
            pltpu.VMEM((2, 3 * COLS, LANES), f32),
            pltpu.SemaphoreType.DMA((2, NODES // 2)),
            pltpu.SemaphoreType.DMA((2,)),
        ],
        compiler_params=params(),
    )(core, grid, other, parts, parts_other)


def lane_index(rows):
    return lax.broadcasted_iota(jnp.int32, (rows, LANES), 1)


def flatten(states, first, flat, shifted):
    low = lane_index(20) < LANES // 2
    for k in range(4):
        base = PAIR_ROWS * k
        flat[base : base + 19, :] = states[2 * k, first : first + 19, :]
        shifted[0:1, :] = states[2 * k, first + 19 : first + 20, :]
        shifted[1:21, :] = pltpu.roll(states[2 * k + 1, first : first + 20, :], LANES // 2, 1)
        flat[base + 19 : base + 39, :] = jnp.where(low, shifted[0:20, :], shifted[1:21, :])
    flat[CHUNK_ROWS:CHUNK_PAD, :] = jnp.zeros((CHUNK_PAD - CHUNK_ROWS, LANES), f32)


def own_shard(flat, z):
    odd = lax.rem(z, 2)
    start = PAIR_ROWS * lax.div(z, 2) + odd * 19
    ahead = flat[pl.ds(start, 20), :]
    behind = flat[pl.ds(start + 1, 20), :]
    moved = pltpu.roll(jnp.where(lane_index(20) >= LANES // 2, ahead, behind), LANES // 2, 1)
    return jnp.where(odd == 1, moved, ahead)


def bounds_of(quarter):
    edges = BOUNDS + (LENGTH,)
    result = []
    for j in range(4):
        edge = jnp.int32(edges[j])
        for q in range(1, 4):
            edge = jnp.where(quarter == q, edges[2 * q + j] - q * QUARTER, edge)
        result.append(edge)
    return result


def place(rows):
    return lax.broadcasted_iota(jnp.int32, (rows, LANES), 0) * LANES + lane_index(rows)


def moments(first, second, grad):
    new_first = beta_one * first + (1.0 - beta_one) * grad
    new_second = beta_two * second + (1.0 - beta_two) * grad * grad
    return new_first, new_second, new_first / (jnp.sqrt(new_second) + adam_epsilon)


def step_kernel(where, total, states, own_first, own_second, new_first, new_second, sent, table, own_update, flats, shifted):
    layer, quarter, z = where[0], where[1], where[2]
    offset = place(CHUNK_PAD)
    for i in range(4):
        flatten(states, SHARD_ROWS * i, flats.at[i], shifted)
    inside = offset + quarter * QUARTER
    added = ((inside >= BOUNDS[4]) & (inside < BOUNDS[6])) | (inside >= BOUNDS[7])
    added = added & (layer == LAYERS - 1)
    grad = total[...] * jnp.where(added, 1.0 / PARTS_SCALE, 1.0 / SCALE)
    update = moments(flats[0], flats[1], grad)[2]
    held = flats[2] + flats[3] * (1.0 / LOW_SCALE)
    sent[0, :, :] = update
    sent[1, :, :] = held
    edges = bounds_of(quarter)
    rows = []
    for value in (held, update):
        square = value * value
        for j in range(3):
            mask = (offset >= edges[j]) & (offset < edges[j + 1])
            rows.append(jnp.sum(jnp.where(mask, square, 0.0), axis=0, keepdims=True))
    sums = jnp.concatenate(rows + [jnp.zeros((2, LANES), f32)], axis=0)
    for i in range(32):
        table[i, :, :] = sums
    flats[0, :, :] = grad
    first, second, update = moments(
        own_first[0:SHARD_ROWS, :], own_second[0:SHARD_ROWS, :], own_shard(flats.at[0], z)
    )
    new_first[0:SHARD_ROWS, :] = first
    new_second[0:SHARD_ROWS, :] = second
    own_update[0:SHARD_ROWS, :] = update


def step(where, total, states, first, second):
    shard = jax.ShapeDtypeStruct((PIECE, LANES), f32)
    return pl.pallas_call(
        step_kernel,
        in_specs=[pl.BlockSpec(memory_space=pltpu.SMEM)] + [whole()] * 4,
        out_specs=[whole()] * 5,
        out_shape=[
            shard,
            shard,
            jax.ShapeDtypeStruct((2, CHUNK_PAD, LANES), f32),
            jax.ShapeDtypeStruct((32, 8, LANES), f32),
            shard,
        ],
        scratch_shapes=[pltpu.VMEM((4, CHUNK_PAD, LANES), f32), pltpu.VMEM((24, LANES), f32)],
        compiler_params=params(),
    )(where, total, states, first, second)


def final_kernel(where, tables, own, other, own_master, own_update, new_master, new_params, trust, factors, flat, ratios):
    layer, quarter, z = where[0], where[1], where[2]
    xlo = lax.rem(quarter, 2)
    weight_rows, update_rows = [], []
    for n in range(LAYERS):
        quarters = [tables[4 * n + q, :, :] for q in range(4)]
        for k in range(8):
            q, j = k // 2, k % 2
            for rows, first in ((weight_rows, 0), (update_rows, 3)):
                value = quarters[q][first + j : first + j + 1, :]
                if j == 0 and q > 0:
                    value = value + quarters[q - 1][first + 2 : first + 3, :]
                rows.append(value)
    weight_sq = jnp.sum(jnp.concatenate(weight_rows, axis=0), axis=1, keepdims=True)
    update_sq = jnp.sum(jnp.concatenate(update_rows, axis=0), axis=1, keepdims=True)
    ratio = jnp.sqrt(weight_sq) / (jnp.sqrt(update_sq) + adam_epsilon)
    ratios[...] = jnp.broadcast_to(ratio, (8 * LAYERS, LANES))
    diagonal = lane_index(8 * LAYERS) == lax.broadcasted_iota(jnp.int32, (8 * LAYERS, LANES), 0)
    trust[...] = jnp.sum(jnp.where(diagonal, ratios[...], 0.0), axis=0, keepdims=True)
    offset = place(CHUNK_PAD)

    def factor_of(q):
        edges = bounds_of(q)
        rows = [ratios[pl.ds(8 * layer + lax.min(2 * q + j, 7), 1), :] for j in range(3)]
        factor = jnp.broadcast_to(rows[0], (CHUNK_PAD, LANES))
        for j in (1, 2):
            factor = jnp.where(offset >= edges[j], rows[j], factor)
        return factor

    factor = factor_of(quarter)
    mine = own[1, :, :] - learn_rate * factor * own[0, :, :]
    theirs = other[1, :, :] - learn_rate * factor_of(quarter + 1 - 2 * xlo) * other[0, :, :]
    flat[0:CHUNK_ROWS, :] = jnp.where(xlo == 0, mine, theirs)[0:CHUNK_ROWS, :]
    flat[CHUNK_ROWS:NODE_ROWS, :] = jnp.where(xlo == 0, theirs, mine)[0:CHUNK_ROWS, :]
    new_params[...] = flat[...].astype(jnp.bfloat16)
    factors[...] = factor
    new_master[0:SHARD_ROWS, :] = (
        own_master[0:SHARD_ROWS, :] - learn_rate * own_shard(factors, z) * own_update[0:SHARD_ROWS, :]
    )


def finish(where, tables, own, other, master, update):
    return pl.pallas_call(
        final_kernel,
        in_specs=[pl.BlockSpec(memory_space=pltpu.SMEM)] + [whole()] * 5,
        out_specs=[whole()] * 3,
        out_shape=[
            jax.ShapeDtypeStruct((PIECE, LANES), f32),
            jax.ShapeDtypeStruct((NODE_ROWS, LANES), jnp.bfloat16),
            jax.ShapeDtypeStruct((1, LANES), f32),
        ],
        scratch_shapes=[
            pltpu.VMEM((CHUNK_PAD, LANES), f32),
            pltpu.VMEM((NODE_ROWS, LANES), f32),
            pltpu.VMEM((8 * LAYERS, LANES), f32),
        ],
        compiler_params=params(),
    )(where, tables, own, other, master, update)


def padded(vector):
    return jnp.pad(vector, (0, PIECE * LANES - SHARD)).reshape(PIECE, LANES)


def local(partials, master, first, second, acts, up_cot, out_cot, ln_gain):
    core = lax.axis_index("c")
    layer = lax.axis_index("y") * 2 + lax.axis_index("xh")
    quarter = core * 2 + lax.axis_index("xl")
    swap = ((0, 1), (1, 0))
    core_scalar = core.astype(jnp.int32).reshape(1)
    where = jnp.stack([layer, quarter, lax.axis_index("z")]).astype(jnp.int32)

    grid = partials.reshape(NODES // 2, 2, NODE_ROWS, LANES)
    sent = lax.dynamic_index_in_dim(grid, 1 - core, axis=1, keepdims=False)
    other = lax.ppermute(sent, "c", swap)
    parts, center_rows, inverse_rows = token_sums(acts, up_cot, out_cot)
    parts_other = lax.ppermute(parts, "c", swap)
    chunks = pair_sum(core_scalar, grid, other, parts, parts_other)
    input_grad = input_gradient(acts, up_cot, out_cot, ln_gain, center_rows, inverse_rows)
    chunks = chunks.reshape(NODES, CHUNK_PAD, LANES).astype(f16)

    master, first, second = padded(master), padded(first), padded(second)
    high = master.astype(f16)
    low = ((master - high.astype(f32)) * LOW_SCALE).astype(f16)
    states = [v[0:SHARD_ROWS, :] for v in (first.astype(f16), second.astype(f16), high, low)]
    states = jnp.concatenate(states, axis=0)
    chunks, states, master, first, second, where = lax.optimization_barrier(
        (chunks, states, master, first, second, where)
    )
    blocks = lax.all_to_all(chunks, ("y", "xh", "xl"), 0, 0, tiled=True)
    plane = jnp.sum(blocks.astype(f32), axis=0).astype(f16)
    plane, input_grad = lax.optimization_barrier((plane, input_grad))
    message = jnp.concatenate([plane, states], axis=0)
    message = jnp.broadcast_to(message[None], (8,) + message.shape)
    pieces = lax.all_to_all(message, "z", 0, 0, tiled=True)
    total = jnp.sum(pieces[:, :CHUNK_PAD].astype(f32), axis=0)
    states = pieces[:, CHUNK_PAD:].astype(f32)
    new_first, new_second, stepped, table, update = step(where, total, states, first, second)
    other = lax.ppermute(stepped, "xl", swap)
    tables = lax.all_to_all(table, ("y", "xh", "c", "xl"), 0, 0, tiled=True)
    new_master, new_params, trust = finish(where, tables, stepped, other, master, update)

    def flat(piece):
        return piece.reshape(PIECE * LANES)[:SHARD]

    return (
        flat(new_master),
        flat(new_first),
        flat(new_second),
        new_params.reshape(NODE_PART),
        trust.reshape(LANES)[: 8 * LAYERS],
        input_grad,
    )


def solution(mesh):
    fine = Mesh(mesh.devices.reshape(4, 2, 2, 2, 8), ("y", "xh", "c", "xl", "z"))
    every = ("y", "xh", "c", "xl", "z")
    in_specs = (P(every, None), P(every), P(every), P(every), P(every, None), P(every, None), P(every, None), P())
    out_specs = (P(every), P(every), P(every), P(("y", "xh", "c")), P(), P(every, None))
    return jax.shard_map(local, mesh=fine, in_specs=in_specs, out_specs=out_specs, check_vma=False)
```

time: 453 us -> 76.6 us (0.17); the launches traced: 444 us -> 76.2 us
  waiting for transfers between devices: 323 us -> 8.83 us
  blocking collectives: 77.5 us -> 36.9 us
  between operations: 14.6 us -> 0.85 us
  Pallas kernels: 0 us -> 12.8 us
  local copies, waits for them, and re-layouts: 18.1 us -> 5.37 us
  starting transfers between devices: 0.12 us -> 9.1 us
  other arithmetic: 9.18 us -> 2.37 us
    unnamed x5 -> x0, waiting for transfers between devices: 253 us -> none
    psum x1 -> x0, blocking collectives: 77.5 us -> none  [local(): update_sq = lax.psum(update_part, ('node', 'local'))]
    reduce_scatter x1 -> x0, waiting for transfers between devices: 69.7 us -> none  [local(): within = lax.psum_scatter(grid, 'local', scatter_dimension=1, tiled=True)]
    all_to_all x0 -> x2, blocking collectives: none -> 36.9 us  [the longest x1 22.4 us: local(): pieces = lax.all_to_all(message, 'z', 0, 0, tiled=True)]
    pallas_call x0 -> x5, Pallas kernels: none -> 12.8 us  [the longest x1 4 us: token_sums(): pl.pallas_call(parts_kernel, in_specs=[hbm, hbm, hbm], out_specs=[whole()...]
    all_to_all x0 -> x1, waiting for transfers between devices: none -> 7.7 us  [local(): blocks = lax.all_to_all(chunks, ('y', 'xh', 'xl'), 0, 0, tiled=True)]
    reshape x3, local copies, waits for them, and re-layouts: 7.1 us -> 0.02 us  [the longest x1 0.02 us: input_gradient(): gain.reshape(1, D)]
    unnamed x32 -> x22, local copies, waits for them, and re-layouts: 8.46 us -> 2.33 us
  transfers between devices with their start and end apart: 3 -> 4, of which waited for: 3 -> 2; matrix products, arithmetic and copies ran while one was open for 0% -> 0% of each run, Pallas kernels for 0% -> 9%
where the time goes in v2:
time: 76.6 us; the launch traced here: 76.2 us
  blocking collectives  36.9 us (48%)
  Pallas kernels  12.8 us (17%)
  starting transfers between devices  9.1 us (12%)
  waiting for transfers between devices  8.83 us (12%)
  local copies, waits for them, and re-layouts  5.37 us (7%)
  other arithmetic  2.37 us (3%)
  between operations  0.85 us (1%)
    all_to_all x1, blocking collectives, local(): pieces = lax.all_to_all(message, 'z', 0, 0, tiled=True)  22.4 us
    all_to_all x1, blocking collectives, local(): tables = lax.all_to_all(table, ('y', 'xh', 'c', 'xl'), 0, 0, tiled=True)  14.5 us
    all_to_all x1, waiting for transfers between devices, local(): blocks = lax.all_to_all(chunks, ('y', 'xh', 'xl'), 0, 0, tiled=True)  7.7 us
    all_to_all x1, starting transfers between devices, local(): blocks = lax.all_to_all(chunks, ('y', 'xh', 'xl'), 0, 0, tiled=True)  5.24 us
    pallas_call x1, Pallas kernels, token_sums(): pl.pallas_call(parts_kernel, in_specs=[hbm, hbm, hbm], out_specs=[whole()...  4 us
    ppermute x1, starting transfers between devices, local(): other = lax.ppermute(sent, 'c', swap)  3.33 us
    pallas_call x1, Pallas kernels, input_gradient(): pl.pallas_call(grad_kernel, grid=(tokens // TOKENS_STEP,), in_specs=[bloc...  3.19 us
    pallas_call x1, Pallas kernels, pair_sum(): pl.pallas_call(pair_kernel, in_specs=[pl.BlockSpec(memory_space=pltpu.SME...  2.8 us
  transfers between devices with their start and end apart: 4, of which 2 were waited for; matrix products, arithmetic and copies ran while one was open for 0% of the time, Pallas kernels for 9%

profile of v2, /device:TPU:1, one launch (start us, length us, event | category | flops | bytes accessed | tf_op | source)
XLA Modules:
  0.0 76.2 jit_solution(7813098610779415008)
XLA Ops:
  0.6 2.4 %dynamic-slice_bitcast_fusion = f32[8,312,128]{2,1,0:T(8,128)} fusion(f32[8,2,312,128]{3,2,1,0:T(8,128)} %bitcast.26, s32[]{:T(128)S(6)} %select_n.4), kind=kLoop, calls=%fused_computation.1 | loop fusion | bytes 2555908 | tf_op jit(solution)/shard_map/jit(dynamic_index_in_dim)/squeeze | solution.py:389
  3.1 0.0 copy-start.7
  3.1 0.0 copy-start.8
  3.1 0.0 copy-start.9
  3.1 0.0 copy-start.3
  3.1 3.3 %collective-permute-start = (f32[8,312,128]{2,1,0:T(8,128)}, f32[8,312,128]{2,1,0:T(8,128)}, u32[]{:S(2)}, u32[]{:S(2)}) collective-permute-start(f32[8,312,128]{2,1,0:T(8,128)} %dynamic-slice_bitcast_fusion), channel_id=1, source_target_pairs={{0,16},{16,0},{1,17},{17,1},{2,18},{18,2},{3,19},{19,3},{4,20},{20... | collective-permute-start | bytes 3833864 | tf_op jit(solution)/shard_map/ppermute | solution.py:390
  6.4 4.0 %shard_map.127 = (f32[144,128]{1,0:T(8,128)}, f32[128,128]{1,0:T(8,128)}, f32[128,128]{1,0:T(8,128)}) custom-call(bf16[128,6144]{1,0:T(8,128)(2,1)} %acts.3, bf16[128,6144]{1,0:T(8,128)(2,1)} %up.3, bf16[128,6144]{1,0:T(8,128)(2,1)} %out.3), custom_call_target="tpu_custom_call" | custom-call | flops 11796480 | bytes 4718592 | tf_op jit(solution)/shard_map/pallas_call | solution.py:110
  10.4 0.3 collective-permute-start.1
  10.7 0.0 copy-done.7
  10.7 0.0 copy-done.8
  10.7 0.0 copy-done.9
  10.8 0.1 pad_add_fusion.where
  10.9 1.1 %collective-permute-done.1.parts_other = f32[144,128]{1,0:T(8,128)S(1)} collective-permute-done((f32[144,128]{1,0:T(8,128)}, f32[144,128]{1,0:T(8,128)S(1)}, u32[]{:S(2)}, u32[]{:S(2)}) %collective-permute-start.1) | collective-permute-done | bytes 73760 | tf_op jit(solution)/shard_map/ppermute | solution.py:392
  12.0 0.0 collective-permute-done.other
  12.0 0.0 copy-done.3
  12.0 0.0 copy-start.4
  12.0 0.9 %copy-done.4 = f32[144,128]{1,0:T(8,128)S(1)} copy-done((f32[144,128]{1,0:T(8,128)S(1)}, f32[144,128]{1,0:T(8,128)}, u32[]{:S(2)}) %copy-start.4) | copy-done | bytes 73752
  12.9 0.0 copy-start.10
  12.9 2.8 %shard_map.128 = f32[8,2,160,128]{3,2,1,0:T(8,128)S(1)} custom-call(s32[1]{0:T(128)} %bitcast.core, f32[8,2,312,128]{3,2,1,0:T(8,128)S(1)} %bitcast.27, f32[8,312,128]{2,1,0:T(8,128)} %collective-permute-done.other, f32[144,128]{1,0:T(8,128)S(1)} %copy-done.4, f32[144,128]{1,0:T(8,128)S(1)} %collective-permute-done.1.parts_other), custom_call_target="tpu_custom_call" | custom-call | tf_op jit(solution)/shard_map/pallas_call | solution.py:205
  15.7 0.0 copy-start
  15.7 0.0 copy-start.1
  15.7 0.0 copy-start.5
  15.7 0.0 copy-start.6
  15.7 1.0 %convert_element_type.37 = f16[8,2,160,128]{3,2,1,0:T(8,128)(2,1)} convert(f32[8,2,160,128]{3,2,1,0:T(8,128)S(1)} %shard_map.128) | non-fusion elementwise | flops 327680 | bytes 1966080 | tf_op jit(solution)/shard_map/convert_element_type | solution.py:395
  16.7 5.2 %all-to-all-start = ((f16[16,160,128]{2,1,0:T(8,128)(2,1)}), f16[16,160,128]{2,1,0:T(8,128)(2,1)}, u32[]{:S(2)}, u32[]{:S(2)}) async-start(f16[16,160,128]{2,1,0:T(8,128)(2,1)} %bitcast.28), calls=%async_computation | async-start | bytes 1310720 | tf_op jit(solution)/shard_map/all_to_all | solution.py:405
  21.9 0.0 copy-done.10
  22.0 0.0 copy-done
  22.0 0.0 copy-done.1
  22.0 0.0 copy-done.5
  22.0 0.0 copy-done.6
  22.0 0.0 copy-start.2
  22.0 1.4 %copy-done.2 = bf16[128,6144]{1,0:T(8,128)(2,1)S(1)} copy-done((bf16[128,6144]{1,0:T(8,128)(2,1)S(1)}, bf16[128,6144]{1,0:T(8,128)(2,1)}, u32[]{:S(2)}) %copy-start.2) | copy-done | bytes 1572888
  23.4 3.2 %shard_map.129 = bf16[128,6144]{1,0:T(8,128)(2,1)} custom-call(bf16[128,6144]{1,0:T(8,128)(2,1)S(1)} %copy-done, bf16[128,6144]{1,0:T(8,128)(2,1)S(1)} %copy-done.1, bf16[128,6144]{1,0:T(8,128)(2,1)S(1)} %copy-done.2, bf16[1,6144]{1,0:T(2,128)(2,1)S(1)} %reshape.52.gain, f32[128,128]{1,0:T(8,128)S(1)} %copy-done.5, f32[128,128]{1,0:T(8,128)S(1)} %copy-done.6), custom_call_target="tpu_custom_call" | custom-call | flops 11796480 | bytes 6291456 | tf_op jit(solution)/shard_map/pallas_call | solution.py:149
  26.6 7.7 %all-to-all-done = f16[16,160,128]{2,1,0:T(8,128)(2,1)} async-done(((f16[16,160,128]{2,1,0:T(8,128)(2,1)}), f16[16,160,128]{2,1,0:T(8,128)(2,1)}, u32[]{:S(2)}, u32[]{:S(2)}) %all-to-all-start) | async-done | bytes 655392 | tf_op jit(solution)/shard_map/all_to_all | solution.py:405
  34.3 1.2 %convert_reduce_fusion = f32[160,128]{1,0:T(8,128)S(1)} fusion(f16[16,160,128]{2,1,0:T(8,128)(2,1)} %all-to-all-done), kind=kLoop, calls=%fused_computation | loop fusion | flops 634880 | bytes 737280 | tf_op jit(solution)/shard_map/reduce_sum | solution.py:406
  35.5 0.1 broadcast_in_dim.2
  35.6 22.4 %all_to_all.15 = f16[8,240,128]{2,1,0:T(8,128)(2,1)S(1)} all-to-all(f16[8,240,128]{2,1,0:T(8,128)(2,1)S(1)} %broadcast_in_dim.2), channel_id=1, replica_groups=mesh['y'=4,'xh'=2,'c'=2,'xl'=2,'z'=8] {'z'}, dimensions={0} | all-to-all | bytes 983040 | tf_op jit(solution)/shard_map/all_to_all | solution.py:410
  58.1 1.4 %shard_map.130 = (f32[24,128]{1,0:T(8,128)}, f32[24,128]{1,0:T(8,128)}, f32[2,160,128]{2,1,0:T(8,128)S(1)}, f32[32,8,128]{2,1,0:T(8,128)S(1)}, f32[24,128]{1,0:T(8,128)S(1)}) custom-call(s32[3]{0:T(128)S(1)} %pad_add_fusion.where, f32[160,128]{1,0:T(8,128)S(1)} %convert_reduce_fusion.1.total, f32[8,80,128]{2,1,0:T(8,128)S(1)} %slice_convert_fusion.states, ...), custom_call_target="tpu_custom_call" | custom-call | tf_op jit(solution)/shard_map/pallas_call | solution.py:300
  59.5 0.3 collective-permute-start.2
  59.8 14.5 %all_to_all.16.tables = f32[32,8,128]{2,1,0:T(8,128)S(1)} all-to-all(f32[32,8,128]{2,1,0:T(8,128)S(1)} %get-tuple-element.34), channel_id=1, replica_groups=mesh['y'=4,'xh'=2,'c'=2,'xl'=2,'z'=8] {'y','xh','c','xl'}, dimensions={0} | all-to-all | bytes 262144 | tf_op jit(solution)/shard_map/all_to_all | solution.py:415
  74.3 0.0 collective-permute-done.2.other
  74.3 1.4 %shard_map.131 = (f32[24,128]{1,0:T(8,128)}, bf16[312,128]{1,0:T(8,128)(2,1)}, f32[1,128]{1,0:T(1,128)S(1)}) custom-call(s32[3]{0:T(128)S(1)} %pad_add_fusion.where, f32[32,8,128]{2,1,0:T(8,128)S(1)} %all_to_all.16.tables, f32[2,160,128]{2,1,0:T(8,128)S(1)} %get-tuple-element.35.own, f32[2,160,128]{2,1,0:T(8,128)S(1)} %collective-permute-done.2.other, ...), custom_call_target="tpu_custom_call" | custom-call | tf_op jit(solution)/shard_map/pallas_call | solution.py:358
  75.7 0.5 slice_bitcast_fusion
  (11 shorter events, 0.2 us)
Async XLA Ops:
  3.1 7.6 %copy-start.7 = (f32[2496]{0:T(1024)S(1)}, f32[2496]{0:T(1024)}, u32[]{:S(2)}) copy-start(f32[2496]{0:T(1024)} %param.11) | copy-start | bytes 29956
  3.1 7.6 %copy-start.8 = (f32[2496]{0:T(1024)S(1)}, f32[2496]{0:T(1024)}, u32[]{:S(2)}) copy-start(f32[2496]{0:T(1024)} %param.10) | copy-start | bytes 29956
  3.1 7.6 %copy-start.9 = (f32[2496]{0:T(1024)S(1)}, f32[2496]{0:T(1024)}, u32[]{:S(2)}) copy-start(f32[2496]{0:T(1024)} %param.9) | copy-start | bytes 29956
  3.1 8.9 %copy-start.3 = (f32[1,638976]{1,0:T(1,128)S(1)}, f32[1,638976]{1,0:T(1,128)}, u32[]{:S(2)}) copy-start(f32[1,638976]{1,0:T(1,128)} %param.8) | copy-start | bytes 7667716
  3.1 8.9 %collective-permute-start = (f32[8,312,128]{2,1,0:T(8,128)}, f32[8,312,128]{2,1,0:T(8,128)}, u32[]{:S(2)}, u32[]{:S(2)}) collective-permute-start(f32[8,312,128]{2,1,0:T(8,128)} %dynamic-slice_bitcast_fusion), channel_id=1, source_target_pairs={{0,16},{16,0},{1,17},{17,1},{2,18},{18,2},{3,19},{19,3},{4,20},{20... | collective-permute-start | bytes 3833864 | tf_op jit(solution)/shard_map/ppermute | solution.py:390
  10.4 1.6 %collective-permute-start.1 = (f32[144,128]{1,0:T(8,128)}, f32[144,128]{1,0:T(8,128)S(1)}, u32[]{:S(2)}, u32[]{:S(2)}) collective-permute-start(f32[144,128]{1,0:T(8,128)} %get-tuple-element.25.parts), channel_id=1, source_target_pairs={{0,16},{16,0},{1,17},{17,1},{2,18},{18,2},{3,19},{19,3},{4,20},{20... | collective-permute-start | bytes 221192 | tf_op jit(solution)/shard_map/ppermute | solution.py:392
  12.0 0.9 %copy-start.4 = (f32[144,128]{1,0:T(8,128)S(1)}, f32[144,128]{1,0:T(8,128)}, u32[]{:S(2)}) copy-start(f32[144,128]{1,0:T(8,128)} %get-tuple-element.25.parts) | copy-start | bytes 221188
  12.9 9.1 %copy-start.10 = (bf16[6144]{0:T(1024)(128)(2,1)S(1)}, bf16[6144]{0:T(1024)(128)(2,1)}, u32[]{:S(2)}) copy-start(bf16[6144]{0:T(1024)(128)(2,1)} %param.15) | copy-start | bytes 36868
  15.7 6.3 %copy-start = (bf16[128,6144]{1,0:T(8,128)(2,1)S(1)}, bf16[128,6144]{1,0:T(8,128)(2,1)}, u32[]{:S(2)}) copy-start(bf16[128,6144]{1,0:T(8,128)(2,1)} %acts.3) | copy-start | bytes 4718596
  15.7 6.3 %copy-start.1 = (bf16[128,6144]{1,0:T(8,128)(2,1)S(1)}, bf16[128,6144]{1,0:T(8,128)(2,1)}, u32[]{:S(2)}) copy-start(bf16[128,6144]{1,0:T(8,128)(2,1)} %up.3) | copy-start | bytes 4718596
  15.7 6.3 %copy-start.5 = (f32[128,128]{1,0:T(8,128)S(1)}, f32[128,128]{1,0:T(8,128)}, u32[]{:S(2)}) copy-start(f32[128,128]{1,0:T(8,128)} %get-tuple-element.28.center_rows) | copy-start | bytes 196612
  15.7 6.3 %copy-start.6 = (f32[128,128]{1,0:T(8,128)S(1)}, f32[128,128]{1,0:T(8,128)}, u32[]{:S(2)}) copy-start(f32[128,128]{1,0:T(8,128)} %get-tuple-element.29.inverse_rows) | copy-start | bytes 196612
  16.7 17.6 %all-to-all-start = ((f16[16,160,128]{2,1,0:T(8,128)(2,1)}), f16[16,160,128]{2,1,0:T(8,128)(2,1)}, u32[]{:S(2)}, u32[]{:S(2)}) async-start(f16[16,160,128]{2,1,0:T(8,128)(2,1)} %bitcast.28), calls=%async_computation | async-start | bytes 1310720 | tf_op jit(solution)/shard_map/all_to_all | solution.py:405
  22.0 1.4 %copy-start.2 = (bf16[128,6144]{1,0:T(8,128)(2,1)S(1)}, bf16[128,6144]{1,0:T(8,128)(2,1)}, u32[]{:S(2)}) copy-start(bf16[128,6144]{1,0:T(8,128)(2,1)} %out.3) | copy-start | bytes 4718596
  59.5 14.8 %collective-permute-start.2 = (f32[2,160,128]{2,1,0:T(8,128)S(1)}, f32[2,160,128]{2,1,0:T(8,128)S(1)}, u32[]{:S(2)}, u32[]{:S(2)}) collective-permute-start(f32[2,160,128]{2,1,0:T(8,128)S(1)} %get-tuple-element.35.own), channel_id=1, source_target_pairs={{0,8},{8,0},{1,9},{9,1},{2,10},{10,2},{3,11},{11,3},{4,12},{12,4},... | collective-permute-start | bytes 491528 | tf_op jit(solution)/shard_map/ppermute | solution.py:414

commit v3 on v2

v3 whole, which is shorter than its diff:
```python
import jax
import jax.numpy as jnp
from jax import lax
from jax.experimental import pallas as pl
from jax.experimental.pallas import tpu as pltpu
from jax.sharding import Mesh, PartitionSpec as P

D = 6144
FF = 24576
LAYERS = 8
LENGTH = 9 * D + FF
PARAMS = LAYERS * LENGTH
LANES = 128
NODES = 16
LOCALS = 16
SHARD = PARAMS // (NODES * LOCALS)
NODE_PART = PARAMS // NODES
NODE_ROWS = NODE_PART // LANES
QUARTER_ROWS = NODE_ROWS // 2
PAIR_ROWS = 2 * SHARD // LANES
SHARD_ROWS = 20
PIECE = 24
GROUP = 4
GROUP_ROWS = GROUP * SHARD_ROWS
QUARTER = LENGTH // 4
BOUNDS = (0, D, 2 * D, 5 * D, 6 * D, 7 * D, 8 * D, 8 * D + FF, LENGTH)

beta_one = 0.9
beta_two = 0.999
adam_epsilon = 1e-06
norm_epsilon = 1e-05
learn_rate = 0.01

f32 = jnp.float32
f16 = jnp.float16
SCALE = 128.0
PARTS_SCALE = 1.0 / 64.0
LOW_SCALE = 2048.0
TOKENS_STEP = 32
COLS = D // LANES
VMEM_LIMIT = 16 * 1024 * 1024


def whole():
    return pl.BlockSpec(memory_space=pltpu.VMEM)


def held(x):
    return pltpu.with_memory_space_constraint(x, pltpu.VMEM)


def away(x):
    return pltpu.with_memory_space_constraint(x, pltpu.HBM)


def params():
    return pltpu.CompilerParams(vmem_limit_bytes=VMEM_LIMIT)


def cols(j):
    return slice(j * LANES, (j + 1) * LANES)


def wide(column):
    return jnp.broadcast_to(column, (column.shape[0], LANES))


def norm_kernel(acts, up, out, gain, grad, parts, acts_buf, up_buf, out_buf, grad_buf, sums, sems, grad_sems):
    steps = acts.shape[0] // TOKENS_STEP

    def rows_of(i):
        return pl.ds(pl.multiple_of(i * TOKENS_STEP, TOKENS_STEP), TOKENS_STEP)

    def loads(i):
        rows = rows_of(i)
        pairs = ((acts, acts_buf), (up, up_buf), (out, out_buf))
        return [pltpu.make_async_copy(a.at[rows], b.at[rows], sems.at[k, i]) for k, (a, b) in enumerate(pairs)]

    def store(i):
        rows = rows_of(i)
        return pltpu.make_async_copy(grad_buf.at[rows], grad.at[rows], grad_sems.at[i])

    for i in range(steps):
        for copy in loads(i):
            copy.start()
    sums[...] = jnp.zeros_like(sums)

    def fold(v):
        return jnp.sum(v.reshape(TOKENS_STEP // 8, 8, LANES), axis=0)

    def body(i, carry):
        rows = rows_of(i)
        for copy in loads(i):
            copy.wait()
        total = jnp.zeros((TOKENS_STEP, LANES), f32)
        for j in range(COLS):
            total = total + acts_buf[rows, cols(j)].astype(f32)
        center = wide(jnp.sum(total, axis=1, keepdims=True) * (1.0 / D))
        squares = jnp.zeros((TOKENS_STEP, LANES), f32)
        scaled = jnp.zeros((TOKENS_STEP, LANES), f32)
        cross = jnp.zeros((TOKENS_STEP, LANES), f32)
        for j in range(COLS):
            x = acts_buf[rows, cols(j)].astype(f32) - center
            s = up_buf[rows, cols(j)].astype(f32) * gain[:, cols(j)].astype(f32)
            squares = squares + x * x
            scaled = scaled + s
            cross = cross + s * x
        variance = jnp.sum(squares, axis=1, keepdims=True) * (1.0 / D)
        inverse_col = lax.rsqrt(variance + norm_epsilon)
        inverse = wide(inverse_col)
        mean_scaled = wide(jnp.sum(scaled, axis=1, keepdims=True) * (1.0 / D))
        mean_cross = wide(jnp.sum(cross, axis=1, keepdims=True) * (1.0 / D) * inverse_col)
        for j in range(COLS):
            normed = (acts_buf[rows, cols(j)].astype(f32) - center) * inverse
            u = up_buf[rows, cols(j)].astype(f32)
            o = out_buf[rows, cols(j)].astype(f32)
            inner = u * gain[:, cols(j)].astype(f32) - mean_scaled - normed * mean_cross
            grad_buf[rows, cols(j)] = (o + inverse * inner).astype(jnp.bfloat16)
            sums[0, :, cols(j)] += fold(u * normed)
            sums[1, :, cols(j)] += fold(u)
            sums[2, :, cols(j)] += fold(o)
        store(i).start()
        return carry

    lax.fori_loop(0, steps, body, 0)
    for which in range(3):
        for j in range(COLS):
            row = which * COLS + j
            parts[row : row + 1, :] = jnp.sum(sums[which, :, cols(j)], axis=0, keepdims=True)
    for i in range(steps):
        store(i).wait()


def norm_backward(acts, up, out, gain):
    tokens = acts.shape[0]
    steps = tokens // TOKENS_STEP
    hbm = pl.BlockSpec(memory_space=pltpu.HBM)
    return pl.pallas_call(
        norm_kernel,
        in_specs=[hbm, hbm, hbm, whole()],
        out_specs=[hbm, whole()],
        out_shape=[
            jax.ShapeDtypeStruct((tokens, D), jnp.bfloat16),
            pltpu.VMEM((3 * COLS, LANES), f32),
        ],
        scratch_shapes=[pltpu.VMEM((tokens, D), jnp.bfloat16)] * 4
        + [
            pltpu.VMEM((3, 8, D), f32),
            pltpu.SemaphoreType.DMA((3, steps)),
            pltpu.SemaphoreType.DMA((steps,)),
        ],
        compiler_params=params(),
        cost_estimate=pl.CostEstimate(flops=30 * tokens * D, bytes_accessed=8 * tokens * D, transcendentals=0),
    )(away(acts), away(up), away(out), gain.reshape(1, D))


def lane_index(rows):
    return lax.broadcasted_iota(jnp.int32, (rows, LANES), 1)


def half_kernel(core, grid, half, sems):
    copies = [
        pltpu.make_async_copy(grid.at[i, 1 - core[0]], half.at[i], sems.at[i]) for i in range(NODES // 2)
    ]
    for copy in copies:
        copy.start()
    for copy in copies:
        copy.wait()


def other_half(core, grid):
    return pl.pallas_call(
        half_kernel,
        in_specs=[pl.BlockSpec(memory_space=pltpu.SMEM), pl.BlockSpec(memory_space=pltpu.HBM)],
        out_specs=whole(),
        out_shape=pltpu.VMEM((NODES // 2, NODE_ROWS, LANES), f32),
        scratch_shapes=[pltpu.SemaphoreType.DMA((NODES // 2,))],
        compiler_params=params(),
    )(core, away(grid))


def pair_kernel(core, grid, other, parts, parts_other, result, total, sems):
    count = NODES // 2
    last = count - 1

    def load(i):
        return pltpu.make_async_copy(grid.at[i, core[0]], total.at[i, 0:NODE_ROWS], sems.at[i])

    for i in range(count):
        load(i).start()
    high = lane_index(SHARD_ROWS) >= LANES // 2

    def add(i):
        load(i).wait()
        total[i, 0:NODE_ROWS, :] = (total[i, 0:NODE_ROWS, :] + other[i]) * SCALE
        total[i, NODE_ROWS : NODE_ROWS + 8, :] = jnp.zeros((8, LANES), f32)

    def pack(i):
        for xl in range(2):
            for z in range(8):
                base = QUARTER_ROWS * xl + PAIR_ROWS * (z // 2)
                if z % 2 == 0:
                    piece = total[i, base : base + SHARD_ROWS, :]
                else:
                    first = base + PAIR_ROWS // 2
                    ahead = total[i, first : first + SHARD_ROWS, :]
                    behind = total[i, first + 1 : first + 1 + SHARD_ROWS, :]
                    piece = pltpu.roll(jnp.where(high, ahead, behind), LANES // 2, 1)
                row = SHARD_ROWS * (z // 2)
                result[i, 2 * xl + z % 2, row : row + SHARD_ROWS, :] = piece

    def body(i, carry):
        add(i)
        pack(i)
        return carry

    lax.fori_loop(0, last, body, 0)
    add(last)

    def join(row, first, count):
        added = parts[first : first + count, :] + parts_other[first : first + count, :]
        sums = total[last, row : row + count, :] * (1.0 / SCALE)
        total[last, row : row + count, :] = (sums + added) * PARTS_SCALE

    @pl.when(core[0] == 0)
    def _():
        join(NODE_ROWS - COLS // 2, 0, COLS // 2)

    @pl.when(core[0] == 1)
    def _():
        join(0, COLS // 2, 3 * COLS // 2)
        join(NODE_ROWS - COLS, 2 * COLS, COLS)

    pack(last)


def pair_sum(core, grid, other, parts, parts_other):
    return pl.pallas_call(
        pair_kernel,
        in_specs=[pl.BlockSpec(memory_space=pltpu.SMEM), pl.BlockSpec(memory_space=pltpu.HBM)] + [whole()] * 3,
        out_specs=whole(),
        out_shape=pltpu.VMEM((NODES // 2, 4, GROUP_ROWS, LANES), f32),
        scratch_shapes=[
            pltpu.VMEM((NODES // 2, NODE_ROWS + 8, LANES), f32),
            pltpu.SemaphoreType.DMA((NODES // 2,)),
        ],
        compiler_params=params(),
    )(core, away(grid), held(other), held(parts), held(parts_other))


def place():
    return lax.broadcasted_iota(jnp.int32, (SHARD_ROWS, LANES), 0) * LANES + lane_index(SHARD_ROWS)


def bounds_of(quarter):
    edges = BOUNDS + (LENGTH,)
    result = []
    for j in range(4):
        edge = jnp.int32(edges[j])
        for q in range(1, 4):
            edge = jnp.where(quarter == q, edges[2 * q + j] - q * QUARTER, edge)
        result.append(edge)
    return result


def moments(first, second, grad):
    new_first = beta_one * first + (1.0 - beta_one) * grad
    new_second = beta_two * second + (1.0 - beta_two) * grad * grad
    return new_first, new_second, new_first / (jnp.sqrt(new_second) + adam_epsilon)


def step_kernel(where, total, states, own_first, own_second, new_first, new_second, sent, table, own_update, grads):
    layer, quarter, zh, zb = where[0], where[1], where[2], where[3]
    edges = bounds_of(quarter)
    inside = place()
    valid = inside < SHARD
    weights = [jnp.zeros((SHARD_ROWS, LANES), f32) for _ in range(3)]
    updates = [jnp.zeros((SHARD_ROWS, LANES), f32) for _ in range(3)]
    for i in range(GROUP):
        rows = slice(SHARD_ROWS * i, SHARD_ROWS * (i + 1))
        offset = inside + (2 * i + zb) * SHARD
        place_in_layer = offset + quarter * QUARTER
        added = ((place_in_layer >= BOUNDS[4]) & (place_in_layer < BOUNDS[6])) | (place_in_layer >= BOUNDS[7])
        added = added & (layer == LAYERS - 1)
        grad = total[rows, :] * jnp.where(added, 1.0 / PARTS_SCALE, 1.0 / SCALE)
        grads[i, 0:SHARD_ROWS, :] = grad
        first, second, high, low = (states[i, SHARD_ROWS * k : SHARD_ROWS * (k + 1), :] for k in range(4))
        update = moments(first, second, grad)[2]
        held = high + low * (1.0 / LOW_SCALE)
        sent[0, rows, :] = update
        sent[1, rows, :] = held
        for value, sums in ((held, weights), (update, updates)):
            square = jnp.where(valid, value * value, 0.0)
            for j in range(3):
                mask = (offset >= edges[j]) & (offset < edges[j + 1])
                sums[j] = sums[j] + jnp.where(mask, square, 0.0)
    lane = lane_index(1)
    row = jnp.zeros((1, LANES), f32)
    for base, sums in ((0, weights), (8, updates)):
        for j in range(3):
            column = jnp.sum(jnp.sum(sums[j], axis=0, keepdims=True), axis=1, keepdims=True)
            row = row + jnp.where(lane == base + 2 * quarter + j, column, 0.0)
    table[...] = jnp.broadcast_to(row, (64, LANES))
    first, second, update = moments(
        own_first[0:SHARD_ROWS, :], own_second[0:SHARD_ROWS, :], grads[zh, 0:SHARD_ROWS, :]
    )
    new_first[0:SHARD_ROWS, :] = first
    new_second[0:SHARD_ROWS, :] = second
    own_update[0:SHARD_ROWS, :] = update


def step(where, total, states, first, second):
    shard = jax.ShapeDtypeStruct((PIECE, LANES), f32)
    return pl.pallas_call(
        step_kernel,
        in_specs=[pl.BlockSpec(memory_space=pltpu.SMEM)] + [whole()] * 4,
        out_specs=[whole()] * 5,
        out_shape=[
            shard,
            shard,
            jax.ShapeDtypeStruct((2, GROUP_ROWS, LANES), f32),
            jax.ShapeDtypeStruct((64, LANES), f32),
            shard,
        ],
        scratch_shapes=[pltpu.VMEM((GROUP, PIECE, LANES), f32)],
        compiler_params=params(),
    )(where, total, states, first, second)


def kinds_of(piece):
    found = set()
    for half in range(2):
        low = half * NODE_PART + piece * SHARD
        high = low + SHARD
        found |= {k for k in range(8) if BOUNDS[k] < high and BOUNDS[k + 1] > low}
    return sorted(found)


def final_kernel(where, tables, own, by_xl, by_zb, by_both, master, update, new_master, new_params, trust,
                 gathered, masters, factors, flat, shifted, ratios):
    layer, quarter, zh, zb = where[0], where[1], where[2], where[3]
    core, xl = lax.div(quarter, 2), lax.rem(quarter, 2)
    for n in range(LAYERS):
        table = jnp.sum(tables[8 * n : 8 * n + 8, :], axis=0, keepdims=True)
        ratios[n : n + 1, :] = table
    roots = jnp.sqrt(ratios[...])
    ratio = roots / (pltpu.roll(roots, LANES - 8, 1) + adam_epsilon)
    ratio = jnp.where(lane_index(8) < 8, ratio, 0.0)
    ratios[...] = ratio
    row = jnp.zeros((1, LANES), f32)
    for n in range(LAYERS):
        line = ratios[n : n + 1, :]
        row = row + (pltpu.roll(line, 8 * n, 1) if n else line)
    trust[...] = row
    mine = ratios[pl.ds(layer, 1), :]
    lane = lane_index(1)
    values = [jnp.sum(jnp.where(lane == k, mine, 0.0), axis=1, keepdims=True) for k in range(8)]
    groups = ((own, xl, zb), (by_xl, 1 - xl, zb), (by_zb, xl, 1 - zb), (by_both, 1 - xl, 1 - zb))
    for source, a, b in groups:
        for i in range(GROUP):
            index = 8 * a + 2 * i + b
            for k in range(2):
                gathered[k, index, 0:SHARD_ROWS, :] = source[k, SHARD_ROWS * i : SHARD_ROWS * (i + 1), :]
    start = core * NODE_PART
    inside = place()
    for i in range(LOCALS):
        offset = inside + (start + i * SHARD)
        kinds = kinds_of(i)
        factor = jnp.broadcast_to(values[kinds[0]], (SHARD_ROWS, LANES))
        for k in kinds[1:]:
            factor = jnp.where(offset >= BOUNDS[k], values[k], factor)
        factors[i, 0:SHARD_ROWS, :] = factor
        masters[i, 0:SHARD_ROWS, :] = (
            gathered[1, i, 0:SHARD_ROWS, :] - learn_rate * factor * gathered[0, i, 0:SHARD_ROWS, :]
        )
    index = 8 * xl + 2 * zh + zb
    new_master[0:SHARD_ROWS, :] = (
        master[0:SHARD_ROWS, :] - learn_rate * factors[index, 0:SHARD_ROWS, :] * update[0:SHARD_ROWS, :]
    )
    low = lane_index(SHARD_ROWS) < LANES // 2
    for k in range(LOCALS // 2):
        base = PAIR_ROWS * k
        flat[base : base + 19, :] = masters[2 * k, 0:19, :]
        shifted[0:1, :] = masters[2 * k, 19:20, :]
        shifted[1:21, :] = pltpu.roll(masters[2 * k + 1, 0:SHARD_ROWS, :], LANES // 2, 1)
        flat[base + 19 : base + 39, :] = jnp.where(low, shifted[0:20, :], shifted[1:21, :])
    new_params[...] = flat[...].astype(jnp.bfloat16)


def finish(where, tables, groups, master, update):
    return pl.pallas_call(
        final_kernel,
        in_specs=[pl.BlockSpec(memory_space=pltpu.SMEM)] + [whole()] * 7,
        out_specs=[whole()] * 3,
        out_shape=[
            jax.ShapeDtypeStruct((PIECE, LANES), f32),
            jax.ShapeDtypeStruct((NODE_ROWS, LANES), jnp.bfloat16),
            jax.ShapeDtypeStruct((1, LANES), f32),
        ],
        scratch_shapes=[
            pltpu.VMEM((2, LOCALS, PIECE, LANES), f32),
            pltpu.VMEM((LOCALS, PIECE, LANES), f32),
            pltpu.VMEM((LOCALS, PIECE, LANES), f32),
            pltpu.VMEM((NODE_ROWS, LANES), f32),
            pltpu.VMEM((PIECE, LANES), f32),
            pltpu.VMEM((LAYERS, LANES), f32),
        ],
        compiler_params=params(),
    )(where, tables, *groups, master, update)


def padded(vector):
    return jnp.pad(vector, (0, PIECE * LANES - SHARD)).reshape(PIECE, LANES)


def local(partials, master, first, second, acts, up_cot, out_cot, ln_gain):
    core = lax.axis_index("c")
    layer = lax.axis_index("y") * 2 + lax.axis_index("xh")
    quarter = core * 2 + lax.axis_index("xl")
    swap = ((0, 1), (1, 0))
    core_scalar = core.astype(jnp.int32).reshape(1)
    where = jnp.stack([layer, quarter, lax.axis_index("zh"), lax.axis_index("zb")]).astype(jnp.int32)

    grid = partials.reshape(NODES // 2, 2, NODE_ROWS, LANES)
    sent = other_half(core_scalar, grid)
    other = lax.ppermute(sent, "c", swap)
    input_grad, parts = norm_backward(acts, up_cot, out_cot, ln_gain)
    parts_other = lax.ppermute(parts, "c", swap)
    chunks = pair_sum(core_scalar, grid, other, parts, parts_other)
    chunks = chunks.reshape(32, GROUP_ROWS, LANES).astype(f16)

    master, first, second = padded(master), padded(first), padded(second)
    high = master.astype(f16)
    low = ((master - high.astype(f32)) * LOW_SCALE).astype(f16)
    states = [v[0:SHARD_ROWS, :] for v in (first.astype(f16), second.astype(f16), high, low)]
    states = jnp.concatenate(states, axis=0)
    chunks, states, master, first, second, where = lax.optimization_barrier(
        (chunks, states, master, first, second, where)
    )
    blocks = lax.all_to_all(chunks, ("y", "xh", "xl", "zb"), 0, 0, tiled=True)
    plane = jnp.sum(blocks.astype(f32), axis=0).astype(f16)
    message = jnp.concatenate([plane, states], axis=0)
    message = jnp.broadcast_to(message[None], (GROUP,) + message.shape)
    pieces = lax.all_to_all(message, "zh", 0, 0, tiled=True)
    total = jnp.sum(pieces[:, :GROUP_ROWS].astype(f32), axis=0)
    states = pieces[:, GROUP_ROWS:].astype(f32)
    new_first, new_second, stepped, table, update = step(where, total, states, first, second)
    groups = [
        stepped,
        lax.ppermute(stepped, "xl", swap),
        lax.ppermute(stepped, "zb", swap),
        lax.ppermute(stepped, ("xl", "zb"), ((0, 3), (3, 0), (1, 2), (2, 1))),
    ]
    tables = lax.all_to_all(table.reshape(64, 1, LANES), ("y", "xh", "c", "xl", "zb"), 0, 0, tiled=True)
    new_master, new_params, trust = finish(where, tables.reshape(64, LANES), groups, master, update)

    def flat(piece):
        return piece.reshape(PIECE * LANES)[:SHARD]

    return (
        flat(new_master),
        flat(new_first),
        flat(new_second),
        new_params.reshape(NODE_PART),
        trust.reshape(LANES)[: 8 * LAYERS],
        input_grad,
    )


def solution(mesh):
    every = ("y", "xh", "c", "xl", "zh", "zb")
    fine = Mesh(mesh.devices.reshape(4, 2, 2, 2, 4, 2), every)
    in_specs = (P(every, None), P(every), P(every), P(every), P(every, None), P(every, None), P(every, None), P())
    out_specs = (P(every), P(every), P(every), P(("y", "xh", "c")), P(), P(every, None))
    return jax.shard_map(local, mesh=fine, in_specs=in_specs, out_specs=out_specs, check_vma=False)
```

time: 76.6 us -> 70.4 us (0.919)
  blocking collectives: 36.9 us -> 49.6 us
  waiting for transfers between devices: 8.83 us -> 1.04 us
  local copies, waits for them, and re-layouts: 5.37 us -> 0.59 us
  starting transfers between devices: 9.1 us -> 6.09 us
  other arithmetic: 2.37 us -> 0.38 us
  Pallas kernels: 12.8 us -> 11.6 us
    all_to_all x2 -> x3, blocking collectives: 36.9 us -> 49.6 us  [the longest x1 19.5 us: local(): blocks = lax.all_to_all(chunks, ('y', 'xh', 'xl', 'zb'), 0, 0, tiled=True)]
    all_to_all x1 -> x0, waiting for transfers between devices: 7.7 us -> none  [local(): blocks = lax.all_to_all(chunks, ('y', 'xh', 'xl'), 0, 0, tiled=True)]
    all_to_all x1 -> x0, starting transfers between devices: 5.24 us -> none  [local(): blocks = lax.all_to_all(chunks, ('y', 'xh', 'xl'), 0, 0, tiled=True)]
    squeeze x1 -> x0, local copies, waits for them, and re-layouts: 2.44 us -> none  [local(): sent = lax.dynamic_index_in_dim(grid, 1 - core, axis=1, keepdims=False)]
    ppermute x1 -> x3, starting transfers between devices: 0.28 us -> 2.65 us  [the longest x1 1.67 us: local(): lax.ppermute(stepped, ('xl', 'zb'), ((0, 3), (3, 0), (1, 2), (2, 1)))]
    unnamed x22 -> x8, local copies, waits for them, and re-layouts: 2.33 us -> 0.02 us
    reduce_sum x1, other arithmetic: 1.19 us -> 0.1 us  [local(): plane = jnp.sum(blocks.astype(f32), axis=0).astype(f16)]
    pallas_call x1, Pallas kernels: 2.8 us -> 1.92 us  [pair_sum(): pl.pallas_call(pair_kernel, in_specs=[pl.BlockSpec(memory_space=pltpu.SME...]
  transfers between devices with their start and end apart: 4 -> 5, of which waited for: 2 -> 1; matrix products, arithmetic and copies ran while one was open for 0% -> 0% of each run, Pallas kernels for 9% -> 8%
where the time goes in v3:
time: 70.4 us; the launch traced here: 70.2 us
  blocking collectives  49.6 us (70%)
  Pallas kernels  11.6 us (16%)
  starting transfers between devices  6.09 us (9%)
  waiting for transfers between devices  1.04 us (1%)
  between operations  0.82 us (1%)
    all_to_all x1, blocking collectives, local(): blocks = lax.all_to_all(chunks, ('y', 'xh', 'xl', 'zb'), 0, 0, tiled=True)  19.5 us
    all_to_all x1, blocking collectives, local(): lax.all_to_all(table.reshape(64, 1, LANES), ('y', 'xh', 'c', 'xl', 'zb'),...  15.7 us
    all_to_all x1, blocking collectives, local(): pieces = lax.all_to_all(message, 'zh', 0, 0, tiled=True)  14.5 us
    pallas_call x1, Pallas kernels, norm_backward(): pl.pallas_call(norm_kernel, in_specs=[hbm, hbm, hbm, whole()], out_specs=...  5.48 us
    ppermute x1, starting transfers between devices, local(): other = lax.ppermute(sent, 'c', swap)  3.33 us
    pallas_call x1, Pallas kernels, pair_sum(): pl.pallas_call(pair_kernel, in_specs=[pl.BlockSpec(memory_space=pltpu.SME...  1.92 us
    ppermute x1, starting transfers between devices, local(): lax.ppermute(stepped, ('xl', 'zb'), ((0, 3), (3, 0), (1, 2), (2, 1)))  1.67 us
    pallas_call x1, Pallas kernels, finish(): pl.pallas_call(final_kernel, in_specs=[pl.BlockSpec(memory_space=pltpu.SM...  1.51 us
  transfers between devices with their start and end apart: 5, of which 1 were waited for; matrix products, arithmetic and copies ran while one was open for 0% of the time, Pallas kernels for 8%

profile of v3, /device:TPU:1, one launch (start us, length us, event | category | flops | bytes accessed | tf_op | source)
XLA Modules:
  0.0 70.2 jit_solution(6190172392658296532)
XLA Ops:
  0.6 0.0 copy-start.2
  0.6 1.4 %shard_map.127 = f32[8,312,128]{2,1,0:T(8,128)S(1)} custom-call(s32[1]{0:T(128)} %bitcast.core, f32[8,2,312,128]{3,2,1,0:T(8,128)} %bitcast.31), custom_call_target="tpu_custom_call" | custom-call | tf_op jit(solution)/shard_map/pallas_call | solution.py:172
  2.1 3.3 %collective-permute-start = (f32[8,312,128]{2,1,0:T(8,128)S(1)}, f32[8,312,128]{2,1,0:T(8,128)S(1)}, u32[]{:S(2)}, u32[]{:S(2)}) collective-permute-start(f32[8,312,128]{2,1,0:T(8,128)S(1)} %shard_map.127), channel_id=1, source_target_pairs={{0,16},{16,0},{1,17},{17,1},{2,18},{18,2},{3,19},{19,3},{4,20},{20... | collective-permute-start | bytes 3833864 | tf_op jit(solution)/shard_map/ppermute | solution.py:426
  5.4 0.0 copy-done.2
  5.5 0.0 copy-start
  5.5 0.0 copy-start.1
  5.5 0.0 copy-start.3
  5.5 5.5 %shard_map.128 = (bf16[128,6144]{1,0:T(8,128)(2,1)}, f32[144,128]{1,0:T(8,128)S(1)}) custom-call(bf16[128,6144]{1,0:T(8,128)(2,1)} %acts.1, bf16[128,6144]{1,0:T(8,128)(2,1)} %up.1, bf16[128,6144]{1,0:T(8,128)(2,1)} %out.1, bf16[1,6144]{1,0:T(2,128)(2,1)S(1)} %reshape.55.gain), custom_call_target="tpu_custom_call" | custom-call | flops 23592960 | bytes 6291456 | tf_op jit(solution)/shard_map/pallas_call | solution.py:138
  11.0 0.1 collective-permute-start.1
  11.1 0.0 copy-done
  11.1 0.0 copy-done.1
  11.1 0.0 copy-done.3
  11.2 0.1 pad_add_fusion.where
  11.3 1.0 %collective-permute-done.1.parts_other = f32[144,128]{1,0:T(8,128)S(1)} collective-permute-done((f32[144,128]{1,0:T(8,128)S(1)}, f32[144,128]{1,0:T(8,128)S(1)}, u32[]{:S(2)}, u32[]{:S(2)}) %collective-permute-start.1) | collective-permute-done | bytes 73760 | tf_op jit(solution)/shard_map/ppermute | solution.py:428
  12.3 0.0 collective-permute-done.other
  12.3 1.9 %shard_map.129 = f32[8,4,80,128]{3,2,1,0:T(8,128)S(1)} custom-call(s32[1]{0:T(128)} %bitcast.core, f32[8,2,312,128]{3,2,1,0:T(8,128)} %bitcast.32, f32[8,312,128]{2,1,0:T(8,128)S(1)} %collective-permute-done.other, f32[144,128]{1,0:T(8,128)S(1)} %get-tuple-element.22.parts, f32[144,128]{1,0:T(8,128)S(1)} %collective-permute-done.1.parts_other), custom_call_target="tpu_custom_call" | custom-call | tf_op jit(solution)/shard_map/pallas_call | solution.py:238
  14.3 0.1 convert_element_type.37
  14.4 19.5 %all_to_all.15 = f16[32,80,128]{2,1,0:T(8,128)(2,1)S(1)} all-to-all(f16[32,80,128]{2,1,0:T(8,128)(2,1)S(1)} %bitcast.33), channel_id=1, replica_groups=mesh['y'=4,'xh'=2,'c'=2,'xl'=2,'zh'=4,'zb'=2] {'y','xh','xl','zb'}, dimensions={0} | all-to-all | bytes 1310720 | tf_op jit(solution)/shard_map/all_to_all | solution.py:440
  33.8 0.1 convert_reduce_fusion
  34.0 14.5 %all_to_all.16 = f16[4,160,128]{2,1,0:T(8,128)(2,1)S(1)} all-to-all(f16[4,160,128]{2,1,0:T(8,128)(2,1)S(1)} %broadcast_in_dim.2), channel_id=1, replica_groups=mesh['y'=4,'xh'=2,'c'=2,'xl'=2,'zh'=4,'zb'=2] {'zh'}, dimensions={0} | all-to-all | bytes 327680 | tf_op jit(solution)/shard_map/all_to_all | solution.py:444
  48.5 1.3 %shard_map.130 = (f32[24,128]{1,0:T(8,128)}, f32[24,128]{1,0:T(8,128)}, f32[2,80,128]{2,1,0:T(8,128)S(1)}, f32[64,128]{1,0:T(8,128)S(1)}, f32[24,128]{1,0:T(8,128)S(1)}) custom-call(s32[4]{0:T(128)S(1)} %pad_add_fusion.where, f32[80,128]{1,0:T(8,128)S(1)} %convert_reduce_fusion.1.total, f32[4,80,128]{2,1,0:T(8,128)S(1)} %slice_convert_fusion.states, ...), custom_call_target="tpu_custom_call" | custom-call | tf_op jit(solution)/shard_map/pallas_call | solution.py:314
  49.8 0.6 collective-permute-start.2
  50.4 0.4 collective-permute-start.3
  50.8 1.7 %collective-permute-start.4 = (f32[2,80,128]{2,1,0:T(8,128)S(1)}, f32[2,80,128]{2,1,0:T(8,128)S(1)}, u32[]{:S(2)}, u32[]{:S(2)}) collective-permute-start(f32[2,80,128]{2,1,0:T(8,128)S(1)} %get-tuple-element.29.own), channel_id=1, source_target_pairs={{0,9},{9,0},{1,8},{8,1},{2,11},{11,2},{3,10},{10,3},{4,13},{13,4},... | collective-permute-start | bytes 245768 | tf_op jit(solution)/shard_map/ppermute | solution.py:452
  52.4 15.7 %all_to_all.17 = f32[64,1,128]{2,1,0:T(1,128)S(1)} all-to-all(f32[64,1,128]{2,1,0:T(1,128)S(1)} %bitcast.30), channel_id=1, replica_groups=mesh['y'=4,'xh'=2,'c'=2,'xl'=2,'zh'=4,'zb'=2] {'y','xh','c','xl','zb'}, dimensions={0} | all-to-all | bytes 65536 | tf_op jit(solution)/shard_map/all_to_all | solution.py:454
  68.1 0.0 collective-permute-done.2.by_xl
  68.1 0.0 collective-permute-done.3.by_zb
  68.1 0.0 collective-permute-done.4.by_both
  68.1 1.5 %shard_map.131 = (f32[24,128]{1,0:T(8,128)}, bf16[312,128]{1,0:T(8,128)(2,1)}, f32[1,128]{1,0:T(1,128)S(1)}) custom-call(s32[4]{0:T(128)S(1)} %pad_add_fusion.where, f32[64,128]{1,0:T(8,128)S(1)} %bitcast.29, f32[2,80,128]{2,1,0:T(8,128)S(1)} %get-tuple-element.29.own, f32[2,80,128]{2,1,0:T(8,128)S(1)} %collective-permute-done.2.by_xl, ...), custom_call_target="tpu_custom_call" | custom-call | tf_op jit(solution)/shard_map/pallas_call | solution.py:391
  69.6 0.5 slice_bitcast_fusion
  (12 shorter events, 0.1 us)
Async XLA Ops:
  0.6 4.8 %copy-start.2 = (bf16[6144]{0:T(1024)(128)(2,1)S(1)}, bf16[6144]{0:T(1024)(128)(2,1)}, u32[]{:S(2)}) copy-start(bf16[6144]{0:T(1024)(128)(2,1)} %param.15) | copy-start | bytes 36868
  2.1 10.2 %collective-permute-start = (f32[8,312,128]{2,1,0:T(8,128)S(1)}, f32[8,312,128]{2,1,0:T(8,128)S(1)}, u32[]{:S(2)}, u32[]{:S(2)}) collective-permute-start(f32[8,312,128]{2,1,0:T(8,128)S(1)} %shard_map.127), channel_id=1, source_target_pairs={{0,16},{16,0},{1,17},{17,1},{2,18},{18,2},{3,19},{19,3},{4,20},{20... | collective-permute-start | bytes 3833864 | tf_op jit(solution)/shard_map/ppermute | solution.py:426
  5.5 5.6 %copy-start = (f32[2496]{0:T(1024)S(1)}, f32[2496]{0:T(1024)}, u32[]{:S(2)}) copy-start(f32[2496]{0:T(1024)} %param.11) | copy-start | bytes 29956
  5.5 5.7 %copy-start.1 = (f32[2496]{0:T(1024)S(1)}, f32[2496]{0:T(1024)}, u32[]{:S(2)}) copy-start(f32[2496]{0:T(1024)} %param.10) | copy-start | bytes 29956
  5.5 5.7 %copy-start.3 = (f32[2496]{0:T(1024)S(1)}, f32[2496]{0:T(1024)}, u32[]{:S(2)}) copy-start(f32[2496]{0:T(1024)} %param.9) | copy-start | bytes 29956
  11.0 1.4 %collective-permute-start.1 = (f32[144,128]{1,0:T(8,128)S(1)}, f32[144,128]{1,0:T(8,128)S(1)}, u32[]{:S(2)}, u32[]{:S(2)}) collective-permute-start(f32[144,128]{1,0:T(8,128)S(1)} %get-tuple-element.22.parts), channel_id=1, source_target_pairs={{0,16},{16,0},{1,17},{17,1},{2,18},{18,2},{3,19},{19,3},{4,20},{20... | collective-permute-start | bytes 221192 | tf_op jit(solution)/shard_map/ppermute | solution.py:428
  49.8 18.3 %collective-permute-start.2 = (f32[2,80,128]{2,1,0:T(8,128)S(1)}, f32[2,80,128]{2,1,0:T(8,128)S(1)}, u32[]{:S(2)}, u32[]{:S(2)}) collective-permute-start(f32[2,80,128]{2,1,0:T(8,128)S(1)} %get-tuple-element.29.own), channel_id=1, source_target_pairs={{0,8},{8,0},{1,9},{9,1},{2,10},{10,2},{3,11},{11,3},{4,12},{12,4},... | collective-permute-start | bytes 245768 | tf_op jit(solution)/shard_map/ppermute | solution.py:450
  50.4 17.7 %collective-permute-start.3 = (f32[2,80,128]{2,1,0:T(8,128)S(1)}, f32[2,80,128]{2,1,0:T(8,128)S(1)}, u32[]{:S(2)}, u32[]{:S(2)}) collective-permute-start(f32[2,80,128]{2,1,0:T(8,128)S(1)} %get-tuple-element.29.own), channel_id=1, source_target_pairs={{0,1},{1,0},{2,3},{3,2},{4,5},{5,4},{6,7},{7,6},{8,9},{9,8},{10,11... | collective-permute-start | bytes 245768 | tf_op jit(solution)/shard_map/ppermute | solution.py:451
  50.8 17.4 %collective-permute-start.4 = (f32[2,80,128]{2,1,0:T(8,128)S(1)}, f32[2,80,128]{2,1,0:T(8,128)S(1)}, u32[]{:S(2)}, u32[]{:S(2)}) collective-permute-start(f32[2,80,128]{2,1,0:T(8,128)S(1)} %get-tuple-element.29.own), channel_id=1, source_target_pairs={{0,9},{9,0},{1,8},{8,1},{2,11},{11,2},{3,10},{10,3},{4,13},{13,4},... | collective-permute-start | bytes 245768 | tf_op jit(solution)/shard_map/ppermute | solution.py:452

commit v4 on v3

v4 whole, which is shorter than its diff:
```python
import jax
import jax.numpy as jnp
from jax import lax
from jax.experimental import pallas as pl
from jax.experimental.pallas import tpu as pltpu
from jax.sharding import Mesh, PartitionSpec as P

D = 6144
FF = 24576
LAYERS = 8
LENGTH = 9 * D + FF
PARAMS = LAYERS * LENGTH
LANES = 128
NODES = 16
LOCALS = 16
SHARD = PARAMS // (NODES * LOCALS)
NODE_PART = PARAMS // NODES
NODE_ROWS = NODE_PART // LANES
QUARTER_ROWS = NODE_ROWS // 2
PAIR_ROWS = 2 * SHARD // LANES
SHARD_ROWS = 20
PIECE = 24
GROUP = 4
GROUP_ROWS = GROUP * SHARD_ROWS
QUARTER = LENGTH // 4
BOUNDS = (0, D, 2 * D, 5 * D, 6 * D, 7 * D, 8 * D, 8 * D + FF, LENGTH)

beta_one = 0.9
beta_two = 0.999
adam_epsilon = 1e-06
norm_epsilon = 1e-05
learn_rate = 0.01

f32 = jnp.float32
f16 = jnp.float16
SCALE = 128.0
PARTS_SCALE = 1.0 / 64.0
LOW_SCALE = 2048.0
TOKENS_STEP = 32
COLS = D // LANES
VMEM_LIMIT = 16 * 1024 * 1024


def whole():
    return pl.BlockSpec(memory_space=pltpu.VMEM)


def held(x):
    return pltpu.with_memory_space_constraint(x, pltpu.VMEM)


def away(x):
    return pltpu.with_memory_space_constraint(x, pltpu.HBM)


def params():
    return pltpu.CompilerParams(vmem_limit_bytes=VMEM_LIMIT)


def cols(j):
    return slice(j * LANES, (j + 1) * LANES)


def wide(column):
    return jnp.broadcast_to(column, (column.shape[0], LANES))


def parts_kernel(acts, up, out, grid, parts, center_rows, inverse_rows, own,
                 acts_buf, up_buf, out_buf, sums, sems, own_sems):
    core = lax.axis_index("c")
    own_copies = [
        pltpu.make_async_copy(grid.at[i, core], own.at[i], own_sems.at[i]) for i in range(NODES // 2)
    ]
    steps = acts.shape[0] // TOKENS_STEP

    def rows_of(i):
        return pl.ds(pl.multiple_of(i * TOKENS_STEP, TOKENS_STEP), TOKENS_STEP)

    def loads(i):
        rows = rows_of(i)
        pairs = ((acts, acts_buf), (up, up_buf), (out, out_buf))
        return [pltpu.make_async_copy(a.at[rows], b.at[rows], sems.at[k, i]) for k, (a, b) in enumerate(pairs)]

    for i in range(steps):
        for copy in loads(i):
            copy.start()
    for copy in own_copies:
        copy.start()
    sums[...] = jnp.zeros_like(sums)

    def fold(v):
        return jnp.sum(v.reshape(TOKENS_STEP // 8, 8, LANES), axis=0)

    def body(i, carry):
        rows = rows_of(i)
        for copy in loads(i):
            copy.wait()
        total = jnp.zeros((TOKENS_STEP, LANES), f32)
        for j in range(COLS):
            total = total + acts_buf[rows, cols(j)].astype(f32)
        center = wide(jnp.sum(total, axis=1, keepdims=True) * (1.0 / D))
        squares = jnp.zeros((TOKENS_STEP, LANES), f32)
        for j in range(COLS):
            x = acts_buf[rows, cols(j)].astype(f32) - center
            squares = squares + x * x
        variance = jnp.sum(squares, axis=1, keepdims=True) * (1.0 / D)
        inverse = wide(lax.rsqrt(variance + norm_epsilon))
        center_rows[rows, :] = center
        inverse_rows[rows, :] = inverse
        for j in range(COLS):
            normed = (acts_buf[rows, cols(j)].astype(f32) - center) * inverse
            u = up_buf[rows, cols(j)].astype(f32)
            sums[0, :, cols(j)] += fold(u * normed)
            sums[1, :, cols(j)] += fold(u)
            sums[2, :, cols(j)] += fold(out_buf[rows, cols(j)].astype(f32))
        return carry

    lax.fori_loop(0, steps, body, 0)
    for which in range(3):
        for j in range(COLS):
            row = which * COLS + j
            parts[row : row + 1, :] = jnp.sum(sums[which, :, cols(j)], axis=0, keepdims=True)
    for copy in own_copies:
        copy.wait()


def token_sums(acts, up, out, grid):
    tokens = acts.shape[0]
    hbm = pl.BlockSpec(memory_space=pltpu.HBM)
    return pl.pallas_call(
        parts_kernel,
        in_specs=[hbm] * 4,
        out_specs=[whole()] * 4,
        out_shape=[
            pltpu.VMEM((3 * COLS, LANES), f32),
            jax.ShapeDtypeStruct((tokens, LANES), f32),
            jax.ShapeDtypeStruct((tokens, LANES), f32),
            pltpu.VMEM((NODES // 2, NODE_ROWS, LANES), f32),
        ],
        scratch_shapes=[pltpu.VMEM((tokens, D), jnp.bfloat16)] * 3
        + [pltpu.VMEM((3, 8, D), f32), pltpu.SemaphoreType.DMA((3, tokens // TOKENS_STEP)), pltpu.SemaphoreType.DMA((NODES // 2,))],
        compiler_params=params(),
        cost_estimate=pl.CostEstimate(flops=15 * tokens * D, bytes_accessed=6 * tokens * D, transcendentals=0),
    )(away(acts), away(up), away(out), away(grid))


def grad_kernel(acts, up, out, gain, center_rows, inverse_rows, grad):
    rows = acts.shape[0]
    center = center_rows[...]
    inverse = inverse_rows[...]
    scaled = jnp.zeros((rows, LANES), f32)
    cross = jnp.zeros((rows, LANES), f32)
    for j in range(COLS):
        s = up[:, cols(j)].astype(f32) * gain[:, cols(j)].astype(f32)
        scaled = scaled + s
        cross = cross + s * (acts[:, cols(j)].astype(f32) - center)
    mean_scaled = wide(jnp.sum(scaled, axis=1, keepdims=True) * (1.0 / D))
    mean_cross = wide(jnp.sum(cross, axis=1, keepdims=True) * (1.0 / D)) * inverse
    for j in range(COLS):
        normed = (acts[:, cols(j)].astype(f32) - center) * inverse
        s = up[:, cols(j)].astype(f32) * gain[:, cols(j)].astype(f32)
        inner = s - mean_scaled - normed * mean_cross
        grad[:, cols(j)] = (out[:, cols(j)].astype(f32) + inverse * inner).astype(jnp.bfloat16)


def input_gradient(acts, up, out, gain, center_rows, inverse_rows):
    tokens = acts.shape[0]
    block = pl.BlockSpec((TOKENS_STEP, D), lambda i: (i, 0))
    rows = pl.BlockSpec((TOKENS_STEP, LANES), lambda i: (i, 0))
    return pl.pallas_call(
        grad_kernel,
        grid=(tokens // TOKENS_STEP,),
        in_specs=[block, block, block, pl.BlockSpec((1, D), lambda i: (0, 0)), rows, rows],
        out_specs=block,
        out_shape=jax.ShapeDtypeStruct((tokens, D), jnp.bfloat16),
        compiler_params=params(),
        cost_estimate=pl.CostEstimate(flops=15 * tokens * D, bytes_accessed=8 * tokens * D, transcendentals=0),
    )(away(acts), away(up), away(out), gain.reshape(1, D), center_rows, inverse_rows)


def lane_index(rows):
    return lax.broadcasted_iota(jnp.int32, (rows, LANES), 1)


def position():
    layer = lax.axis_index("y") * 2 + lax.axis_index("xh")
    return layer, lax.axis_index("c"), lax.axis_index("xl"), lax.axis_index("zh"), lax.axis_index("zb")


def half_kernel(grid, half, sems):
    core = lax.axis_index("c")
    copies = [
        pltpu.make_async_copy(grid.at[i, 1 - core], half.at[i], sems.at[i]) for i in range(NODES // 2)
    ]
    for copy in copies:
        copy.start()
    for copy in copies:
        copy.wait()


def other_half(grid):
    return pl.pallas_call(
        half_kernel,
        in_specs=[pl.BlockSpec(memory_space=pltpu.HBM)],
        out_specs=whole(),
        out_shape=pltpu.VMEM((NODES // 2, NODE_ROWS, LANES), f32),
        scratch_shapes=[pltpu.SemaphoreType.DMA((NODES // 2,))],
        compiler_params=params(),
    )(away(grid))


def pair_kernel(own, other, parts, parts_other, result, total):
    core = lax.axis_index("c")
    count = NODES // 2
    last = count - 1
    high = lane_index(SHARD_ROWS) >= LANES // 2

    def add(i):
        total[0:NODE_ROWS, :] = (own[i] + other[i]) * SCALE
        total[NODE_ROWS : NODE_ROWS + 8, :] = jnp.zeros((8, LANES), f32)

    def pack(i):
        for xl in range(2):
            for z in range(8):
                base = QUARTER_ROWS * xl + PAIR_ROWS * (z // 2)
                if z % 2 == 0:
                    piece = total[base : base + SHARD_ROWS, :]
                else:
                    first = base + PAIR_ROWS // 2
                    ahead = total[first : first + SHARD_ROWS, :]
                    behind = total[first + 1 : first + 1 + SHARD_ROWS, :]
                    piece = pltpu.roll(jnp.where(high, ahead, behind), LANES // 2, 1)
                row = SHARD_ROWS * (z // 2)
                result[i, 2 * xl + z % 2, row : row + SHARD_ROWS, :] = piece

    def body(i, carry):
        add(i)
        pack(i)
        return carry

    lax.fori_loop(0, last, body, 0)
    add(last)

    def join(row, first, count):
        added = parts[first : first + count, :] + parts_other[first : first + count, :]
        sums = own[last, row : row + count, :] + other[last, row : row + count, :]
        total[row : row + count, :] = (sums + added) * PARTS_SCALE

    @pl.when(core == 0)
    def _():
        join(NODE_ROWS - COLS // 2, 0, COLS // 2)

    @pl.when(core == 1)
    def _():
        join(0, COLS // 2, 3 * COLS // 2)
        join(NODE_ROWS - COLS, 2 * COLS, COLS)

    pack(last)


def pair_sum(own, other, parts, parts_other):
    return pl.pallas_call(
        pair_kernel,
        in_specs=[whole()] * 4,
        out_specs=whole(),
        out_shape=pltpu.VMEM((NODES // 2, 4, GROUP_ROWS, LANES), f32),
        scratch_shapes=[pltpu.VMEM((NODE_ROWS + 8, LANES), f32)],
        compiler_params=params(),
    )(held(own), held(other), held(parts), held(parts_other))


def place(rows):
    return lax.broadcasted_iota(jnp.int32, (rows, LANES), 0) * LANES + lane_index(rows)


def bounds_of(quarter):
    edges = BOUNDS + (LENGTH,)
    result = []
    for j in range(4):
        edge = jnp.int32(edges[j])
        for q in range(1, 4):
            edge = jnp.where(quarter == q, edges[2 * q + j] - q * QUARTER, edge)
        result.append(edge)
    return result


def moments(first, second, grad):
    new_first = beta_one * first + (1.0 - beta_one) * grad
    new_second = beta_two * second + (1.0 - beta_two) * grad * grad
    return new_first, new_second, new_first / (jnp.sqrt(new_second) + adam_epsilon)


def step_kernel(total, states, own_first, own_second, new_first, new_second, sent, table, own_update, grads):
    layer, core, xl, zh, zb = position()
    quarter = 2 * core + xl
    edges = bounds_of(quarter)
    inside = place(SHARD_ROWS)
    valid = inside < SHARD
    weights = [jnp.zeros((SHARD_ROWS, LANES), f32) for _ in range(3)]
    updates = [jnp.zeros((SHARD_ROWS, LANES), f32) for _ in range(3)]
    for i in range(GROUP):
        rows = slice(SHARD_ROWS * i, SHARD_ROWS * (i + 1))
        offset = inside + (2 * i + zb) * SHARD
        place_in_layer = offset + quarter * QUARTER
        added = ((place_in_layer >= BOUNDS[4]) & (place_in_layer < BOUNDS[6])) | (place_in_layer >= BOUNDS[7])
        added = added & (layer == LAYERS - 1)
        grad = total[rows, :] * jnp.where(added, 1.0 / PARTS_SCALE, 1.0 / SCALE)
        grads[i, 0:SHARD_ROWS, :] = grad
        first, second, high, low = (states[i, SHARD_ROWS * k : SHARD_ROWS * (k + 1), :] for k in range(4))
        update = moments(first, second, grad)[2]
        held = high + low * (1.0 / LOW_SCALE)
        sent[0, rows, :] = update
        sent[1, rows, :] = held
        for value, sums in ((held, weights), (update, updates)):
            square = jnp.where(valid, value * value, 0.0)
            for j in range(3):
                mask = (offset >= edges[j]) & (offset < edges[j + 1])
                sums[j] = sums[j] + jnp.where(mask, square, 0.0)
    lane = lane_index(1)
    row = jnp.zeros((1, LANES), f32)
    for base, sums in ((0, weights), (8, updates)):
        for j in range(3):
            column = jnp.sum(jnp.sum(sums[j], axis=0, keepdims=True), axis=1, keepdims=True)
            row = row + jnp.where(lane == base + 2 * quarter + j, column, 0.0)
    table[...] = jnp.broadcast_to(row, (64, LANES))
    first, second, update = moments(
        own_first[0:SHARD_ROWS, :], own_second[0:SHARD_ROWS, :], grads[zh, 0:SHARD_ROWS, :]
    )
    new_first[0:SHARD_ROWS, :] = first
    new_second[0:SHARD_ROWS, :] = second
    own_update[0:SHARD_ROWS, :] = update


def step(total, states, first, second):
    shard = jax.ShapeDtypeStruct((PIECE, LANES), f32)
    return pl.pallas_call(
        step_kernel,
        in_specs=[whole()] * 4,
        out_specs=[whole()] * 5,
        out_shape=[
            shard,
            shard,
            jax.ShapeDtypeStruct((2, GROUP_ROWS, LANES), f32),
            jax.ShapeDtypeStruct((64, LANES), f32),
            shard,
        ],
        scratch_shapes=[pltpu.VMEM((GROUP, PIECE, LANES), f32)],
        compiler_params=params(),
    )(total, states, first, second)


def layout_kernel(own, by_xl, by_zb, by_both, updates, masters, gathered, shifted):
    xl, zb = lax.axis_index("xl"), lax.axis_index("zb")
    groups = ((own, xl, zb), (by_xl, 1 - xl, zb), (by_zb, xl, 1 - zb), (by_both, 1 - xl, 1 - zb))
    low = lane_index(SHARD_ROWS) < LANES // 2
    for k, flat in enumerate((updates, masters)):
        for source, a, b in groups:
            for i in range(GROUP):
                rows = slice(SHARD_ROWS * i, SHARD_ROWS * (i + 1))
                gathered[8 * a + 2 * i + b, 0:SHARD_ROWS, :] = source[k, rows, :]
        for i in range(LOCALS // 2):
            base = PAIR_ROWS * i
            flat[base : base + 19, :] = gathered[2 * i, 0:19, :]
            shifted[0:1, :] = gathered[2 * i, 19:20, :]
            shifted[1:21, :] = pltpu.roll(gathered[2 * i + 1, 0:SHARD_ROWS, :], LANES // 2, 1)
            flat[base + 19 : base + 39, :] = jnp.where(low, shifted[0:20, :], shifted[1:21, :])


def layout(groups):
    return pl.pallas_call(
        layout_kernel,
        in_specs=[whole()] * 4,
        out_specs=[whole()] * 2,
        out_shape=[pltpu.VMEM((NODE_ROWS, LANES), f32)] * 2,
        scratch_shapes=[pltpu.VMEM((LOCALS, PIECE, LANES), f32), pltpu.VMEM((PIECE, LANES), f32)],
        compiler_params=params(),
    )(*groups)


def final_kernel(tables, updates, masters, master, update, new_master, new_params, trust, ratios):
    layer, core, xl, zh, zb = position()
    for n in range(LAYERS):
        ratios[n : n + 1, :] = jnp.sum(tables[8 * n : 8 * n + 8, :], axis=0, keepdims=True)
    roots = jnp.sqrt(ratios[...])
    ratio = roots / (pltpu.roll(roots, LANES - 8, 1) + adam_epsilon)
    ratio = jnp.where(lane_index(8) < 8, ratio, 0.0)
    ratios[...] = ratio
    row = jnp.zeros((1, LANES), f32)
    for n in range(LAYERS):
        line = ratios[n : n + 1, :]
        row = row + (pltpu.roll(line, 8 * n, 1) if n else line)
    trust[...] = row[:, 0 : 8 * LAYERS]
    mine = ratios[pl.ds(layer, 1), :]
    lane = lane_index(1)
    values = [jnp.sum(jnp.where(lane == k, mine, 0.0), axis=1, keepdims=True) for k in range(8)]

    def spread(offset):
        factor = jnp.broadcast_to(values[0], offset.shape)
        for k in range(1, 8):
            factor = jnp.where(offset >= BOUNDS[k], values[k], factor)
        return factor

    start = core * NODE_PART
    index = 8 * xl + 2 * zh + zb
    new_master[0:SHARD_ROWS, :] = (
        master[0:SHARD_ROWS, :]
        - learn_rate * spread(place(SHARD_ROWS) + (start + index * SHARD)) * update[0:SHARD_ROWS, :]
    )
    step_rows = 104
    for i in range(NODE_ROWS // step_rows):
        rows = slice(step_rows * i, step_rows * (i + 1))
        factor = spread(place(step_rows) + (start + i * step_rows * LANES))
        new_params[rows, :] = (masters[rows, :] - learn_rate * factor * updates[rows, :]).astype(jnp.bfloat16)


def finish(tables, updates, masters, master, update):
    return pl.pallas_call(
        final_kernel,
        in_specs=[whole()] * 5,
        out_specs=[whole()] * 3,
        out_shape=[
            jax.ShapeDtypeStruct((PIECE, LANES), f32),
            jax.ShapeDtypeStruct((NODE_ROWS, LANES), jnp.bfloat16),
            jax.ShapeDtypeStruct((1, 8 * LAYERS), f32),
        ],
        scratch_shapes=[pltpu.VMEM((LAYERS, LANES), f32)],
        compiler_params=params(),
    )(tables, updates, masters, master, update)


def padded(vector):
    return jnp.pad(vector, (0, PIECE * LANES - SHARD)).reshape(PIECE, LANES)


def local(partials, master, first, second, acts, up_cot, out_cot, ln_gain):
    swap = ((0, 1), (1, 0))
    grid = partials.reshape(NODES // 2, 2, NODE_ROWS, LANES)
    sent = other_half(grid)
    other = lax.ppermute(sent, "c", swap)
    parts, center_rows, inverse_rows, own = token_sums(acts, up_cot, out_cot, grid)
    parts_other = lax.ppermute(parts, "c", swap)
    chunks = pair_sum(own, other, parts, parts_other)
    chunks = chunks.reshape(32, GROUP_ROWS, LANES).astype(f16)

    master, first, second = padded(master), padded(first), padded(second)
    high = master.astype(f16)
    low = ((master - high.astype(f32)) * LOW_SCALE).astype(f16)
    states = [v[0:SHARD_ROWS, :] for v in (first.astype(f16), second.astype(f16), high, low)]
    states = jnp.concatenate(states, axis=0)
    chunks, states, master, first, second = lax.optimization_barrier((chunks, states, master, first, second))
    blocks = lax.all_to_all(chunks, ("y", "xh", "xl", "zb"), 0, 0, tiled=True)
    plane = jnp.sum(blocks.astype(f32), axis=0).astype(f16)
    message = jnp.concatenate([plane, states], axis=0)
    message = jnp.broadcast_to(message[None], (GROUP,) + message.shape)
    pieces = lax.all_to_all(message, "zh", 0, 0, tiled=True)
    total = jnp.sum(pieces[:, :GROUP_ROWS].astype(f32), axis=0)
    states = pieces[:, GROUP_ROWS:].astype(f32)
    new_first, new_second, stepped, table, update = step(total, states, first, second)
    table, center_rows, inverse_rows = lax.optimization_barrier((table, center_rows, inverse_rows))
    input_grad = input_gradient(acts, up_cot, out_cot, ln_gain, center_rows, inverse_rows)
    groups = [
        stepped,
        lax.ppermute(stepped, "xl", swap),
        lax.ppermute(stepped, "zb", swap),
        lax.ppermute(stepped, ("xl", "zb"), ((0, 3), (3, 0), (1, 2), (2, 1))),
    ]
    tables = lax.all_to_all(table.reshape(64, 1, LANES), ("y", "xh", "c", "xl", "zb"), 0, 0, tiled=True)
    updates, masters = layout(groups)
    new_master, new_params, trust = finish(tables.reshape(64, LANES), updates, masters, master, update)

    def flat(piece):
        return piece.reshape(PIECE * LANES)[:SHARD]

    return (
        flat(new_master),
        flat(new_first),
        flat(new_second),
        new_params.reshape(NODE_PART),
        trust.reshape(8 * LAYERS),
        input_grad,
    )


def solution(mesh):
    every = ("y", "xh", "c", "xl", "zh", "zb")
    fine = Mesh(mesh.devices.reshape(4, 2, 2, 2, 4, 2), every)
    in_specs = (P(every, None), P(every), P(every), P(every), P(every, None), P(every, None), P(every, None), P())
    out_specs = (P(every), P(every), P(every), P(("y", "xh", "c")), P(), P(every, None))
    return jax.shard_map(local, mesh=fine, in_specs=in_specs, out_specs=out_specs, check_vma=False)
```

time: 70.4 us -> 66.5 us (0.945)
  blocking collectives: 49.6 us -> 34 us
  starting transfers between devices: 6.09 us -> 14.5 us
  waiting for transfers between devices: 1.04 us -> 3.51 us
  Pallas kernels: 11.6 us -> 13 us
    all_to_all x1 -> x0, blocking collectives: 15.7 us -> none  [local(): lax.all_to_all(table.reshape(64, 1, LANES), ('y', 'xh', 'c', 'xl', 'zb'),...]
    all_to_all x0 -> x1, starting transfers between devices: none -> 8.36 us  [local(): lax.all_to_all(table.reshape(64, 1, LANES), ('y', 'xh', 'c', 'xl', 'zb'),...]
    all_to_all x0 -> x1, waiting for transfers between devices: none -> 2.41 us  [local(): lax.all_to_all(table.reshape(64, 1, LANES), ('y', 'xh', 'c', 'xl', 'zb'),...]
    pallas_call x5 -> x7, Pallas kernels: 11.6 us -> 13 us  [the longest x1 5.18 us: input_gradient(): pl.pallas_call(grad_kernel, grid=(tokens // TOKENS_STEP,), in_specs=[bloc...]
  transfers between devices with their start and end apart: 5 -> 6, of which waited for: 1 -> 2; matrix products, arithmetic and copies ran while one was open for 0% -> 0% of each run, Pallas kernels for 8% -> 13%
where the time goes in v4:
time: 66.5 us; the launch traced here: 66.1 us
  blocking collectives  34 us (51%)
  starting transfers between devices  14.5 us (22%)
  Pallas kernels  13 us (20%)
  waiting for transfers between devices  3.51 us (5%)
  between operations  0.81 us (1%)
    all_to_all x1, blocking collectives, local(): blocks = lax.all_to_all(chunks, ('y', 'xh', 'xl', 'zb'), 0, 0, tiled=True)  19.5 us
    all_to_all x1, blocking collectives, local(): pieces = lax.all_to_all(message, 'zh', 0, 0, tiled=True)  14.5 us
    all_to_all x1, starting transfers between devices, local(): lax.all_to_all(table.reshape(64, 1, LANES), ('y', 'xh', 'c', 'xl', 'zb'),...  8.36 us
    pallas_call x1, Pallas kernels, input_gradient(): pl.pallas_call(grad_kernel, grid=(tokens // TOKENS_STEP,), in_specs=[bloc...  5.18 us
    pallas_call x1, Pallas kernels, token_sums(): pl.pallas_call(parts_kernel, in_specs=[hbm] * 4, out_specs=[whole()] * 4,...  3.44 us
    ppermute x1, starting transfers between devices, local(): other = lax.ppermute(sent, 'c', swap)  3.33 us
    all_to_all x1, waiting for transfers between devices, local(): lax.all_to_all(table.reshape(64, 1, LANES), ('y', 'xh', 'c', 'xl', 'zb'),...  2.41 us
    ppermute x1, starting transfers between devices, local(): lax.ppermute(stepped, ('xl', 'zb'), ((0, 3), (3, 0), (1, 2), (2, 1)))  1.68 us
  transfers between devices with their start and end apart: 6, of which 2 were waited for; matrix products, arithmetic and copies ran while one was open for 0% of the time, Pallas kernels for 13%

profile of v4, /device:TPU:1, one launch (start us, length us, event | category | flops | bytes accessed | tf_op | source)
XLA Modules:
  0.0 66.1 jit_solution(3101130082540244026)
XLA Ops:
  0.6 1.5 %shard_map.128 = f32[8,312,128]{2,1,0:T(8,128)S(1)} custom-call(f32[8,2,312,128]{3,2,1,0:T(8,128)} %bitcast.24), custom_call_target="tpu_custom_call" | custom-call | tf_op jit(solution)/shard_map/pallas_call | solution.py:202
  2.1 0.0 copy-start
  2.1 0.0 copy-start.1
  2.1 0.0 copy-start.2
  2.1 3.3 %collective-permute-start = (f32[8,312,128]{2,1,0:T(8,128)S(1)}, f32[8,312,128]{2,1,0:T(8,128)S(1)}, u32[]{:S(2)}, u32[]{:S(2)}) collective-permute-start(f32[8,312,128]{2,1,0:T(8,128)S(1)} %shard_map.128), channel_id=1, source_target_pairs={{0,16},{16,0},{1,17},{17,1},{2,18},{18,2},{3,19},{19,3},{4,20},{20... | collective-permute-start | bytes 3833864 | tf_op jit(solution)/shard_map/ppermute | solution.py:439
  5.5 3.4 %shard_map.127 = (f32[144,128]{1,0:T(8,128)S(1)}, f32[128,128]{1,0:T(8,128)S(1)}, f32[128,128]{1,0:T(8,128)S(1)}, f32[8,312,128]{2,1,0:T(8,128)S(1)}) custom-call(bf16[128,6144]{1,0:T(8,128)(2,1)} %acts.3, bf16[128,6144]{1,0:T(8,128)(2,1)} %up.3, bf16[128,6144]{1,0:T(8,128)(2,1)} %out.3, f32[8,2,312,128]{3,2,1,0:T(8,128)} %bitcast.25), custom_call_target="tpu_custom_call" | custom-call | flops 11796480 | bytes 4718592 | tf_op jit(solution)/shard_map/pallas_call | solution.py:130
  8.9 0.2 collective-permute-start.1
  9.1 0.0 copy-done
  9.1 0.0 copy-done.1
  9.1 0.0 copy-done.2
  9.2 1.1 %collective-permute-done.1.parts_other = f32[144,128]{1,0:T(8,128)S(1)} collective-permute-done((f32[144,128]{1,0:T(8,128)S(1)}, f32[144,128]{1,0:T(8,128)S(1)}, u32[]{:S(2)}, u32[]{:S(2)}) %collective-permute-start.1) | collective-permute-done | bytes 73760 | tf_op jit(solution)/shard_map/ppermute | solution.py:441
  10.3 0.0 collective-permute-done.other
  10.3 0.9 %shard_map.129 = f32[8,4,80,128]{3,2,1,0:T(8,128)S(1)} custom-call(f32[8,312,128]{2,1,0:T(8,128)S(1)} %get-tuple-element.28.own, f32[8,312,128]{2,1,0:T(8,128)S(1)} %collective-permute-done.other, f32[144,128]{1,0:T(8,128)S(1)} %get-tuple-element.29.parts, f32[144,128]{1,0:T(8,128)S(1)} %collective-permute-done.1.parts_other), custom_call_target="tpu_custom_call" | custom-call | tf_op jit(solution)/shard_map/pallas_call | solution.py:262
  11.2 0.1 convert_element_type.37
  11.3 0.0 copy-start.3
  11.3 19.5 %all_to_all.15 = f16[32,80,128]{2,1,0:T(8,128)(2,1)S(1)} all-to-all(f16[32,80,128]{2,1,0:T(8,128)(2,1)S(1)} %bitcast.26), channel_id=1, replica_groups=mesh['y'=4,'xh'=2,'c'=2,'xl'=2,'zh'=4,'zb'=2] {'y','xh','xl','zb'}, dimensions={0} | all-to-all | bytes 1310720 | tf_op jit(solution)/shard_map/all_to_all | solution.py:451
  30.8 0.1 convert_reduce_fusion
  31.0 14.5 %all_to_all.16 = f16[4,160,128]{2,1,0:T(8,128)(2,1)S(1)} all-to-all(f16[4,160,128]{2,1,0:T(8,128)(2,1)S(1)} %broadcast_in_dim.2), channel_id=1, replica_groups=mesh['y'=4,'xh'=2,'c'=2,'xl'=2,'zh'=4,'zb'=2] {'zh'}, dimensions={0} | all-to-all | bytes 327680 | tf_op jit(solution)/shard_map/all_to_all | solution.py:455
  45.5 0.8 %shard_map.130 = (f32[24,128]{1,0:T(8,128)}, f32[24,128]{1,0:T(8,128)}, f32[2,80,128]{2,1,0:T(8,128)S(1)}, f32[64,128]{1,0:T(8,128)}, f32[24,128]{1,0:T(8,128)S(1)}) custom-call(f32[80,128]{1,0:T(8,128)S(1)} %convert_reduce_fusion.1.total, f32[4,80,128]{2,1,0:T(8,128)S(1)} %slice_convert_fusion.states, f32[24,128]{1,0:T(8,128)S(1)} %pad_bitcast_fusion.2.own_first, ...), custom_call_target="tpu_custom_call" | custom-call | tf_op jit(solution)/shard_map/pallas_call | solution.py:336
  46.3 0.6 collective-permute-start.2
  46.9 0.4 collective-permute-start.3
  47.3 1.7 %collective-permute-start.4 = (f32[2,80,128]{2,1,0:T(8,128)S(1)}, f32[2,80,128]{2,1,0:T(8,128)S(1)}, u32[]{:S(2)}, u32[]{:S(2)}) collective-permute-start(f32[2,80,128]{2,1,0:T(8,128)S(1)} %get-tuple-element.38.own), channel_id=1, source_target_pairs={{0,9},{9,0},{1,8},{8,1},{2,11},{11,2},{3,10},{10,3},{4,13},{13,4},... | collective-permute-start | bytes 245768 | tf_op jit(solution)/shard_map/ppermute | solution.py:465
  49.0 8.4 %all-to-all-start.2 = ((f32[64,1,128]{2,1,0:T(1,128)}), f32[64,1,128]{2,1,0:T(1,128)S(1)}, u32[]{:S(2)}, u32[]{:S(2)}) async-start(f32[64,1,128]{2,1,0:T(1,128)} %bitcast.6), calls=%async_computation.2 | async-start | bytes 65536 | tf_op jit(solution)/shard_map/all_to_all | solution.py:467
  57.3 0.0 copy-done.3
  57.4 5.2 %shard_map.133 = bf16[128,6144]{1,0:T(8,128)(2,1)} custom-call(bf16[128,6144]{1,0:T(8,128)(2,1)} %acts.3, bf16[128,6144]{1,0:T(8,128)(2,1)} %up.3, bf16[128,6144]{1,0:T(8,128)(2,1)} %out.3, bf16[1,6144]{1,0:T(2,128)(2,1)S(1)} %reshape.62.gain, f32[128,128]{1,0:T(8,128)S(1)} %get-tuple-element.48.center_rows, f32[128,128]{1,0:T(8,128)S(1)} %get-tuple-element.49.inverse_rows), custom_call_target="tpu_custom_call" | custom-call | flops 11796480 | bytes 6291456 | tf_op jit(solution)/shard_map/pallas_call | solution.py:170
  62.5 0.0 collective-permute-done.2.by_xl
  62.5 0.0 collective-permute-done.3.by_zb
  62.5 0.0 collective-permute-done.4.by_both
  62.6 0.2 shard_map.131
  62.8 2.4 %all-to-all-done.2 = f32[64,1,128]{2,1,0:T(1,128)S(1)} async-done(((f32[64,1,128]{2,1,0:T(1,128)}), f32[64,1,128]{2,1,0:T(1,128)S(1)}, u32[]{:S(2)}, u32[]{:S(2)}) %all-to-all-start.2) | async-done | bytes 32800 | tf_op jit(solution)/shard_map/all_to_all | solution.py:467
  65.2 0.9 %shard_map.132 = (f32[24,128]{1,0:T(8,128)}, bf16[312,128]{1,0:T(8,128)(2,1)}, f32[1,64]{1,0:T(1,128)}) custom-call(f32[64,128]{1,0:T(8,128)S(1)} %bitcast.23, f32[312,128]{1,0:T(8,128)S(1)} %get-tuple-element.39.updates, f32[312,128]{1,0:T(8,128)S(1)} %get-tuple-element.40.masters, f32[24,128]{1,0:T(8,128)S(1)} %get-tuple-element.41.master, ...), custom_call_target="tpu_custom_call" | custom-call | tf_op jit(solution)/shard_map/pallas_call | solution.py:417
  (12 shorter events, 0.1 us)
Async XLA Ops:
  2.1 7.0 %copy-start = (f32[2496]{0:T(1024)S(1)}, f32[2496]{0:T(1024)}, u32[]{:S(2)}) copy-start(f32[2496]{0:T(1024)} %param.11) | copy-start | bytes 29956
  2.1 7.0 %copy-start.1 = (f32[2496]{0:T(1024)S(1)}, f32[2496]{0:T(1024)}, u32[]{:S(2)}) copy-start(f32[2496]{0:T(1024)} %param.10) | copy-start | bytes 29956
  2.1 7.0 %copy-start.2 = (f32[2496]{0:T(1024)S(1)}, f32[2496]{0:T(1024)}, u32[]{:S(2)}) copy-start(f32[2496]{0:T(1024)} %param.9) | copy-start | bytes 29956
  2.1 8.1 %collective-permute-start = (f32[8,312,128]{2,1,0:T(8,128)S(1)}, f32[8,312,128]{2,1,0:T(8,128)S(1)}, u32[]{:S(2)}, u32[]{:S(2)}) collective-permute-start(f32[8,312,128]{2,1,0:T(8,128)S(1)} %shard_map.128), channel_id=1, source_target_pairs={{0,16},{16,0},{1,17},{17,1},{2,18},{18,2},{3,19},{19,3},{4,20},{20... | collective-permute-start | bytes 3833864 | tf_op jit(solution)/shard_map/ppermute | solution.py:439
  8.9 1.4 %collective-permute-start.1 = (f32[144,128]{1,0:T(8,128)S(1)}, f32[144,128]{1,0:T(8,128)S(1)}, u32[]{:S(2)}, u32[]{:S(2)}) collective-permute-start(f32[144,128]{1,0:T(8,128)S(1)} %get-tuple-element.29.parts), channel_id=1, source_target_pairs={{0,16},{16,0},{1,17},{17,1},{2,18},{18,2},{3,19},{19,3},{4,20},{20... | collective-permute-start | bytes 221192 | tf_op jit(solution)/shard_map/ppermute | solution.py:441
  11.3 46.0 %copy-start.3 = (bf16[6144]{0:T(1024)(128)(2,1)S(1)}, bf16[6144]{0:T(1024)(128)(2,1)}, u32[]{:S(2)}) copy-start(bf16[6144]{0:T(1024)(128)(2,1)} %param.15) | copy-start | bytes 36868
  46.3 16.2 %collective-permute-start.2 = (f32[2,80,128]{2,1,0:T(8,128)S(1)}, f32[2,80,128]{2,1,0:T(8,128)S(1)}, u32[]{:S(2)}, u32[]{:S(2)}) collective-permute-start(f32[2,80,128]{2,1,0:T(8,128)S(1)} %get-tuple-element.38.own), channel_id=1, source_target_pairs={{0,8},{8,0},{1,9},{9,1},{2,10},{10,2},{3,11},{11,3},{4,12},{12,4},... | collective-permute-start | bytes 245768 | tf_op jit(solution)/shard_map/ppermute | solution.py:463
  46.9 15.6 %collective-permute-start.3 = (f32[2,80,128]{2,1,0:T(8,128)S(1)}, f32[2,80,128]{2,1,0:T(8,128)S(1)}, u32[]{:S(2)}, u32[]{:S(2)}) collective-permute-start(f32[2,80,128]{2,1,0:T(8,128)S(1)} %get-tuple-element.38.own), channel_id=1, source_target_pairs={{0,1},{1,0},{2,3},{3,2},{4,5},{5,4},{6,7},{7,6},{8,9},{9,8},{10,11... | collective-permute-start | bytes 245768 | tf_op jit(solution)/shard_map/ppermute | solution.py:464
  47.3 15.3 %collective-permute-start.4 = (f32[2,80,128]{2,1,0:T(8,128)S(1)}, f32[2,80,128]{2,1,0:T(8,128)S(1)}, u32[]{:S(2)}, u32[]{:S(2)}) collective-permute-start(f32[2,80,128]{2,1,0:T(8,128)S(1)} %get-tuple-element.38.own), channel_id=1, source_target_pairs={{0,9},{9,0},{1,8},{8,1},{2,11},{11,2},{3,10},{10,3},{4,13},{13,4},... | collective-permute-start | bytes 245768 | tf_op jit(solution)/shard_map/ppermute | solution.py:465
  49.0 16.2 %all-to-all-start.2 = ((f32[64,1,128]{2,1,0:T(1,128)}), f32[64,1,128]{2,1,0:T(1,128)S(1)}, u32[]{:S(2)}, u32[]{:S(2)}) async-start(f32[64,1,128]{2,1,0:T(1,128)} %bitcast.6), calls=%async_computation.2 | async-start | bytes 65536 | tf_op jit(solution)/shard_map/all_to_all | solution.py:467

commit v5 on v4

--- a/solution.py
+++ b/solution.py
@@ -37,6 +37,7 @@
 PARTS_SCALE = 1.0 / 64.0
 LOW_SCALE = 2048.0
 TOKENS_STEP = 32
+SUMS_STEP = 64
 COLS = D // LANES
 VMEM_LIMIT = 16 * 1024 * 1024
 
@@ -66,19 +67,19 @@
 
 
 def parts_kernel(acts, up, out, grid, parts, center_rows, inverse_rows, own,
-                 acts_buf, up_buf, out_buf, sums, sems, own_sems):
+                 up_buf, out_buf, sums, sems, own_sems):
     core = lax.axis_index("c")
     own_copies = [
         pltpu.make_async_copy(grid.at[i, core], own.at[i], own_sems.at[i]) for i in range(NODES // 2)
     ]
-    steps = acts.shape[0] // TOKENS_STEP
+    steps = acts.shape[0] // SUMS_STEP
 
     def rows_of(i):
-        return pl.ds(pl.multiple_of(i * TOKENS_STEP, TOKENS_STEP), TOKENS_STEP)
+        return pl.ds(pl.multiple_of(i * SUMS_STEP, SUMS_STEP), SUMS_STEP)
 
     def loads(i):
         rows = rows_of(i)
-        pairs = ((acts, acts_buf), (up, up_buf), (out, out_buf))
+        pairs = ((up, up_buf), (out, out_buf))
         return [pltpu.make_async_copy(a.at[rows], b.at[rows], sems.at[k, i]) for k, (a, b) in enumerate(pairs)]
 
     for i in range(steps):
@@ -89,26 +90,26 @@
     sums[...] = jnp.zeros_like(sums)
 
     def fold(v):
-        return jnp.sum(v.reshape(TOKENS_STEP // 8, 8, LANES), axis=0)
+        return jnp.sum(v.reshape(SUMS_STEP // 8, 8, LANES), axis=0)
 
     def body(i, carry):
         rows = rows_of(i)
-        for copy in loads(i):
-            copy.wait()
-        total = jnp.zeros((TOKENS_STEP, LANES), f32)
+        total = jnp.zeros((SUMS_STEP, LANES), f32)
         for j in range(COLS):
-            total = total + acts_buf[rows, cols(j)].astype(f32)
+            total = total + acts[rows, cols(j)].astype(f32)
         center = wide(jnp.sum(total, axis=1, keepdims=True) * (1.0 / D))
-        squares = jnp.zeros((TOKENS_STEP, LANES), f32)
+        squares = jnp.zeros((SUMS_STEP, LANES), f32)
         for j in range(COLS):
-            x = acts_buf[rows, cols(j)].astype(f32) - center
+            x = acts[rows, cols(j)].astype(f32) - center
             squares = squares + x * x
         variance = jnp.sum(squares, axis=1, keepdims=True) * (1.0 / D)
         inverse = wide(lax.rsqrt(variance + norm_epsilon))
         center_rows[rows, :] = center
         inverse_rows[rows, :] = inverse
+        for copy in loads(i):
+            copy.wait()
         for j in range(COLS):
-            normed = (acts_buf[rows, cols(j)].astype(f32) - center) * inverse
+            normed = (acts[rows, cols(j)].astype(f32) - center) * inverse
             u = up_buf[rows, cols(j)].astype(f32)
             sums[0, :, cols(j)] += fold(u * normed)
             sums[1, :, cols(j)] += fold(u)
@@ -129,7 +130,7 @@
     hbm = pl.BlockSpec(memory_space=pltpu.HBM)
     return pl.pallas_call(
         parts_kernel,
-        in_specs=[hbm] * 4,
+        in_specs=[whole()] + [hbm] * 3,
         out_specs=[whole()] * 4,
         out_shape=[
             pltpu.VMEM((3 * COLS, LANES), f32),
@@ -137,11 +138,11 @@
             jax.ShapeDtypeStruct((tokens, LANES), f32),
             pltpu.VMEM((NODES // 2, NODE_ROWS, LANES), f32),
         ],
-        scratch_shapes=[pltpu.VMEM((tokens, D), jnp.bfloat16)] * 3
-        + [pltpu.VMEM((3, 8, D), f32), pltpu.SemaphoreType.DMA((3, tokens // TOKENS_STEP)), pltpu.SemaphoreType.DMA((NODES // 2,))],
+        scratch_shapes=[pltpu.VMEM((tokens, D), jnp.bfloat16)] * 2
+        + [pltpu.VMEM((3, 8, D), f32), pltpu.SemaphoreType.DMA((2, tokens // SUMS_STEP)), pltpu.SemaphoreType.DMA((NODES // 2,))],
         compiler_params=params(),
         cost_estimate=pl.CostEstimate(flops=15 * tokens * D, bytes_accessed=6 * tokens * D, transcendentals=0),
-    )(away(acts), away(up), away(out), away(grid))
+    )(held(acts), away(up), away(out), away(grid))
 
 
 def grad_kernel(acts, up, out, gain, center_rows, inverse_rows, grad):
@@ -231,7 +232,8 @@
                     behind = total[first + 1 : first + 1 + SHARD_ROWS, :]
                     piece = pltpu.roll(jnp.where(high, ahead, behind), LANES // 2, 1)
                 row = SHARD_ROWS * (z // 2)
-                result[i, 2 * xl + z % 2, row : row + SHARD_ROWS, :] = piece
+                block = lax.rem(i, 2) * 16 + 8 * xl + 4 * (z % 2) + lax.div(i, 2)
+                result[block, row : row + SHARD_ROWS, :] = piece
 
     def body(i, carry):
         add(i)
@@ -255,7 +257,7 @@
         join(0, COLS // 2, 3 * COLS // 2)
         join(NODE_ROWS - COLS, 2 * COLS, COLS)
 
-    pack(last)
+    pack(jnp.int32(last))
 
 
 def pair_sum(own, other, parts, parts_other):
@@ -263,7 +265,7 @@
         pair_kernel,
         in_specs=[whole()] * 4,
         out_specs=whole(),
-        out_shape=pltpu.VMEM((NODES // 2, 4, GROUP_ROWS, LANES), f32),
+        out_shape=pltpu.VMEM((32, GROUP_ROWS, LANES), f32),
         scratch_shapes=[pltpu.VMEM((NODE_ROWS + 8, LANES), f32)],
         compiler_params=params(),
     )(held(own), held(other), held(parts), held(parts_other))
@@ -290,10 +292,14 @@
     return new_first, new_second, new_first / (jnp.sqrt(new_second) + adam_epsilon)
 
 
-def step_kernel(total, states, own_first, own_second, new_first, new_second, sent, table, own_update, grads):
+def step_kernel(ours, near, mid, far, own_first, own_second, new_first, new_second, sent, table, own_update,
+                grads, pieces):
     layer, core, xl, zh, zb = position()
     quarter = 2 * core + xl
     edges = bounds_of(quarter)
+    for k, piece in enumerate((ours, near, mid, far)):
+        pieces[k, :, :] = piece[...]
+    source = [lax.bitwise_xor(zh, i) for i in range(GROUP)]
     inside = place(SHARD_ROWS)
     valid = inside < SHARD
     weights = [jnp.zeros((SHARD_ROWS, LANES), f32) for _ in range(3)]
@@ -304,9 +310,14 @@
         place_in_layer = offset + quarter * QUARTER
         added = ((place_in_layer >= BOUNDS[4]) & (place_in_layer < BOUNDS[6])) | (place_in_layer >= BOUNDS[7])
         added = added & (layer == LAYERS - 1)
-        grad = total[rows, :] * jnp.where(added, 1.0 / PARTS_SCALE, 1.0 / SCALE)
+        total = pieces[source[0], rows, :]
+        for k in range(1, GROUP):
+            total = total + pieces[source[k], rows, :]
+        grad = total * jnp.where(added, 1.0 / PARTS_SCALE, 1.0 / SCALE)
         grads[i, 0:SHARD_ROWS, :] = grad
-        first, second, high, low = (states[i, SHARD_ROWS * k : SHARD_ROWS * (k + 1), :] for k in range(4))
+        first, second, high, low = (
+            pieces[source[i], GROUP_ROWS + SHARD_ROWS * k : GROUP_ROWS + SHARD_ROWS * (k + 1), :] for k in range(4)
+        )
         update = moments(first, second, grad)[2]
         held = high + low * (1.0 / LOW_SCALE)
         sent[0, rows, :] = update
@@ -331,11 +342,11 @@
     own_update[0:SHARD_ROWS, :] = update
 
 
-def step(total, states, first, second):
+def step(pieces, first, second):
     shard = jax.ShapeDtypeStruct((PIECE, LANES), f32)
     return pl.pallas_call(
         step_kernel,
-        in_specs=[whole()] * 4,
+        in_specs=[whole()] * 6,
         out_specs=[whole()] * 5,
         out_shape=[
             shard,
@@ -344,9 +355,12 @@
             jax.ShapeDtypeStruct((64, LANES), f32),
             shard,
         ],
-        scratch_shapes=[pltpu.VMEM((GROUP, PIECE, LANES), f32)],
-        compiler_params=params(),
-    )(total, states, first, second)
+        scratch_shapes=[
+            pltpu.VMEM((GROUP, PIECE, LANES), f32),
+            pltpu.VMEM((GROUP, 2 * GROUP_ROWS, LANES), f32),
+        ],
+        compiler_params=params(),
+    )(*pieces, first, second)
 
 
 def layout_kernel(own, by_xl, by_zb, by_both, updates, masters, gathered, shifted):
@@ -440,7 +454,7 @@
     parts, center_rows, inverse_rows, own = token_sums(acts, up_cot, out_cot, grid)
     parts_other = lax.ppermute(parts, "c", swap)
     chunks = pair_sum(own, other, parts, parts_other)
-    chunks = chunks.reshape(32, GROUP_ROWS, LANES).astype(f16)
+    chunks = chunks.astype(f16)
 
     master, first, second = padded(master), padded(first), padded(second)
     high = master.astype(f16)
@@ -448,14 +462,12 @@
     states = [v[0:SHARD_ROWS, :] for v in (first.astype(f16), second.astype(f16), high, low)]
     states = jnp.concatenate(states, axis=0)
     chunks, states, master, first, second = lax.optimization_barrier((chunks, states, master, first, second))
-    blocks = lax.all_to_all(chunks, ("y", "xh", "xl", "zb"), 0, 0, tiled=True)
+    blocks = lax.all_to_all(chunks, ("xh", "xl", "zb", "y"), 0, 0, tiled=True)
     plane = jnp.sum(blocks.astype(f32), axis=0).astype(f16)
     message = jnp.concatenate([plane, states], axis=0)
-    message = jnp.broadcast_to(message[None], (GROUP,) + message.shape)
-    pieces = lax.all_to_all(message, "zh", 0, 0, tiled=True)
-    total = jnp.sum(pieces[:, :GROUP_ROWS].astype(f32), axis=0)
-    states = pieces[:, GROUP_ROWS:].astype(f32)
-    new_first, new_second, stepped, table, update = step(total, states, first, second)
+    pieces = [message] + [lax.ppermute(message, "zh", [(i, i ^ k) for i in range(GROUP)]) for k in (1, 2, 3)]
+    pieces = [piece.astype(f32) for piece in pieces]
+    new_first, new_second, stepped, table, update = step(pieces, first, second)
     table, center_rows, inverse_rows = lax.optimization_barrier((table, center_rows, inverse_rows))
     input_grad = input_gradient(acts, up_cot, out_cot, ln_gain, center_rows, inverse_rows)
     groups = [

time: 66.5 us -> 63.1 us (0.949)
  blocking collectives: 34 us -> 18.2 us
  starting transfers between devices: 14.5 us -> 22.1 us
  waiting for transfers between devices: 3.51 us -> 8.64 us
    all_to_all x2 -> x1, blocking collectives: 34 us -> 18.2 us  [local(): blocks = lax.all_to_all(chunks, ('xh', 'xl', 'zb', 'y'), 0, 0, tiled=True)]
    ppermute x0 -> x3, starting transfers between devices: none -> 7.29 us  [local(): lax.ppermute(message, 'zh', [(i, i ^ k) for i in range(GROUP)])]
    ppermute x0 -> x3, waiting for transfers between devices: none -> 5.35 us  [local(): lax.ppermute(message, 'zh', [(i, i ^ k) for i in range(GROUP)])]
    ppermute x1, starting transfers between devices: 0.38 us -> 1.38 us  [local(): lax.ppermute(stepped, 'zb', swap)]
  transfers between devices with their start and end apart: 6 -> 9, of which waited for: 2 -> 4; matrix products, arithmetic and copies ran while one was open for 0% -> 0% of each run, Pallas kernels for 13% -> 13%
where the time goes in v5:
time: 63.1 us; the launch traced here: 62.8 us
  starting transfers between devices  22.1 us (35%)
  blocking collectives  18.2 us (29%)
  Pallas kernels  12.7 us (20%)
  waiting for transfers between devices  8.64 us (14%)
  between operations  0.81 us (1%)
    all_to_all x1, blocking collectives, local(): blocks = lax.all_to_all(chunks, ('xh', 'xl', 'zb', 'y'), 0, 0, tiled=True)  18.2 us
    all_to_all x1, starting transfers between devices, local(): lax.all_to_all(table.reshape(64, 1, LANES), ('y', 'xh', 'c', 'xl', 'zb'),...  8.55 us
    ppermute x3, starting transfers between devices, local(): lax.ppermute(message, 'zh', [(i, i ^ k) for i in range(GROUP)])  7.29 us
    ppermute x3, waiting for transfers between devices, local(): lax.ppermute(message, 'zh', [(i, i ^ k) for i in range(GROUP)])  5.35 us
    pallas_call x1, Pallas kernels, input_gradient(): pl.pallas_call(grad_kernel, grid=(tokens // TOKENS_STEP,), in_specs=[bloc...  5.18 us
    ppermute x1, starting transfers between devices, local(): other = lax.ppermute(sent, 'c', swap)  3.33 us
    pallas_call x1, Pallas kernels, token_sums(): pl.pallas_call(parts_kernel, in_specs=[whole()] + [hbm] * 3, out_specs=[w...  3.03 us
    all_to_all x1, waiting for transfers between devices, local(): lax.all_to_all(table.reshape(64, 1, LANES), ('y', 'xh', 'c', 'xl', 'zb'),...  2.32 us
  transfers between devices with their start and end apart: 9, of which 4 were waited for; matrix products, arithmetic and copies ran while one was open for 0% of the time, Pallas kernels for 13%

profile of v5, /device:TPU:1, one launch (start us, length us, event | category | flops | bytes accessed | tf_op | source)
XLA Modules:
  0.0 62.8 jit_solution(2396635363207639259)
XLA Ops:
  0.6 0.0 copy-start
  0.6 1.6 %shard_map.128 = f32[8,312,128]{2,1,0:T(8,128)S(1)} custom-call(f32[8,2,312,128]{3,2,1,0:T(8,128)} %bitcast.23), custom_call_target="tpu_custom_call" | custom-call | tf_op jit(solution)/shard_map/pallas_call | solution.py:203
  2.2 0.0 copy-start.1
  2.2 0.0 copy-start.2
  2.2 0.0 copy-start.3
  2.2 3.3 %collective-permute-start = (f32[8,312,128]{2,1,0:T(8,128)S(1)}, f32[8,312,128]{2,1,0:T(8,128)S(1)}, u32[]{:S(2)}, u32[]{:S(2)}) collective-permute-start(f32[8,312,128]{2,1,0:T(8,128)S(1)} %shard_map.128), channel_id=1, source_target_pairs={{0,16},{16,0},{1,17},{17,1},{2,18},{18,2},{3,19},{19,3},{4,20},{20... | collective-permute-start | bytes 3833864 | tf_op jit(solution)/shard_map/ppermute | solution.py:453
  5.6 0.0 copy-done
  5.6 3.0 %shard_map.127 = (f32[144,128]{1,0:T(8,128)S(1)}, f32[128,128]{1,0:T(8,128)S(1)}, f32[128,128]{1,0:T(8,128)S(1)}, f32[8,312,128]{2,1,0:T(8,128)S(1)}) custom-call(bf16[128,6144]{1,0:T(8,128)(2,1)S(1)} %copy-done, bf16[128,6144]{1,0:T(8,128)(2,1)} %up.3, bf16[128,6144]{1,0:T(8,128)(2,1)} %out.3, f32[8,2,312,128]{3,2,1,0:T(8,128)} %bitcast.24), custom_call_target="tpu_custom_call" | custom-call | flops 11796480 | bytes 4718592 | tf_op jit(solution)/shard_map/pallas_call | solution.py:131
  8.6 0.3 collective-permute-start.1
  8.9 0.0 copy-done.1
  8.9 0.0 copy-done.2
  8.9 0.0 copy-done.3
  9.0 1.0 %collective-permute-done.1.parts_other = f32[144,128]{1,0:T(8,128)S(1)} collective-permute-done((f32[144,128]{1,0:T(8,128)S(1)}, f32[144,128]{1,0:T(8,128)S(1)}, u32[]{:S(2)}, u32[]{:S(2)}) %collective-permute-start.1) | collective-permute-done | bytes 73760 | tf_op jit(solution)/shard_map/ppermute | solution.py:455
  10.0 0.0 collective-permute-done.other
  10.0 0.9 %shard_map.129 = f32[32,80,128]{2,1,0:T(8,128)S(1)} custom-call(f32[8,312,128]{2,1,0:T(8,128)S(1)} %get-tuple-element.28.own, f32[8,312,128]{2,1,0:T(8,128)S(1)} %collective-permute-done.other, f32[144,128]{1,0:T(8,128)S(1)} %get-tuple-element.29.parts, f32[144,128]{1,0:T(8,128)S(1)} %collective-permute-done.1.parts_other), custom_call_target="tpu_custom_call" | custom-call | tf_op jit(solution)/shard_map/pallas_call | solution.py:264
  10.9 0.1 convert_element_type.40
  11.0 0.0 copy-start.4
  11.0 18.2 %all_to_all.10 = f16[32,80,128]{2,1,0:T(8,128)(2,1)S(1)} all-to-all(f16[32,80,128]{2,1,0:T(8,128)(2,1)S(1)} %convert_element_type.40), channel_id=1, replica_groups=mesh['y'=4,'xh'=2,'c'=2,'xl'=2,'zh'=4,'zb'=2] {'xh','xl','zb','y'}, dimensions={0} | all-to-all | bytes 1310720 | tf_op jit(solution)/shard_map/all_to_all | solution.py:465
  29.3 0.1 convert_reduce_fusion
  29.4 3.1 %collective-permute-start.2 = (f16[160,128]{1,0:T(8,128)(2,1)S(1)}, f16[160,128]{1,0:T(8,128)(2,1)S(1)}, u32[]{:S(2)}, u32[]{:S(2)}) collective-permute-start(f16[160,128]{1,0:T(8,128)(2,1)S(1)} %get-tuple-element.50), channel_id=1, source_target_pairs={{0,2},{2,0},{4,6},{6,4},{1,3},{3,1},{5,7},{7,5},{8,10},{10,8},{12,... | collective-permute-start | bytes 122888 | tf_op jit(solution)/shard_map/ppermute | solution.py:468
  32.5 4.2 %collective-permute-start.3 = (f16[160,128]{1,0:T(8,128)(2,1)S(1)}, f16[160,128]{1,0:T(8,128)(2,1)S(1)}, u32[]{:S(2)}, u32[]{:S(2)}) collective-permute-start(f16[160,128]{1,0:T(8,128)(2,1)S(1)} %get-tuple-element.50), channel_id=1, source_target_pairs={{0,4},{2,6},{4,0},{6,2},{1,5},{3,7},{5,1},{7,3},{8,12},{10,14},{12... | collective-permute-start | bytes 122888 | tf_op jit(solution)/shard_map/ppermute | solution.py:468
  36.7 0.0 collective-permute-start.4
  36.7 0.0 collective-permute-done.2
  36.7 2.6 %collective-permute-done.3 = f16[160,128]{1,0:T(8,128)(2,1)S(1)} collective-permute-done((f16[160,128]{1,0:T(8,128)(2,1)S(1)}, f16[160,128]{1,0:T(8,128)(2,1)S(1)}, u32[]{:S(2)}, u32[]{:S(2)}) %collective-permute-start.3) | collective-permute-done | bytes 40992 | tf_op jit(solution)/shard_map/ppermute | solution.py:468
  39.3 2.8 %collective-permute-done.4 = f16[160,128]{1,0:T(8,128)(2,1)S(1)} collective-permute-done((f16[160,128]{1,0:T(8,128)(2,1)S(1)}, f16[160,128]{1,0:T(8,128)(2,1)S(1)}, u32[]{:S(2)}, u32[]{:S(2)}) %collective-permute-start.4) | collective-permute-done | bytes 40992 | tf_op jit(solution)/shard_map/ppermute | solution.py:468
  42.1 0.8 %shard_map.130 = (f32[24,128]{1,0:T(8,128)}, f32[24,128]{1,0:T(8,128)}, f32[2,80,128]{2,1,0:T(8,128)S(1)}, f32[64,128]{1,0:T(8,128)}, f32[24,128]{1,0:T(8,128)S(1)}) custom-call(f32[160,128]{1,0:T(8,128)S(1)} %get-tuple-element.51.ours, f32[160,128]{1,0:T(8,128)S(1)} %convert_element_type.49.near, f32[160,128]{1,0:T(8,128)S(1)} %convert_element_type.50.mid, ...), custom_call_target="tpu_custom_call" | custom-call | tf_op jit(solution)/shard_map/pallas_call | solution.py:347
  42.9 0.0 collective-permute-start.5
  42.9 1.4 %collective-permute-start.6 = (f32[2,80,128]{2,1,0:T(8,128)S(1)}, f32[2,80,128]{2,1,0:T(8,128)S(1)}, u32[]{:S(2)}, u32[]{:S(2)}) collective-permute-start(f32[2,80,128]{2,1,0:T(8,128)S(1)} %get-tuple-element.38.own), channel_id=1, source_target_pairs={{0,1},{1,0},{2,3},{3,2},{4,5},{5,4},{6,7},{7,6},{8,9},{9,8},{10,11... | collective-permute-start | bytes 245768 | tf_op jit(solution)/shard_map/ppermute | solution.py:476
  44.3 1.3 %collective-permute-start.7 = (f32[2,80,128]{2,1,0:T(8,128)S(1)}, f32[2,80,128]{2,1,0:T(8,128)S(1)}, u32[]{:S(2)}, u32[]{:S(2)}) collective-permute-start(f32[2,80,128]{2,1,0:T(8,128)S(1)} %get-tuple-element.38.own), channel_id=1, source_target_pairs={{0,9},{9,0},{1,8},{8,1},{2,11},{11,2},{3,10},{10,3},{4,13},{13,4},... | collective-permute-start | bytes 245768 | tf_op jit(solution)/shard_map/ppermute | solution.py:477
  45.6 8.6 %all-to-all-start.1 = ((f32[64,1,128]{2,1,0:T(1,128)}), f32[64,1,128]{2,1,0:T(1,128)S(1)}, u32[]{:S(2)}, u32[]{:S(2)}) async-start(f32[64,1,128]{2,1,0:T(1,128)} %bitcast.5), calls=%async_computation.1 | async-start | bytes 65536 | tf_op jit(solution)/shard_map/all_to_all | solution.py:479
  54.1 0.0 copy-done.4
  54.2 5.2 %shard_map.133 = bf16[128,6144]{1,0:T(8,128)(2,1)} custom-call(bf16[128,6144]{1,0:T(8,128)(2,1)} %acts.3, bf16[128,6144]{1,0:T(8,128)(2,1)} %up.3, bf16[128,6144]{1,0:T(8,128)(2,1)} %out.3, bf16[1,6144]{1,0:T(2,128)(2,1)S(1)} %reshape.59.gain, f32[128,128]{1,0:T(8,128)S(1)} %get-tuple-element.48.center_rows, f32[128,128]{1,0:T(8,128)S(1)} %get-tuple-element.49.inverse_rows), custom_call_target="tpu_custom_call" | custom-call | flops 11796480 | bytes 6291456 | tf_op jit(solution)/shard_map/pallas_call | solution.py:171
  59.3 0.0 collective-permute-done.5.by_xl
  59.3 0.0 collective-permute-done.6.by_zb
  59.3 0.0 collective-permute-done.7.by_both
  59.4 0.2 shard_map.131
  59.6 2.3 %all-to-all-done.1 = f32[64,1,128]{2,1,0:T(1,128)S(1)} async-done(((f32[64,1,128]{2,1,0:T(1,128)}), f32[64,1,128]{2,1,0:T(1,128)S(1)}, u32[]{:S(2)}, u32[]{:S(2)}) %all-to-all-start.1) | async-done | bytes 32800 | tf_op jit(solution)/shard_map/all_to_all | solution.py:479
  61.9 0.9 %shard_map.132 = (f32[24,128]{1,0:T(8,128)}, bf16[312,128]{1,0:T(8,128)(2,1)}, f32[1,64]{1,0:T(1,128)}) custom-call(f32[64,128]{1,0:T(8,128)S(1)} %bitcast.22, f32[312,128]{1,0:T(8,128)S(1)} %get-tuple-element.39.updates, f32[312,128]{1,0:T(8,128)S(1)} %get-tuple-element.40.masters, f32[24,128]{1,0:T(8,128)S(1)} %get-tuple-element.41.master, ...), custom_call_target="tpu_custom_call" | custom-call | tf_op jit(solution)/shard_map/pallas_call | solution.py:431
  (12 shorter events, 0.1 us)
Async XLA Ops:
  0.6 4.9 %copy-start = (bf16[128,6144]{1,0:T(8,128)(2,1)S(1)}, bf16[128,6144]{1,0:T(8,128)(2,1)}, u32[]{:S(2)}) copy-start(bf16[128,6144]{1,0:T(8,128)(2,1)} %acts.3) | copy-start | bytes 4718596
  2.2 6.7 %copy-start.1 = (f32[2496]{0:T(1024)S(1)}, f32[2496]{0:T(1024)}, u32[]{:S(2)}) copy-start(f32[2496]{0:T(1024)} %param.11) | copy-start | bytes 29956
  2.2 6.7 %copy-start.2 = (f32[2496]{0:T(1024)S(1)}, f32[2496]{0:T(1024)}, u32[]{:S(2)}) copy-start(f32[2496]{0:T(1024)} %param.10) | copy-start | bytes 29956
  2.2 6.7 %copy-start.3 = (f32[2496]{0:T(1024)S(1)}, f32[2496]{0:T(1024)}, u32[]{:S(2)}) copy-start(f32[2496]{0:T(1024)} %param.9) | copy-start | bytes 29956
  2.2 7.7 %collective-permute-start = (f32[8,312,128]{2,1,0:T(8,128)S(1)}, f32[8,312,128]{2,1,0:T(8,128)S(1)}, u32[]{:S(2)}, u32[]{:S(2)}) collective-permute-start(f32[8,312,128]{2,1,0:T(8,128)S(1)} %shard_map.128), channel_id=1, source_target_pairs={{0,16},{16,0},{1,17},{17,1},{2,18},{18,2},{3,19},{19,3},{4,20},{20... | collective-permute-start | bytes 3833864 | tf_op jit(solution)/shard_map/ppermute | solution.py:453
  8.6 1.4 %collective-permute-start.1 = (f32[144,128]{1,0:T(8,128)S(1)}, f32[144,128]{1,0:T(8,128)S(1)}, u32[]{:S(2)}, u32[]{:S(2)}) collective-permute-start(f32[144,128]{1,0:T(8,128)S(1)} %get-tuple-element.29.parts), channel_id=1, source_target_pairs={{0,16},{16,0},{1,17},{17,1},{2,18},{18,2},{3,19},{19,3},{4,20},{20... | collective-permute-start | bytes 221192 | tf_op jit(solution)/shard_map/ppermute | solution.py:455
  11.0 43.1 %copy-start.4 = (bf16[6144]{0:T(1024)(128)(2,1)S(1)}, bf16[6144]{0:T(1024)(128)(2,1)}, u32[]{:S(2)}) copy-start(bf16[6144]{0:T(1024)(128)(2,1)} %param.15) | copy-start | bytes 36868
  29.4 7.3 %collective-permute-start.2 = (f16[160,128]{1,0:T(8,128)(2,1)S(1)}, f16[160,128]{1,0:T(8,128)(2,1)S(1)}, u32[]{:S(2)}, u32[]{:S(2)}) collective-permute-start(f16[160,128]{1,0:T(8,128)(2,1)S(1)} %get-tuple-element.50), channel_id=1, source_target_pairs={{0,2},{2,0},{4,6},{6,4},{1,3},{3,1},{5,7},{7,5},{8,10},{10,8},{12,... | collective-permute-start | bytes 122888 | tf_op jit(solution)/shard_map/ppermute | solution.py:468
  32.5 6.8 %collective-permute-start.3 = (f16[160,128]{1,0:T(8,128)(2,1)S(1)}, f16[160,128]{1,0:T(8,128)(2,1)S(1)}, u32[]{:S(2)}, u32[]{:S(2)}) collective-permute-start(f16[160,128]{1,0:T(8,128)(2,1)S(1)} %get-tuple-element.50), channel_id=1, source_target_pairs={{0,4},{2,6},{4,0},{6,2},{1,5},{3,7},{5,1},{7,3},{8,12},{10,14},{12... | collective-permute-start | bytes 122888 | tf_op jit(solution)/shard_map/ppermute | solution.py:468
  36.7 5.4 %collective-permute-start.4 = (f16[160,128]{1,0:T(8,128)(2,1)S(1)}, f16[160,128]{1,0:T(8,128)(2,1)S(1)}, u32[]{:S(2)}, u32[]{:S(2)}) collective-permute-start(f16[160,128]{1,0:T(8,128)(2,1)S(1)} %get-tuple-element.50), channel_id=1, source_target_pairs={{0,6},{2,4},{4,2},{6,0},{1,7},{3,5},{5,3},{7,1},{8,14},{10,12},{12... | collective-permute-start | bytes 122888 | tf_op jit(solution)/shard_map/ppermute | solution.py:468
  42.9 16.4 %collective-permute-start.5 = (f32[2,80,128]{2,1,0:T(8,128)S(1)}, f32[2,80,128]{2,1,0:T(8,128)S(1)}, u32[]{:S(2)}, u32[]{:S(2)}) collective-permute-start(f32[2,80,128]{2,1,0:T(8,128)S(1)} %get-tuple-element.38.own), channel_id=1, source_target_pairs={{0,8},{8,0},{1,9},{9,1},{2,10},{10,2},{3,11},{11,3},{4,12},{12,4},... | collective-permute-start | bytes 245768 | tf_op jit(solution)/shard_map/ppermute | solution.py:475
  42.9 16.4 %collective-permute-start.6 = (f32[2,80,128]{2,1,0:T(8,128)S(1)}, f32[2,80,128]{2,1,0:T(8,128)S(1)}, u32[]{:S(2)}, u32[]{:S(2)}) collective-permute-start(f32[2,80,128]{2,1,0:T(8,128)S(1)} %get-tuple-element.38.own), channel_id=1, source_target_pairs={{0,1},{1,0},{2,3},{3,2},{4,5},{5,4},{6,7},{7,6},{8,9},{9,8},{10,11... | collective-permute-start | bytes 245768 | tf_op jit(solution)/shard_map/ppermute | solution.py:476
  44.3 15.1 %collective-permute-start.7 = (f32[2,80,128]{2,1,0:T(8,128)S(1)}, f32[2,80,128]{2,1,0:T(8,128)S(1)}, u32[]{:S(2)}, u32[]{:S(2)}) collective-permute-start(f32[2,80,128]{2,1,0:T(8,128)S(1)} %get-tuple-element.38.own), channel_id=1, source_target_pairs={{0,9},{9,0},{1,8},{8,1},{2,11},{11,2},{3,10},{10,3},{4,13},{13,4},... | collective-permute-start | bytes 245768 | tf_op jit(solution)/shard_map/ppermute | solution.py:477
  45.6 16.3 %all-to-all-start.1 = ((f32[64,1,128]{2,1,0:T(1,128)}), f32[64,1,128]{2,1,0:T(1,128)S(1)}, u32[]{:S(2)}, u32[]{:S(2)}) async-start(f32[64,1,128]{2,1,0:T(1,128)} %bitcast.5), calls=%async_computation.1 | async-start | bytes 65536 | tf_op jit(solution)/shard_map/all_to_all | solution.py:479

commit v6 on v5

--- a/solution.py
+++ b/solution.py
@@ -145,35 +145,65 @@
     )(held(acts), away(up), away(out), away(grid))
 
 
-def grad_kernel(acts, up, out, gain, center_rows, inverse_rows, grad):
-    rows = acts.shape[0]
-    center = center_rows[...]
-    inverse = inverse_rows[...]
-    scaled = jnp.zeros((rows, LANES), f32)
-    cross = jnp.zeros((rows, LANES), f32)
-    for j in range(COLS):
-        s = up[:, cols(j)].astype(f32) * gain[:, cols(j)].astype(f32)
-        scaled = scaled + s
-        cross = cross + s * (acts[:, cols(j)].astype(f32) - center)
-    mean_scaled = wide(jnp.sum(scaled, axis=1, keepdims=True) * (1.0 / D))
-    mean_cross = wide(jnp.sum(cross, axis=1, keepdims=True) * (1.0 / D)) * inverse
-    for j in range(COLS):
-        normed = (acts[:, cols(j)].astype(f32) - center) * inverse
-        s = up[:, cols(j)].astype(f32) * gain[:, cols(j)].astype(f32)
-        inner = s - mean_scaled - normed * mean_cross
-        grad[:, cols(j)] = (out[:, cols(j)].astype(f32) + inverse * inner).astype(jnp.bfloat16)
+def grad_kernel(acts_hbm, up_hbm, out_hbm, gain, center_rows, inverse_rows, grad,
+                acts, up, out, grad_buf, load_sems, sems):
+    steps = acts.shape[0] // TOKENS_STEP
+
+    def rows_of(i):
+        return pl.ds(pl.multiple_of(i * TOKENS_STEP, TOKENS_STEP), TOKENS_STEP)
+
+    def loads(i):
+        rows = rows_of(i)
+        pairs = ((acts_hbm, acts), (up_hbm, up), (out_hbm, out))
+        return [pltpu.make_async_copy(a.at[rows], b.at[rows], load_sems.at[k, i]) for k, (a, b) in enumerate(pairs)]
+
+    def store(i):
+        rows = rows_of(i)
+        return pltpu.make_async_copy(grad_buf.at[rows], grad.at[rows], sems.at[i])
+
+    for i in range(steps):
+        for copy in loads(i):
+            copy.start()
+
+    def body(i, carry):
+        rows = rows_of(i)
+        for copy in loads(i):
+            copy.wait()
+        center = center_rows[rows, :]
+        inverse = inverse_rows[rows, :]
+        scaled = jnp.zeros((TOKENS_STEP, LANES), f32)
+        cross = jnp.zeros((TOKENS_STEP, LANES), f32)
+        for j in range(COLS):
+            s = up[rows, cols(j)].astype(f32) * gain[:, cols(j)].astype(f32)
+            scaled = scaled + s
+            cross = cross + s * (acts[rows, cols(j)].astype(f32) - center)
+        mean_scaled = wide(jnp.sum(scaled, axis=1, keepdims=True) * (1.0 / D))
+        mean_cross = wide(jnp.sum(cross, axis=1, keepdims=True) * (1.0 / D)) * inverse
+        for j in range(COLS):
+            normed = (acts[rows, cols(j)].astype(f32) - center) * inverse
+            s = up[rows, cols(j)].astype(f32) * gain[:, cols(j)].astype(f32)
+            inner = s - mean_scaled - normed * mean_cross
+            grad_buf[rows, cols(j)] = (out[rows, cols(j)].astype(f32) + inverse * inner).astype(jnp.bfloat16)
+        store(i).start()
+        return carry
+
+    lax.fori_loop(0, steps, body, 0)
+    for i in range(steps):
+        store(i).wait()
 
 
 def input_gradient(acts, up, out, gain, center_rows, inverse_rows):
     tokens = acts.shape[0]
-    block = pl.BlockSpec((TOKENS_STEP, D), lambda i: (i, 0))
-    rows = pl.BlockSpec((TOKENS_STEP, LANES), lambda i: (i, 0))
     return pl.pallas_call(
         grad_kernel,
-        grid=(tokens // TOKENS_STEP,),
-        in_specs=[block, block, block, pl.BlockSpec((1, D), lambda i: (0, 0)), rows, rows],
-        out_specs=block,
+        in_specs=[pl.BlockSpec(memory_space=pltpu.HBM)] * 3 + [whole()] * 3,
+        out_specs=pl.BlockSpec(memory_space=pltpu.HBM),
         out_shape=jax.ShapeDtypeStruct((tokens, D), jnp.bfloat16),
+        scratch_shapes=[pltpu.VMEM((tokens, D), jnp.bfloat16)] * 4
+        + [
+            pltpu.SemaphoreType.DMA((3, tokens // TOKENS_STEP)),
+            pltpu.SemaphoreType.DMA((tokens // TOKENS_STEP,)),
+        ],
         compiler_params=params(),
         cost_estimate=pl.CostEstimate(flops=15 * tokens * D, bytes_accessed=8 * tokens * D, transcendentals=0),
     )(away(acts), away(up), away(out), gain.reshape(1, D), center_rows, inverse_rows)
@@ -292,14 +322,14 @@
     return new_first, new_second, new_first / (jnp.sqrt(new_second) + adam_epsilon)
 
 
-def step_kernel(ours, near, mid, far, own_first, own_second, new_first, new_second, sent, table, own_update,
+def step_kernel(far, ours, ahead, behind, own_first, own_second, new_first, new_second, sent, table, own_update,
                 grads, pieces):
     layer, core, xl, zh, zb = position()
     quarter = 2 * core + xl
     edges = bounds_of(quarter)
-    for k, piece in enumerate((ours, near, mid, far)):
+    for k, piece in enumerate((ours, ahead, far, behind)):
         pieces[k, :, :] = piece[...]
-    source = [lax.bitwise_xor(zh, i) for i in range(GROUP)]
+    source = [lax.rem(i + GROUP - zh, GROUP) for i in range(GROUP)]
     inside = place(SHARD_ROWS)
     valid = inside < SHARD
     weights = [jnp.zeros((SHARD_ROWS, LANES), f32) for _ in range(3)]
@@ -393,9 +423,10 @@
 
 def final_kernel(tables, updates, masters, master, update, new_master, new_params, trust, ratios):
     layer, core, xl, zh, zb = position()
-    for n in range(LAYERS):
-        ratios[n : n + 1, :] = jnp.sum(tables[8 * n : 8 * n + 8, :], axis=0, keepdims=True)
-    roots = jnp.sqrt(ratios[...])
+    sums = tables[0:LAYERS, :]
+    for n in range(1, 8):
+        sums = sums + tables[LAYERS * n : LAYERS * (n + 1), :]
+    roots = jnp.sqrt(sums)
     ratio = roots / (pltpu.roll(roots, LANES - 8, 1) + adam_epsilon)
     ratio = jnp.where(lane_index(8) < 8, ratio, 0.0)
     ratios[...] = ratio
@@ -465,7 +496,9 @@
     blocks = lax.all_to_all(chunks, ("xh", "xl", "zb", "y"), 0, 0, tiled=True)
     plane = jnp.sum(blocks.astype(f32), axis=0).astype(f16)
     message = jnp.concatenate([plane, states], axis=0)
-    pieces = [message] + [lax.ppermute(message, "zh", [(i, i ^ k) for i in range(GROUP)]) for k in (1, 2, 3)]
+    far = lax.ppermute(message, "zh", [(i, i ^ 2) for i in range(GROUP)])
+    near = [lax.ppermute(message, "zh", [(i, (i + k) % GROUP) for i in range(GROUP)]) for k in (1, 3)]
+    pieces = [far, message, near[1], near[0]]
     pieces = [piece.astype(f32) for piece in pieces]
     new_first, new_second, stepped, table, update = step(pieces, first, second)
     table, center_rows, inverse_rows = lax.optimization_barrier((table, center_rows, inverse_rows))
@@ -476,7 +509,7 @@
         lax.ppermute(stepped, "zb", swap),
         lax.ppermute(stepped, ("xl", "zb"), ((0, 3), (3, 0), (1, 2), (2, 1))),
     ]
-    tables = lax.all_to_all(table.reshape(64, 1, LANES), ("y", "xh", "c", "xl", "zb"), 0, 0, tiled=True)
+    tables = lax.all_to_all(table.reshape(64, 1, LANES), ("c", "xl", "zb", "y", "xh"), 0, 0, tiled=True)
     updates, masters = layout(groups)
     new_master, new_params, trust = finish(tables.reshape(64, LANES), updates, masters, master, update)
 

time: 63.1 us -> 62.2 us (0.986)
  waiting for transfers between devices: 8.64 us -> 6.99 us
  starting transfers between devices: 22.1 us -> 23.7 us
  Pallas kernels: 12.7 us -> 11.9 us
    ppermute x3, waiting for transfers between devices: 5.35 us -> 2.98 us  [the longest x2 2.98 us: local(): lax.ppermute(message, 'zh', [(i, (i + k) % GROUP) for i in range(GROUP)])]
    ppermute x3, starting transfers between devices: 7.29 us -> 8.46 us  [the longest x1 6.1 us: local(): far = lax.ppermute(message, 'zh', [(i, i ^ 2) for i in range(GROUP)])]
    pallas_call x1, Pallas kernels: 5.18 us -> 4.36 us  [input_gradient(): pl.pallas_call(grad_kernel, in_specs=[pl.BlockSpec(memory_space=pltpu.HBM...]
    all_to_all x1, waiting for transfers between devices: 2.32 us -> 3.05 us  [local(): lax.all_to_all(table.reshape(64, 1, LANES), ('c', 'xl', 'zb', 'y', 'xh'),...]
  transfers between devices with their start and end apart: 9 -> 9, of which waited for: 4 -> 4; matrix products, arithmetic and copies ran while one was open for 0% -> 0% of each run, Pallas kernels for 13% -> 12%
where the time goes in v6:
time: 62.2 us; the launch traced here: 61.9 us
  starting transfers between devices  23.7 us (38%)
  blocking collectives  18.2 us (29%)
  Pallas kernels  11.9 us (19%)
  waiting for transfers between devices  6.99 us (11%)
  between operations  0.83 us (1%)
    all_to_all x1, blocking collectives, local(): blocks = lax.all_to_all(chunks, ('xh', 'xl', 'zb', 'y'), 0, 0, tiled=True)  18.2 us
    all_to_all x1, starting transfers between devices, local(): lax.all_to_all(table.reshape(64, 1, LANES), ('c', 'xl', 'zb', 'y', 'xh'),...  8.94 us
    ppermute x1, starting transfers between devices, local(): far = lax.ppermute(message, 'zh', [(i, i ^ 2) for i in range(GROUP)])  6.1 us
    pallas_call x1, Pallas kernels, input_gradient(): pl.pallas_call(grad_kernel, in_specs=[pl.BlockSpec(memory_space=pltpu.HBM...  4.36 us
    ppermute x1, starting transfers between devices, local(): other = lax.ppermute(sent, 'c', swap)  3.33 us
    all_to_all x1, waiting for transfers between devices, local(): lax.all_to_all(table.reshape(64, 1, LANES), ('c', 'xl', 'zb', 'y', 'xh'),...  3.05 us
    pallas_call x1, Pallas kernels, token_sums(): pl.pallas_call(parts_kernel, in_specs=[whole()] + [hbm] * 3, out_specs=[w...  3.03 us
    ppermute x2, waiting for transfers between devices, local(): lax.ppermute(message, 'zh', [(i, (i + k) % GROUP) for i in range(GROUP)])  2.98 us
  transfers between devices with their start and end apart: 9, of which 4 were waited for; matrix products, arithmetic and copies ran while one was open for 0% of the time, Pallas kernels for 12%

profile of v6, /device:TPU:1, one launch (start us, length us, event | category | flops | bytes accessed | tf_op | source)
XLA Modules:
  0.0 61.9 jit_solution(12462591092656674647)
XLA Ops:
  0.6 0.0 copy-start
  0.6 1.6 %shard_map.128 = f32[8,312,128]{2,1,0:T(8,128)S(1)} custom-call(f32[8,2,312,128]{3,2,1,0:T(8,128)} %bitcast.23), custom_call_target="tpu_custom_call" | custom-call | tf_op jit(solution)/shard_map/pallas_call | solution.py:233
  2.2 0.0 copy-start.1
  2.2 0.0 copy-start.2
  2.2 0.0 copy-start.3
  2.2 3.3 %collective-permute-start = (f32[8,312,128]{2,1,0:T(8,128)S(1)}, f32[8,312,128]{2,1,0:T(8,128)S(1)}, u32[]{:S(2)}, u32[]{:S(2)}) collective-permute-start(f32[8,312,128]{2,1,0:T(8,128)S(1)} %shard_map.128), channel_id=1, source_target_pairs={{0,16},{16,0},{1,17},{17,1},{2,18},{18,2},{3,19},{19,3},{4,20},{20... | collective-permute-start | bytes 3833864 | tf_op jit(solution)/shard_map/ppermute | solution.py:484
  5.6 0.0 copy-done
  5.6 3.0 %shard_map.127 = (f32[144,128]{1,0:T(8,128)S(1)}, f32[128,128]{1,0:T(8,128)S(1)}, f32[128,128]{1,0:T(8,128)S(1)}, f32[8,312,128]{2,1,0:T(8,128)S(1)}) custom-call(bf16[128,6144]{1,0:T(8,128)(2,1)S(1)} %copy-done, bf16[128,6144]{1,0:T(8,128)(2,1)} %up_hbm.1, bf16[128,6144]{1,0:T(8,128)(2,1)} %out_hbm.1, f32[8,2,312,128]{3,2,1,0:T(8,128)} %bitcast.24), custom_call_target="tpu_custom_call" | custom-call | flops 11796480 | bytes 4718592 | tf_op jit(solution)/shard_map/pallas_call | solution.py:131
  8.6 0.3 collective-permute-start.1
  8.9 0.0 copy-done.1
  8.9 0.0 copy-done.2
  8.9 0.0 copy-done.3
  9.0 1.0 %collective-permute-done.1.parts_other = f32[144,128]{1,0:T(8,128)S(1)} collective-permute-done((f32[144,128]{1,0:T(8,128)S(1)}, f32[144,128]{1,0:T(8,128)S(1)}, u32[]{:S(2)}, u32[]{:S(2)}) %collective-permute-start.1) | collective-permute-done | bytes 73760 | tf_op jit(solution)/shard_map/ppermute | solution.py:486
  10.0 0.0 collective-permute-done.other
  10.0 0.9 %shard_map.129 = f32[32,80,128]{2,1,0:T(8,128)S(1)} custom-call(f32[8,312,128]{2,1,0:T(8,128)S(1)} %get-tuple-element.28.own, f32[8,312,128]{2,1,0:T(8,128)S(1)} %collective-permute-done.other, f32[144,128]{1,0:T(8,128)S(1)} %get-tuple-element.29.parts, f32[144,128]{1,0:T(8,128)S(1)} %collective-permute-done.1.parts_other), custom_call_target="tpu_custom_call" | custom-call | tf_op jit(solution)/shard_map/pallas_call | solution.py:294
  10.9 0.1 convert_element_type.40
  11.0 0.0 copy-start.4
  11.0 18.2 %all_to_all.10 = f16[32,80,128]{2,1,0:T(8,128)(2,1)S(1)} all-to-all(f16[32,80,128]{2,1,0:T(8,128)(2,1)S(1)} %convert_element_type.40), channel_id=1, replica_groups=mesh['y'=4,'xh'=2,'c'=2,'xl'=2,'zh'=4,'zb'=2] {'xh','xl','zb','y'}, dimensions={0} | all-to-all | bytes 1310720 | tf_op jit(solution)/shard_map/all_to_all | solution.py:496
  29.3 0.1 convert_reduce_fusion
  29.4 6.1 %collective-permute-start.2 = (f16[160,128]{1,0:T(8,128)(2,1)S(1)}, f16[160,128]{1,0:T(8,128)(2,1)S(1)}, u32[]{:S(2)}, u32[]{:S(2)}) collective-permute-start(f16[160,128]{1,0:T(8,128)(2,1)S(1)} %get-tuple-element.51), channel_id=1, source_target_pairs={{0,4},{2,6},{4,0},{6,2},{1,5},{3,7},{5,1},{7,3},{8,12},{10,14},{12... | collective-permute-start | bytes 122888 | tf_op jit(solution)/shard_map/ppermute | solution.py:499
  35.5 0.3 collective-permute-start.3
  35.8 2.1 %collective-permute-start.4 = (f16[160,128]{1,0:T(8,128)(2,1)S(1)}, f16[160,128]{1,0:T(8,128)(2,1)S(1)}, u32[]{:S(2)}, u32[]{:S(2)}) collective-permute-start(f16[160,128]{1,0:T(8,128)(2,1)S(1)} %get-tuple-element.51), channel_id=1, source_target_pairs={{0,2},{2,4},{4,6},{6,0},{1,3},{3,5},{5,7},{7,1},{8,10},{10,12},{12... | collective-permute-start | bytes 122888 | tf_op jit(solution)/shard_map/ppermute | solution.py:500
  37.9 0.0 collective-permute-done.2
  37.9 1.4 %collective-permute-done.3 = f16[160,128]{1,0:T(8,128)(2,1)S(1)} collective-permute-done((f16[160,128]{1,0:T(8,128)(2,1)S(1)}, f16[160,128]{1,0:T(8,128)(2,1)S(1)}, u32[]{:S(2)}, u32[]{:S(2)}) %collective-permute-start.3) | collective-permute-done | bytes 40992 | tf_op jit(solution)/shard_map/ppermute | solution.py:500
  39.3 1.5 %collective-permute-done.4 = f16[160,128]{1,0:T(8,128)(2,1)S(1)} collective-permute-done((f16[160,128]{1,0:T(8,128)(2,1)S(1)}, f16[160,128]{1,0:T(8,128)(2,1)S(1)}, u32[]{:S(2)}, u32[]{:S(2)}) %collective-permute-start.4) | collective-permute-done | bytes 40992 | tf_op jit(solution)/shard_map/ppermute | solution.py:500
  40.9 0.8 %shard_map.130 = (f32[24,128]{1,0:T(8,128)}, f32[24,128]{1,0:T(8,128)}, f32[2,80,128]{2,1,0:T(8,128)S(1)}, f32[64,128]{1,0:T(8,128)}, f32[24,128]{1,0:T(8,128)S(1)}) custom-call(f32[160,128]{1,0:T(8,128)S(1)} %convert_element_type.48.far, f32[160,128]{1,0:T(8,128)S(1)} %get-tuple-element.50.ours, f32[160,128]{1,0:T(8,128)S(1)} %convert_element_type.50.ahead, ...), custom_call_target="tpu_custom_call" | custom-call | tf_op jit(solution)/shard_map/pallas_call | solution.py:377
  41.7 0.0 collective-permute-start.5
  41.7 1.2 %collective-permute-start.6 = (f32[2,80,128]{2,1,0:T(8,128)S(1)}, f32[2,80,128]{2,1,0:T(8,128)S(1)}, u32[]{:S(2)}, u32[]{:S(2)}) collective-permute-start(f32[2,80,128]{2,1,0:T(8,128)S(1)} %get-tuple-element.38.own), channel_id=1, source_target_pairs={{0,1},{1,0},{2,3},{3,2},{4,5},{5,4},{6,7},{7,6},{8,9},{9,8},{10,11... | collective-permute-start | bytes 245768 | tf_op jit(solution)/shard_map/ppermute | solution.py:509
  42.9 1.5 %collective-permute-start.7 = (f32[2,80,128]{2,1,0:T(8,128)S(1)}, f32[2,80,128]{2,1,0:T(8,128)S(1)}, u32[]{:S(2)}, u32[]{:S(2)}) collective-permute-start(f32[2,80,128]{2,1,0:T(8,128)S(1)} %get-tuple-element.38.own), channel_id=1, source_target_pairs={{0,9},{9,0},{1,8},{8,1},{2,11},{11,2},{3,10},{10,3},{4,13},{13,4},... | collective-permute-start | bytes 245768 | tf_op jit(solution)/shard_map/ppermute | solution.py:510
  44.4 8.9 %all-to-all-start.1 = ((f32[64,1,128]{2,1,0:T(1,128)}), f32[64,1,128]{2,1,0:T(1,128)S(1)}, u32[]{:S(2)}, u32[]{:S(2)}) async-start(f32[64,1,128]{2,1,0:T(1,128)} %bitcast.5), calls=%async_computation.1 | async-start | bytes 65536 | tf_op jit(solution)/shard_map/all_to_all | solution.py:512
  53.3 0.0 copy-done.4
  53.3 4.4 %shard_map.133 = bf16[128,6144]{1,0:T(8,128)(2,1)} custom-call(bf16[128,6144]{1,0:T(8,128)(2,1)} %acts_hbm.1, bf16[128,6144]{1,0:T(8,128)(2,1)} %up_hbm.1, bf16[128,6144]{1,0:T(8,128)(2,1)} %out_hbm.1, bf16[1,6144]{1,0:T(2,128)(2,1)S(1)} %reshape.59.gain, f32[128,128]{1,0:T(8,128)S(1)} %get-tuple-element.48.center_rows, ...), custom_call_target="tpu_custom_call" | custom-call | flops 11796480 | bytes 6291456 | tf_op jit(solution)/shard_map/pallas_call | solution.py:197
  57.7 0.0 collective-permute-done.5.by_xl
  57.7 0.0 collective-permute-done.6.by_zb
  57.7 0.0 collective-permute-done.7.by_both
  57.7 0.2 shard_map.131
  57.9 3.0 %all-to-all-done.1 = f32[64,1,128]{2,1,0:T(1,128)S(1)} async-done(((f32[64,1,128]{2,1,0:T(1,128)}), f32[64,1,128]{2,1,0:T(1,128)S(1)}, u32[]{:S(2)}, u32[]{:S(2)}) %all-to-all-start.1) | async-done | bytes 32800 | tf_op jit(solution)/shard_map/all_to_all | solution.py:512
  61.0 0.9 %shard_map.132 = (f32[24,128]{1,0:T(8,128)}, bf16[312,128]{1,0:T(8,128)(2,1)}, f32[1,64]{1,0:T(1,128)}) custom-call(f32[64,128]{1,0:T(8,128)S(1)} %bitcast.22, f32[312,128]{1,0:T(8,128)S(1)} %get-tuple-element.39.updates, f32[312,128]{1,0:T(8,128)S(1)} %get-tuple-element.40.masters, f32[24,128]{1,0:T(8,128)S(1)} %get-tuple-element.41.master, ...), custom_call_target="tpu_custom_call" | custom-call | tf_op jit(solution)/shard_map/pallas_call | solution.py:462
  (12 shorter events, 0.1 us)
Async XLA Ops:
  0.6 4.9 %copy-start = (bf16[128,6144]{1,0:T(8,128)(2,1)S(1)}, bf16[128,6144]{1,0:T(8,128)(2,1)}, u32[]{:S(2)}) copy-start(bf16[128,6144]{1,0:T(8,128)(2,1)} %acts_hbm.1) | copy-start | bytes 4718596
  2.2 6.7 %copy-start.1 = (f32[2496]{0:T(1024)S(1)}, f32[2496]{0:T(1024)}, u32[]{:S(2)}) copy-start(f32[2496]{0:T(1024)} %param.11) | copy-start | bytes 29956
  2.2 6.7 %copy-start.2 = (f32[2496]{0:T(1024)S(1)}, f32[2496]{0:T(1024)}, u32[]{:S(2)}) copy-start(f32[2496]{0:T(1024)} %param.10) | copy-start | bytes 29956
  2.2 6.7 %copy-start.3 = (f32[2496]{0:T(1024)S(1)}, f32[2496]{0:T(1024)}, u32[]{:S(2)}) copy-start(f32[2496]{0:T(1024)} %param.9) | copy-start | bytes 29956
  2.2 7.7 %collective-permute-start = (f32[8,312,128]{2,1,0:T(8,128)S(1)}, f32[8,312,128]{2,1,0:T(8,128)S(1)}, u32[]{:S(2)}, u32[]{:S(2)}) collective-permute-start(f32[8,312,128]{2,1,0:T(8,128)S(1)} %shard_map.128), channel_id=1, source_target_pairs={{0,16},{16,0},{1,17},{17,1},{2,18},{18,2},{3,19},{19,3},{4,20},{20... | collective-permute-start | bytes 3833864 | tf_op jit(solution)/shard_map/ppermute | solution.py:484
  8.6 1.4 %collective-permute-start.1 = (f32[144,128]{1,0:T(8,128)S(1)}, f32[144,128]{1,0:T(8,128)S(1)}, u32[]{:S(2)}, u32[]{:S(2)}) collective-permute-start(f32[144,128]{1,0:T(8,128)S(1)} %get-tuple-element.29.parts), channel_id=1, source_target_pairs={{0,16},{16,0},{1,17},{17,1},{2,18},{18,2},{3,19},{19,3},{4,20},{20... | collective-permute-start | bytes 221192 | tf_op jit(solution)/shard_map/ppermute | solution.py:486
  11.0 42.3 %copy-start.4 = (bf16[6144]{0:T(1024)(128)(2,1)S(1)}, bf16[6144]{0:T(1024)(128)(2,1)}, u32[]{:S(2)}) copy-start(bf16[6144]{0:T(1024)(128)(2,1)} %param.15) | copy-start | bytes 36868
  29.4 8.5 %collective-permute-start.2 = (f16[160,128]{1,0:T(8,128)(2,1)S(1)}, f16[160,128]{1,0:T(8,128)(2,1)S(1)}, u32[]{:S(2)}, u32[]{:S(2)}) collective-permute-start(f16[160,128]{1,0:T(8,128)(2,1)S(1)} %get-tuple-element.51), channel_id=1, source_target_pairs={{0,4},{2,6},{4,0},{6,2},{1,5},{3,7},{5,1},{7,3},{8,12},{10,14},{12... | collective-permute-start | bytes 122888 | tf_op jit(solution)/shard_map/ppermute | solution.py:499
  35.5 3.8 %collective-permute-start.3 = (f16[160,128]{1,0:T(8,128)(2,1)S(1)}, f16[160,128]{1,0:T(8,128)(2,1)S(1)}, u32[]{:S(2)}, u32[]{:S(2)}) collective-permute-start(f16[160,128]{1,0:T(8,128)(2,1)S(1)} %get-tuple-element.51), channel_id=1, source_target_pairs={{0,6},{2,0},{4,2},{6,4},{1,7},{3,1},{5,3},{7,5},{8,14},{10,8},{12,... | collective-permute-start | bytes 122888 | tf_op jit(solution)/shard_map/ppermute | solution.py:500
  35.8 5.1 %collective-permute-start.4 = (f16[160,128]{1,0:T(8,128)(2,1)S(1)}, f16[160,128]{1,0:T(8,128)(2,1)S(1)}, u32[]{:S(2)}, u32[]{:S(2)}) collective-permute-start(f16[160,128]{1,0:T(8,128)(2,1)S(1)} %get-tuple-element.51), channel_id=1, source_target_pairs={{0,2},{2,4},{4,6},{6,0},{1,3},{3,5},{5,7},{7,1},{8,10},{10,12},{12... | collective-permute-start | bytes 122888 | tf_op jit(solution)/shard_map/ppermute | solution.py:500
  41.7 16.0 %collective-permute-start.5 = (f32[2,80,128]{2,1,0:T(8,128)S(1)}, f32[2,80,128]{2,1,0:T(8,128)S(1)}, u32[]{:S(2)}, u32[]{:S(2)}) collective-permute-start(f32[2,80,128]{2,1,0:T(8,128)S(1)} %get-tuple-element.38.own), channel_id=1, source_target_pairs={{0,8},{8,0},{1,9},{9,1},{2,10},{10,2},{3,11},{11,3},{4,12},{12,4},... | collective-permute-start | bytes 245768 | tf_op jit(solution)/shard_map/ppermute | solution.py:508
  41.7 16.0 %collective-permute-start.6 = (f32[2,80,128]{2,1,0:T(8,128)S(1)}, f32[2,80,128]{2,1,0:T(8,128)S(1)}, u32[]{:S(2)}, u32[]{:S(2)}) collective-permute-start(f32[2,80,128]{2,1,0:T(8,128)S(1)} %get-tuple-element.38.own), channel_id=1, source_target_pairs={{0,1},{1,0},{2,3},{3,2},{4,5},{5,4},{6,7},{7,6},{8,9},{9,8},{10,11... | collective-permute-start | bytes 245768 | tf_op jit(solution)/shard_map/ppermute | solution.py:509
  42.9 14.8 %collective-permute-start.7 = (f32[2,80,128]{2,1,0:T(8,128)S(1)}, f32[2,80,128]{2,1,0:T(8,128)S(1)}, u32[]{:S(2)}, u32[]{:S(2)}) collective-permute-start(f32[2,80,128]{2,1,0:T(8,128)S(1)} %get-tuple-element.38.own), channel_id=1, source_target_pairs={{0,9},{9,0},{1,8},{8,1},{2,11},{11,2},{3,10},{10,3},{4,13},{13,4},... | collective-permute-start | bytes 245768 | tf_op jit(solution)/shard_map/ppermute | solution.py:510
  44.4 16.6 %all-to-all-start.1 = ((f32[64,1,128]{2,1,0:T(1,128)}), f32[64,1,128]{2,1,0:T(1,128)S(1)}, u32[]{:S(2)}, u32[]{:S(2)}) async-start(f32[64,1,128]{2,1,0:T(1,128)} %bitcast.5), calls=%async_computation.1 | async-start | bytes 65536 | tf_op jit(solution)/shard_map/all_to_all | solution.py:512

commit v7 on v6

--- a/solution.py
+++ b/solution.py
@@ -262,7 +262,7 @@
                     behind = total[first + 1 : first + 1 + SHARD_ROWS, :]
                     piece = pltpu.roll(jnp.where(high, ahead, behind), LANES // 2, 1)
                 row = SHARD_ROWS * (z // 2)
-                block = lax.rem(i, 2) * 16 + 8 * xl + 4 * (z % 2) + lax.div(i, 2)
+                block = lax.rem(i, 2) * 16 + 8 * (z % 2) + 4 * xl + lax.div(i, 2)
                 result[block, row : row + SHARD_ROWS, :] = piece
 
     def body(i, carry):
@@ -493,7 +493,7 @@
     states = [v[0:SHARD_ROWS, :] for v in (first.astype(f16), second.astype(f16), high, low)]
     states = jnp.concatenate(states, axis=0)
     chunks, states, master, first, second = lax.optimization_barrier((chunks, states, master, first, second))
-    blocks = lax.all_to_all(chunks, ("xh", "xl", "zb", "y"), 0, 0, tiled=True)
+    blocks = lax.all_to_all(chunks, ("xh", "zb", "xl", "y"), 0, 0, tiled=True)
     plane = jnp.sum(blocks.astype(f32), axis=0).astype(f16)
     message = jnp.concatenate([plane, states], axis=0)
     far = lax.ppermute(message, "zh", [(i, i ^ 2) for i in range(GROUP)])

time: 62.2 us -> 62.4 us (level)
  no operation moved by 1% of the time
where the time goes in v7:
time: 62.4 us; the launch traced here: 62.2 us
  starting transfers between devices  24 us (38%)
  blocking collectives  18.3 us (29%)
  Pallas kernels  11.9 us (19%)
  waiting for transfers between devices  6.86 us (11%)
  between operations  0.83 us (1%)
    all_to_all x1, blocking collectives, local(): blocks = lax.all_to_all(chunks, ('xh', 'zb', 'xl', 'y'), 0, 0, tiled=True)  18.3 us
    all_to_all x1, starting transfers between devices, local(): lax.all_to_all(table.reshape(64, 1, LANES), ('c', 'xl', 'zb', 'y', 'xh'),...  9.04 us
    ppermute x1, starting transfers between devices, local(): far = lax.ppermute(message, 'zh', [(i, i ^ 2) for i in range(GROUP)])  6.1 us
    pallas_call x1, Pallas kernels, input_gradient(): pl.pallas_call(grad_kernel, in_specs=[pl.BlockSpec(memory_space=pltpu.HBM...  4.36 us
    ppermute x1, starting transfers between devices, local(): other = lax.ppermute(sent, 'c', swap)  3.33 us
    all_to_all x1, waiting for transfers between devices, local(): lax.all_to_all(table.reshape(64, 1, LANES), ('c', 'xl', 'zb', 'y', 'xh'),...  3.05 us
    pallas_call x1, Pallas kernels, token_sums(): pl.pallas_call(parts_kernel, in_specs=[whole()] + [hbm] * 3, out_specs=[w...  3.03 us
    ppermute x2, waiting for transfers between devices, local(): lax.ppermute(message, 'zh', [(i, (i + k) % GROUP) for i in range(GROUP)])  2.84 us
  transfers between devices with their start and end apart: 9, of which 4 were waited for; matrix products, arithmetic and copies ran while one was open for 0% of the time, Pallas kernels for 12%

profile of v7, /device:TPU:1, one launch (start us, length us, event | category | flops | bytes accessed | tf_op | source)
XLA Modules:
  0.0 62.2 jit_solution(3254149390831616643)
XLA Ops:
  0.6 0.0 copy-start
  0.6 1.6 %shard_map.128 = f32[8,312,128]{2,1,0:T(8,128)S(1)} custom-call(f32[8,2,312,128]{3,2,1,0:T(8,128)} %bitcast.23), custom_call_target="tpu_custom_call" | custom-call | tf_op jit(solution)/shard_map/pallas_call | solution.py:233
  2.2 0.0 copy-start.1
  2.2 0.0 copy-start.2
  2.2 0.0 copy-start.3
  2.2 3.3 %collective-permute-start = (f32[8,312,128]{2,1,0:T(8,128)S(1)}, f32[8,312,128]{2,1,0:T(8,128)S(1)}, u32[]{:S(2)}, u32[]{:S(2)}) collective-permute-start(f32[8,312,128]{2,1,0:T(8,128)S(1)} %shard_map.128), channel_id=1, source_target_pairs={{0,16},{16,0},{1,17},{17,1},{2,18},{18,2},{3,19},{19,3},{4,20},{20... | collective-permute-start | bytes 3833864 | tf_op jit(solution)/shard_map/ppermute | solution.py:484
  5.6 0.0 copy-done
  5.6 3.0 %shard_map.127 = (f32[144,128]{1,0:T(8,128)S(1)}, f32[128,128]{1,0:T(8,128)S(1)}, f32[128,128]{1,0:T(8,128)S(1)}, f32[8,312,128]{2,1,0:T(8,128)S(1)}) custom-call(bf16[128,6144]{1,0:T(8,128)(2,1)S(1)} %copy-done, bf16[128,6144]{1,0:T(8,128)(2,1)} %up_hbm.1, bf16[128,6144]{1,0:T(8,128)(2,1)} %out_hbm.1, f32[8,2,312,128]{3,2,1,0:T(8,128)} %bitcast.24), custom_call_target="tpu_custom_call" | custom-call | flops 11796480 | bytes 4718592 | tf_op jit(solution)/shard_map/pallas_call | solution.py:131
  8.6 0.3 collective-permute-start.1
  8.9 0.0 copy-done.1
  8.9 0.0 copy-done.2
  8.9 0.0 copy-done.3
  9.0 1.0 %collective-permute-done.1.parts_other = f32[144,128]{1,0:T(8,128)S(1)} collective-permute-done((f32[144,128]{1,0:T(8,128)S(1)}, f32[144,128]{1,0:T(8,128)S(1)}, u32[]{:S(2)}, u32[]{:S(2)}) %collective-permute-start.1) | collective-permute-done | bytes 73760 | tf_op jit(solution)/shard_map/ppermute | solution.py:486
  10.0 0.0 collective-permute-done.other
  10.0 0.9 %shard_map.129 = f32[32,80,128]{2,1,0:T(8,128)S(1)} custom-call(f32[8,312,128]{2,1,0:T(8,128)S(1)} %get-tuple-element.28.own, f32[8,312,128]{2,1,0:T(8,128)S(1)} %collective-permute-done.other, f32[144,128]{1,0:T(8,128)S(1)} %get-tuple-element.29.parts, f32[144,128]{1,0:T(8,128)S(1)} %collective-permute-done.1.parts_other), custom_call_target="tpu_custom_call" | custom-call | tf_op jit(solution)/shard_map/pallas_call | solution.py:294
  10.9 0.1 convert_element_type.40
  11.0 0.0 copy-start.4
  11.0 18.3 %all_to_all.10 = f16[32,80,128]{2,1,0:T(8,128)(2,1)S(1)} all-to-all(f16[32,80,128]{2,1,0:T(8,128)(2,1)S(1)} %convert_element_type.40), channel_id=1, replica_groups=mesh['y'=4,'xh'=2,'c'=2,'xl'=2,'zh'=4,'zb'=2] {'xh','zb','xl','y'}, dimensions={0} | all-to-all | bytes 1310720 | tf_op jit(solution)/shard_map/all_to_all | solution.py:496
  29.3 0.1 convert_reduce_fusion
  29.4 6.1 %collective-permute-start.2 = (f16[160,128]{1,0:T(8,128)(2,1)S(1)}, f16[160,128]{1,0:T(8,128)(2,1)S(1)}, u32[]{:S(2)}, u32[]{:S(2)}) collective-permute-start(f16[160,128]{1,0:T(8,128)(2,1)S(1)} %get-tuple-element.51), channel_id=1, source_target_pairs={{0,4},{2,6},{4,0},{6,2},{1,5},{3,7},{5,1},{7,3},{8,12},{10,14},{12... | collective-permute-start | bytes 122888 | tf_op jit(solution)/shard_map/ppermute | solution.py:499
  35.5 0.3 collective-permute-start.3
  35.8 2.1 %collective-permute-start.4 = (f16[160,128]{1,0:T(8,128)(2,1)S(1)}, f16[160,128]{1,0:T(8,128)(2,1)S(1)}, u32[]{:S(2)}, u32[]{:S(2)}) collective-permute-start(f16[160,128]{1,0:T(8,128)(2,1)S(1)} %get-tuple-element.51), channel_id=1, source_target_pairs={{0,2},{2,4},{4,6},{6,0},{1,3},{3,5},{5,7},{7,1},{8,10},{10,12},{12... | collective-permute-start | bytes 122888 | tf_op jit(solution)/shard_map/ppermute | solution.py:500
  37.9 0.0 collective-permute-done.2
  37.9 2.2 %collective-permute-done.3 = f16[160,128]{1,0:T(8,128)(2,1)S(1)} collective-permute-done((f16[160,128]{1,0:T(8,128)(2,1)S(1)}, f16[160,128]{1,0:T(8,128)(2,1)S(1)}, u32[]{:S(2)}, u32[]{:S(2)}) %collective-permute-start.3) | collective-permute-done | bytes 40992 | tf_op jit(solution)/shard_map/ppermute | solution.py:500
  40.2 0.6 collective-permute-done.4
  40.8 0.8 %shard_map.130 = (f32[24,128]{1,0:T(8,128)}, f32[24,128]{1,0:T(8,128)}, f32[2,80,128]{2,1,0:T(8,128)S(1)}, f32[64,128]{1,0:T(8,128)}, f32[24,128]{1,0:T(8,128)S(1)}) custom-call(f32[160,128]{1,0:T(8,128)S(1)} %convert_element_type.48.far, f32[160,128]{1,0:T(8,128)S(1)} %get-tuple-element.50.ours, f32[160,128]{1,0:T(8,128)S(1)} %convert_element_type.50.ahead, ...), custom_call_target="tpu_custom_call" | custom-call | tf_op jit(solution)/shard_map/pallas_call | solution.py:377
  41.6 0.2 collective-permute-start.5
  41.8 1.6 %collective-permute-start.6 = (f32[2,80,128]{2,1,0:T(8,128)S(1)}, f32[2,80,128]{2,1,0:T(8,128)S(1)}, u32[]{:S(2)}, u32[]{:S(2)}) collective-permute-start(f32[2,80,128]{2,1,0:T(8,128)S(1)} %get-tuple-element.38.own), channel_id=1, source_target_pairs={{0,1},{1,0},{2,3},{3,2},{4,5},{5,4},{6,7},{7,6},{8,9},{9,8},{10,11... | collective-permute-start | bytes 245768 | tf_op jit(solution)/shard_map/ppermute | solution.py:509
  43.4 1.1 %collective-permute-start.7 = (f32[2,80,128]{2,1,0:T(8,128)S(1)}, f32[2,80,128]{2,1,0:T(8,128)S(1)}, u32[]{:S(2)}, u32[]{:S(2)}) collective-permute-start(f32[2,80,128]{2,1,0:T(8,128)S(1)} %get-tuple-element.38.own), channel_id=1, source_target_pairs={{0,9},{9,0},{1,8},{8,1},{2,11},{11,2},{3,10},{10,3},{4,13},{13,4},... | collective-permute-start | bytes 245768 | tf_op jit(solution)/shard_map/ppermute | solution.py:510
  44.5 9.0 %all-to-all-start.1 = ((f32[64,1,128]{2,1,0:T(1,128)}), f32[64,1,128]{2,1,0:T(1,128)S(1)}, u32[]{:S(2)}, u32[]{:S(2)}) async-start(f32[64,1,128]{2,1,0:T(1,128)} %bitcast.5), calls=%async_computation.1 | async-start | bytes 65536 | tf_op jit(solution)/shard_map/all_to_all | solution.py:512
  53.6 0.0 copy-done.4
  53.6 4.4 %shard_map.133 = bf16[128,6144]{1,0:T(8,128)(2,1)} custom-call(bf16[128,6144]{1,0:T(8,128)(2,1)} %acts_hbm.1, bf16[128,6144]{1,0:T(8,128)(2,1)} %up_hbm.1, bf16[128,6144]{1,0:T(8,128)(2,1)} %out_hbm.1, bf16[1,6144]{1,0:T(2,128)(2,1)S(1)} %reshape.59.gain, f32[128,128]{1,0:T(8,128)S(1)} %get-tuple-element.48.center_rows, ...), custom_call_target="tpu_custom_call" | custom-call | flops 11796480 | bytes 6291456 | tf_op jit(solution)/shard_map/pallas_call | solution.py:197
  58.0 0.0 collective-permute-done.5.by_xl
  58.0 0.0 collective-permute-done.6.by_zb
  58.0 0.0 collective-permute-done.7.by_both
  58.0 0.2 shard_map.131
  58.2 3.0 %all-to-all-done.1 = f32[64,1,128]{2,1,0:T(1,128)S(1)} async-done(((f32[64,1,128]{2,1,0:T(1,128)}), f32[64,1,128]{2,1,0:T(1,128)S(1)}, u32[]{:S(2)}, u32[]{:S(2)}) %all-to-all-start.1) | async-done | bytes 32800 | tf_op jit(solution)/shard_map/all_to_all | solution.py:512
  61.2 0.9 %shard_map.132 = (f32[24,128]{1,0:T(8,128)}, bf16[312,128]{1,0:T(8,128)(2,1)}, f32[1,64]{1,0:T(1,128)}) custom-call(f32[64,128]{1,0:T(8,128)S(1)} %bitcast.22, f32[312,128]{1,0:T(8,128)S(1)} %get-tuple-element.39.updates, f32[312,128]{1,0:T(8,128)S(1)} %get-tuple-element.40.masters, f32[24,128]{1,0:T(8,128)S(1)} %get-tuple-element.41.master, ...), custom_call_target="tpu_custom_call" | custom-call | tf_op jit(solution)/shard_map/pallas_call | solution.py:462
  (12 shorter events, 0.1 us)
Async XLA Ops:
  0.6 4.9 %copy-start = (bf16[128,6144]{1,0:T(8,128)(2,1)S(1)}, bf16[128,6144]{1,0:T(8,128)(2,1)}, u32[]{:S(2)}) copy-start(bf16[128,6144]{1,0:T(8,128)(2,1)} %acts_hbm.1) | copy-start | bytes 4718596
  2.2 6.7 %copy-start.1 = (f32[2496]{0:T(1024)S(1)}, f32[2496]{0:T(1024)}, u32[]{:S(2)}) copy-start(f32[2496]{0:T(1024)} %param.11) | copy-start | bytes 29956
  2.2 6.7 %copy-start.2 = (f32[2496]{0:T(1024)S(1)}, f32[2496]{0:T(1024)}, u32[]{:S(2)}) copy-start(f32[2496]{0:T(1024)} %param.10) | copy-start | bytes 29956
  2.2 6.7 %copy-start.3 = (f32[2496]{0:T(1024)S(1)}, f32[2496]{0:T(1024)}, u32[]{:S(2)}) copy-start(f32[2496]{0:T(1024)} %param.9) | copy-start | bytes 29956
  2.2 7.7 %collective-permute-start = (f32[8,312,128]{2,1,0:T(8,128)S(1)}, f32[8,312,128]{2,1,0:T(8,128)S(1)}, u32[]{:S(2)}, u32[]{:S(2)}) collective-permute-start(f32[8,312,128]{2,1,0:T(8,128)S(1)} %shard_map.128), channel_id=1, source_target_pairs={{0,16},{16,0},{1,17},{17,1},{2,18},{18,2},{3,19},{19,3},{4,20},{20... | collective-permute-start | bytes 3833864 | tf_op jit(solution)/shard_map/ppermute | solution.py:484
  8.6 1.4 %collective-permute-start.1 = (f32[144,128]{1,0:T(8,128)S(1)}, f32[144,128]{1,0:T(8,128)S(1)}, u32[]{:S(2)}, u32[]{:S(2)}) collective-permute-start(f32[144,128]{1,0:T(8,128)S(1)} %get-tuple-element.29.parts), channel_id=1, source_target_pairs={{0,16},{16,0},{1,17},{17,1},{2,18},{18,2},{3,19},{19,3},{4,20},{20... | collective-permute-start | bytes 221192 | tf_op jit(solution)/shard_map/ppermute | solution.py:486
  11.0 42.5 %copy-start.4 = (bf16[6144]{0:T(1024)(128)(2,1)S(1)}, bf16[6144]{0:T(1024)(128)(2,1)}, u32[]{:S(2)}) copy-start(bf16[6144]{0:T(1024)(128)(2,1)} %param.15) | copy-start | bytes 36868
  29.4 8.5 %collective-permute-start.2 = (f16[160,128]{1,0:T(8,128)(2,1)S(1)}, f16[160,128]{1,0:T(8,128)(2,1)S(1)}, u32[]{:S(2)}, u32[]{:S(2)}) collective-permute-start(f16[160,128]{1,0:T(8,128)(2,1)S(1)} %get-tuple-element.51), channel_id=1, source_target_pairs={{0,4},{2,6},{4,0},{6,2},{1,5},{3,7},{5,1},{7,3},{8,12},{10,14},{12... | collective-permute-start | bytes 122888 | tf_op jit(solution)/shard_map/ppermute | solution.py:499
  35.5 4.6 %collective-permute-start.3 = (f16[160,128]{1,0:T(8,128)(2,1)S(1)}, f16[160,128]{1,0:T(8,128)(2,1)S(1)}, u32[]{:S(2)}, u32[]{:S(2)}) collective-permute-start(f16[160,128]{1,0:T(8,128)(2,1)S(1)} %get-tuple-element.51), channel_id=1, source_target_pairs={{0,6},{2,0},{4,2},{6,4},{1,7},{3,1},{5,3},{7,5},{8,14},{10,8},{12,... | collective-permute-start | bytes 122888 | tf_op jit(solution)/shard_map/ppermute | solution.py:500
  35.8 5.0 %collective-permute-start.4 = (f16[160,128]{1,0:T(8,128)(2,1)S(1)}, f16[160,128]{1,0:T(8,128)(2,1)S(1)}, u32[]{:S(2)}, u32[]{:S(2)}) collective-permute-start(f16[160,128]{1,0:T(8,128)(2,1)S(1)} %get-tuple-element.51), channel_id=1, source_target_pairs={{0,2},{2,4},{4,6},{6,0},{1,3},{3,5},{5,7},{7,1},{8,10},{10,12},{12... | collective-permute-start | bytes 122888 | tf_op jit(solution)/shard_map/ppermute | solution.py:500
  41.6 16.4 %collective-permute-start.5 = (f32[2,80,128]{2,1,0:T(8,128)S(1)}, f32[2,80,128]{2,1,0:T(8,128)S(1)}, u32[]{:S(2)}, u32[]{:S(2)}) collective-permute-start(f32[2,80,128]{2,1,0:T(8,128)S(1)} %get-tuple-element.38.own), channel_id=1, source_target_pairs={{0,8},{8,0},{1,9},{9,1},{2,10},{10,2},{3,11},{11,3},{4,12},{12,4},... | collective-permute-start | bytes 245768 | tf_op jit(solution)/shard_map/ppermute | solution.py:508
  41.8 16.2 %collective-permute-start.6 = (f32[2,80,128]{2,1,0:T(8,128)S(1)}, f32[2,80,128]{2,1,0:T(8,128)S(1)}, u32[]{:S(2)}, u32[]{:S(2)}) collective-permute-start(f32[2,80,128]{2,1,0:T(8,128)S(1)} %get-tuple-element.38.own), channel_id=1, source_target_pairs={{0,1},{1,0},{2,3},{3,2},{4,5},{5,4},{6,7},{7,6},{8,9},{9,8},{10,11... | collective-permute-start | bytes 245768 | tf_op jit(solution)/shard_map/ppermute | solution.py:509
  43.4 14.6 %collective-permute-start.7 = (f32[2,80,128]{2,1,0:T(8,128)S(1)}, f32[2,80,128]{2,1,0:T(8,128)S(1)}, u32[]{:S(2)}, u32[]{:S(2)}) collective-permute-start(f32[2,80,128]{2,1,0:T(8,128)S(1)} %get-tuple-element.38.own), channel_id=1, source_target_pairs={{0,9},{9,0},{1,8},{8,1},{2,11},{11,2},{3,10},{10,3},{4,13},{13,4},... | collective-permute-start | bytes 245768 | tf_op jit(solution)/shard_map/ppermute | solution.py:510
  44.5 16.7 %all-to-all-start.1 = ((f32[64,1,128]{2,1,0:T(1,128)}), f32[64,1,128]{2,1,0:T(1,128)S(1)}, u32[]{:S(2)}, u32[]{:S(2)}) async-start(f32[64,1,128]{2,1,0:T(1,128)} %bitcast.5), calls=%async_computation.1 | async-start | bytes 65536 | tf_op jit(solution)/shard_map/all_to_all | solution.py:512
